TPU v7x, 256 devices: a whole 4x4x8 slice. The times are simulated.
256 devices in a mesh: branch: 2 (over y_hi), strip: 128 (over y_lo, z, x, core).
Axes of the slice: x: 4, y: 4 (y_hi: 2, y_lo: 2; y = y_hi * 2 + y_lo), z: 8, core: 2. Of those that a mesh axis runs over, the one named last changes fastest.
Arguments:
- feats: bfloat16 [2, 1024, 256, 320], P('branch', 'strip')
- conv_first: bfloat16 [2, 3, 3, 320, 320], P('branch'), may hold values from -0.109375 to 0.109375
- conv_second: bfloat16 [2, 3, 3, 320, 320], P('branch'), may hold values from -0.109375 to 0.109375
- time_shift: float32 [2, 320], P('branch'), may hold values from -6 to 6
- norm_gains: float32 [2, 2, 320], P('branch'), may hold values from 0.1 to 1.9
- zero_conv: bfloat16 [320, 320], replicated, may hold values from -0.3125 to 0.3125
Outputs:
- outputs: bfloat16 [2, 1024, 256, 320], P('branch', 'strip')
All inputs are finite; a program needn't handle non-finite values.
Results may differ from a plain program's by a relative error of at most 0.0042.
The roundings to bfloat16 on the way count: a program that leaves them out, or rounds other values in their place, can miss the bound.
Values may be sent and summed in bfloat16 or wider, within the bound.
No kernel may reach another device: no remote copies, remote signals or barrier semaphores. Data moves between devices by JAX's collectives and lax.ppermute only.
A program may use at most 64 MiB of HBM per device.

v0:
```python
import jax
import jax.numpy as jnp
from jax import lax
from jax.sharding import PartitionSpec as P

G = 32


def padded(block, sides, width):
    for axis, dim in sides:
        count = lax.axis_size(axis)
        forward = [(i, i + 1) for i in range(count - 1)]
        backward = [(target, source) for source, target in forward]
        low = lax.ppermute(
            lax.slice_in_dim(block, block.shape[dim] - width, None, axis=dim), axis, forward
        )
        high = lax.ppermute(lax.slice_in_dim(block, 0, width, axis=dim), axis, backward)
        block = jnp.concatenate([low, block, high], axis=dim)
    return block


def passed_along(block, axis, distance):
    devices = range(lax.axis_size(axis))
    route = [(i - distance, i) for i in devices if i - distance in devices]
    return lax.ppermute(block, axis, route)


def part_sums(values, groups):
    grouped = values.reshape(-1, groups, values.shape[-1] // groups)
    return jnp.sum(grouped, axis=(0, 2))


def spread_groups(stat, channels):
    return jnp.repeat(stat, channels // stat.shape[0])


def group_stats(values, groups, count):
    channels = values.shape[-1]
    total = lax.psum(part_sums(values, groups), "strip")
    mean = total / count
    centered = values - spread_groups(mean, channels)
    spread = lax.psum(part_sums(centered * centered, groups), "strip")
    variance = spread / count
    return (spread_groups(mean, channels), spread_groups(lax.rsqrt(variance + 1e-05), channels))


def conv_rows(inputs, kernel):
    result = lax.conv_general_dilated(
        inputs[None],
        kernel,
        (1, 1),
        ((0, 0), (1, 1)),
        dimension_numbers=("NHWC", "HWIO", "NHWC"),
        preferred_element_type=jnp.float32,
    )
    return result[0]


def on_device(feats, conv_first, conv_second, time_shift, norm_gains, zero_conv):
    source = feats[0]
    rows_dev, width, channels = source.shape
    total_rows = rows_dev * lax.axis_size("strip")
    count = total_rows * width * (channels // G)
    source_f = source.astype(jnp.float32)
    gain_one = norm_gains[0, 0]
    gain_two = norm_gains[0, 1]
    shift_time = time_shift[0]
    mean_one, scale_one = group_stats(source_f, G, count)
    first = jax.nn.silu((source_f - mean_one) * scale_one * gain_one).astype(jnp.bfloat16)
    first_ext = padded(first, (("strip", 0),), 1)
    middle = conv_rows(first_ext, conv_first[0]) + shift_time
    mean_two, scale_two = group_stats(middle, G, count)
    second_own = jax.nn.silu((middle - mean_two) * scale_two * gain_two).astype(jnp.bfloat16)
    second = padded(second_own, (("strip", 0),), 1)
    block = source_f + conv_rows(second, conv_second[0])
    own_rounded = block.astype(jnp.bfloat16)
    residual = jnp.dot(
        own_rounded.reshape(-1, channels), zero_conv, preferred_element_type=jnp.float32
    ).astype(jnp.bfloat16)
    arrived = passed_along(residual.reshape(block.shape), "branch", 1)
    is_unet = lax.axis_index("branch") == 1
    mixed = jnp.where(is_unet, block + arrived.astype(jnp.float32), block).astype(jnp.bfloat16)
    return mixed[None]


def solution(mesh):
    placed = (
        P("branch", "strip", None, None),
        P("branch", None, None, None, None),
        P("branch", None, None, None, None),
        P("branch", None),
        P("branch", None, None),
        P(),
    )
    return jax.shard_map(
        on_device,
        mesh=mesh,
        in_specs=placed,
        out_specs=P("branch", "strip", None, None),
        check_vma=False,
    )
```

profile of v0, /device:TPU:16, one launch (start us, length us, event | category | flops | bytes accessed | tf_op | source)
XLA Modules:
  0.0 1222.8 jit_solution(17295083427461076748)
XLA Ops:
  0.0 3.0 copy.20
  3.0 1.7 convert_reduce_fusion
  5.0 283.8 %psum.28 = f32[32]{0:T(128)S(1)} all-reduce(f32[32]{0:T(128)S(1)} %reduce_sum.51), channel_id=1, replica_groups=mesh['branch'=2,'strip'=128] {'strip'}, use_global_device_ids=true, to_apply=%region_2.0 | all-reduce | flops 32 | bytes 256 | tf_op jit(solution)/shard_map/psum | solution.py:39
  288.9 1.9 fusion.14
  291.1 275.6 %psum.29 = f32[32]{0:T(128)S(1)} all-reduce(f32[32]{0:T(128)S(1)} %reduce_sum.54), channel_id=1, replica_groups=mesh['branch'=2,'strip'=128] {'strip'}, use_global_device_ids=true, to_apply=%region_5.6 | all-reduce | flops 32 | bytes 256 | tf_op jit(solution)/shard_map/psum | solution.py:42
  566.9 2.4 fusion.11
  571.0 1.8 collective-permute-start
  574.3 2.2 collective-permute-done.1
  576.5 3.7 maximum_bitcast_fusion
  581.4 8.6 select_reduce_fusion.1
  590.3 281.2 %psum.30 = f32[32]{0:T(128)S(1)} all-reduce(f32[32]{0:T(128)S(1)} %reduce_sum.72), channel_id=1, replica_groups=mesh['branch'=2,'strip'=128] {'strip'}, use_global_device_ids=true, to_apply=%region_8.9 | all-reduce | flops 32 | bytes 256 | tf_op jit(solution)/shard_map/psum | solution.py:39
  871.7 4.4 copy.24
  877.0 275.6 %psum.31 = f32[32]{0:T(128)S(1)} all-reduce(f32[32]{0:T(128)S(1)} %reduce_sum.75), channel_id=1, replica_groups=mesh['branch'=2,'strip'=128] {'strip'}, use_global_device_ids=true, to_apply=%region_11.12 | all-reduce | flops 32 | bytes 256 | tf_op jit(solution)/shard_map/psum | solution.py:42
  1152.8 2.9 multiply_convert_fusion
  1156.2 1.8 collective-permute-start.2
  1159.3 2.3 collective-permute-done.3
  1161.6 2.2 maximum_bitcast_fusion.1
  1165.9 7.3 fusion.41
  1177.1 2.6 copy.29
  1180.1 1.8 convolution_convert_fusion
  1183.4 29.3 %collective-permute-done.4 = bf16[8,256,320]{1,2,0:T(8,128)(2,1)} collective-permute-done((bf16[8,256,320]{1,2,0:T(8,128)(2,1)S(1)}, bf16[8,256,320]{1,2,0:T(8,128)(2,1)}, u32[]{:S(2)}, u32[]{:S(2)}) %collective-permute-start.4) | collective-permute-done | bytes 1310752 | tf_op jit(solution)/shard_map/ppermute | solution.py:25
  1212.6 2.9 copy.31
  1215.5 4.6 fusion.46
  1220.1 2.8 copy.32
  (58 shorter events, 16.1 us)
Async XLA Ops:
  0.0 581.2 %copy-start = (bf16[1,3,3,320,320]{4,3,2,1,0:T(8,128)(2,1)S(1)}, bf16[1,3,3,320,320]{4,3,2,1,0:T(8,128)(2,1)}, u32[]{:S(2)}) copy-start(bf16[1,3,3,320,320]{4,3,2,1,0:T(8,128)(2,1)} %param.7) | copy-start | bytes 5529604
  0.0 566.9 %copy-start.6 = (f32[1,2,320]{2,1,0:T(2,128)S(1)}, f32[1,2,320]{2,1,0:T(2,128)}, u32[]{:S(2)}) copy-start(f32[1,2,320]{2,1,0:T(2,128)} %param.10) | copy-start | bytes 7684
  288.9 285.3 %copy-start.7 = (f32[1,320]{1,0:T(1,128)S(1)}, f32[1,320]{1,0:T(1,128)}, u32[]{:S(2)}) copy-start(f32[1,320]{1,0:T(1,128)} %param.9) | copy-start | bytes 3844
  569.3 1.2 copy-start.4
  571.0 3.3 collective-permute-start
  572.8 3.7 collective-permute-start.1
  580.7 0.7 copy-start.5
  871.7 4.4 copy-start.3
  1156.2 3.1 collective-permute-start.2
  1158.0 3.6 collective-permute-start.3
  1164.3 1.6 copy-start.8
  1173.3 2.3 copy-start.1
  1173.9 1.7 copy-start.2
  1182.1 30.6 %collective-permute-start.4 = (bf16[8,256,320]{1,2,0:T(8,128)(2,1)S(1)}, bf16[8,256,320]{1,2,0:T(8,128)(2,1)}, u32[]{:S(2)}, u32[]{:S(2)}) collective-permute-start(bf16[8,256,320]{1,2,0:T(8,128)(2,1)S(1)} %bitcast.101), channel_id=1, source_target_pairs={{0,128},{1,129},{2,130},{3,131},{4,132},{5,133},{6,134},{7,135},{8... | collective-permute-start | bytes 3932168 | tf_op jit(solution)/shard_map/ppermute | solution.py:25
where the time goes:
time: 1240 us; the launch traced here: 1220 us
  blocking collectives  1120 us (90%)
  waiting for transfers between devices  33.8 us (3%)
  local copies, waits for them, and re-layouts  24.9 us (2%)
  other arithmetic  22.1 us (2%)
  matrix products  17.8 us (1%)
    psum x2, blocking collectives, group_stats(): total = lax.psum(part_sums(values, groups), 'strip')  565 us
    psum x2, blocking collectives, group_stats(): spread = lax.psum(part_sums(centered * centered, groups), 'strip')  551 us
    ppermute x1, waiting for transfers between devices, passed_along(): return lax.ppermute(block, axis, route)  29.3 us
  transfers between devices with their start and end apart: 5, of which 3 were waited for; matrix products, arithmetic and copies ran while one was open for 0% of the time, Pallas kernels for 0%

commit v1 on v0

v1 whole, which is shorter than its diff:
```python
import functools

import jax
import jax.numpy as jnp
from jax import lax
from jax.experimental import pallas as pl
from jax.experimental.pallas import tpu as pltpu
from jax.sharding import PartitionSpec as P

G = 32
F32 = jnp.float32
BF16 = jnp.bfloat16
VMEM = pl.BlockSpec(memory_space=pltpu.VMEM)
SMEM = pl.BlockSpec(memory_space=pltpu.SMEM)
LANES = 128
EARLY = 2


def call(kernel, name, ins, outs, scratch, mib, flops):
    return pl.pallas_call(
        kernel,
        out_shape=outs,
        in_specs=[SMEM] + [VMEM] * ins,
        out_specs=[VMEM] * len(outs),
        scratch_shapes=scratch,
        compiler_params=pltpu.CompilerParams(vmem_limit_bytes=mib * 2**20),
        cost_estimate=pl.CostEstimate(flops=flops, bytes_accessed=4 * 2**20, transcendentals=0),
        name=name,
    )


def group_masks(channels):
    per = channels // G
    ch = lax.broadcasted_iota(jnp.int32, (channels, LANES), 0)
    low = lax.broadcasted_iota(jnp.int32, (channels, LANES), 1) * per
    high = low - G * per
    first = jnp.where((ch >= low) & (ch < low + per), 1.0, 0.0)
    second = jnp.where((ch >= high) & (ch < high + per), 1.0, 0.0)
    return first, second


def column(row):
    n = row.shape[1]
    eye = lax.broadcasted_iota(jnp.int32, (n, n), 0) == lax.broadcasted_iota(jnp.int32, (n, n), 1)
    return jnp.sum(jnp.where(eye, row, 0.0), axis=1, keepdims=True)


def fold(x):
    parts = [x[:, i : i + LANES] for i in range(0, x.shape[1], LANES)]
    return functools.reduce(jnp.add, parts)


def strip_stats(load, rows, channels, width):
    first, second = group_masks(channels)
    count = rows * width * (channels // G)
    total = functools.reduce(jnp.add, [fold(load(r)) for r in range(rows)])
    total = jnp.sum(total, axis=1, keepdims=True)
    mean = jnp.sum(first * total, axis=0, keepdims=True) / count
    mean_c = jnp.sum(first * mean, axis=1, keepdims=True)
    squares = functools.reduce(
        jnp.add, [fold((load(r) - mean_c) * (load(r) - mean_c)) for r in range(rows)]
    )
    squares = jnp.sum(squares, axis=1, keepdims=True)
    return mean + jnp.sum(second * squares, axis=0, keepdims=True)


def whole_stats(stats, channels, count):
    first, second = group_masks(channels)
    strips = stats.shape[0]
    total = jnp.sum(stats, axis=0, keepdims=True)
    mean = total / strips
    off = stats - mean
    between = jnp.sum(off * off, axis=0, keepdims=True) * count
    mean_c = jnp.sum(first * mean, axis=1, keepdims=True)
    variance = jnp.sum(first * between + second * total, axis=1, keepdims=True) / (strips * count)
    return mean_c, lax.rsqrt(variance + 1e-5)


def silu(v):
    half = 0.5 * v
    return half + half * jnp.tanh(half)


def turned(w, out):
    c = w.shape[2]
    for kx in range(3):
        out[kx * c : (kx + 1) * c, :] = jnp.concatenate([w[ky, kx].T for ky in range(3)], axis=1)


def conv_row(wt, rows):
    c, w = rows.shape[0] // 3, rows.shape[1]
    y = jnp.dot(wt, rows, preferred_element_type=F32)
    lane = lax.broadcasted_iota(jnp.int32, (c, w), 1)
    left = jnp.where(lane == 0, 0.0, pltpu.roll(y[:c], 1, 1))
    right = jnp.where(lane == w - 1, 0.0, pltpu.roll(y[2 * c :], w - 1, 1))
    return y[c : 2 * c] + left + right


def stats_kernel(pos, x, w, out, wt):
    rows, c, width = x.shape
    st = strip_stats(lambda r: x[r].astype(F32), rows, c, width)
    out[...] = jnp.broadcast_to(st, out.shape)
    turned(w, wt)


def first_kernel(pos, x, low, high, st, gains, shift, wt, w2, z, mid, out, w2t, zt, acts):
    rows, c, width = x.shape
    mean, scale = whole_stats(st[...], c, rows * width * (c // G))
    scale = scale * column(gains[0:1, :])
    shift_c = column(shift[...])
    top = jnp.where(pos[0] == 0, 0.0, 1.0)
    bottom = jnp.where(pos[0] == pos[1] - 1, 0.0, 1.0)

    def put(at):
        if at < 2:
            v, keep = low[at], top
        elif at < rows + 2:
            v, keep = x[at - 2], None
        else:
            v, keep = high[at - rows - 2], bottom
        a = silu((v.astype(F32) - mean) * scale)
        if keep is not None:
            a = a * keep
        acts[at * c : (at + 1) * c, :] = a.astype(BF16)

    for at in range(3):
        put(at)
    for r in range(rows + 2):
        mid[r] = conv_row(wt[...], acts[r * c : (r + 3) * c, :]) + shift_c
        if r + 3 < rows + 4:
            put(r + 3)
    turned(w2, w2t)
    zt[...] = z[...].T
    st2 = strip_stats(lambda r: mid[r + 1], rows, c, width)
    out[...] = jnp.broadcast_to(st2, out.shape)


def second_kernel(begin, end, pos, x, mid, st, gains, w2t, zt, block, residual, acts):
    rows, c, width = x.shape
    mean, scale = whole_stats(st[...], c, rows * width * (c // G))
    scale = scale * column(gains[1:2, :])
    top = jnp.where(pos[0] == 0, 0.0, 1.0)
    bottom = jnp.where(pos[0] == pos[1] - 1, 0.0, 1.0)

    def put(at):
        a = silu((mid[begin + at] - mean) * scale)
        if begin + at == 0:
            a = a * top
        if begin + at == rows + 1:
            a = a * bottom
        acts[at * c : (at + 1) * c, :] = a.astype(BF16)

    for at in range(3):
        put(at)
    for r in range(end - begin):
        y = x[begin + r].astype(F32) + conv_row(w2t[...], acts[r * c : (r + 3) * c, :])
        block[r] = y
        control = y.astype(BF16)
        residual[r] = jnp.dot(zt[...], control, preferred_element_type=F32).astype(BF16)
        if r + 3 < end - begin + 2:
            put(r + 3)


def mix_kernel(pos, block, arrived, *rest):
    out = rest[-1]
    unet = pos[2] == 1
    for r in range(block.shape[0]):
        add = jnp.where(unet, arrived[r].astype(F32), 0.0)
        out[r] = (block[r] + add).astype(BF16)


def mix(pos, block, arrived, begin, whole, old):
    n, c, width = block.shape
    piece = pl.BlockSpec((EARLY, c, width), lambda i: (i, 0, 0))
    held = [] if old is None else [old]
    return pl.pallas_call(
        mix_kernel,
        out_shape=whole,
        grid=(n // EARLY,),
        in_specs=[SMEM, piece, piece] + [pl.BlockSpec(memory_space=pl.ANY)] * len(held),
        out_specs=pl.BlockSpec((EARLY, c, width), lambda i: (i + begin // EARLY, 0, 0)),
        input_output_aliases={3: 0} if held else {},
        cost_estimate=pl.CostEstimate(flops=10**6, bytes_accessed=2**21, transcendentals=0),
        name="mix",
    )(pos, block, arrived, *held)


def on_device(feats, conv_first, conv_second, time_shift, norm_gains, zero_conv):
    strips = lax.axis_size("strip")
    here = lax.axis_index("strip")
    pos = jnp.stack([here, strips, lax.axis_index("branch")]).astype(jnp.int32)
    x = jnp.transpose(feats[0], (0, 2, 1))
    rows, c, width = x.shape
    down = [(i, i + 1) for i in range(strips - 1)]
    up = [(i + 1, i) for i in range(strips - 1)]
    low = lax.ppermute(x[rows - 2 :], "strip", down)
    high = lax.ppermute(x[:2], "strip", up)
    stat = jax.ShapeDtypeStruct((strips, LANES), F32)
    wide = jax.ShapeDtypeStruct((3 * c, 3 * c), BF16)
    row_macs = 2 * 9 * c * c * width

    def spread(st):
        return lax.all_to_all(st, "strip", 0, 0)

    st1, w1t = call(stats_kernel, "stats_first", 2, (stat, wide), [], 24, 10**7)(
        pos, x, conv_first[0]
    )
    st1 = spread(st1)
    mid, st2, w2t, zt = call(
        first_kernel,
        "conv_first",
        9,
        (
            jax.ShapeDtypeStruct((rows + 2, c, width), F32),
            stat,
            wide,
            jax.ShapeDtypeStruct((c, c), BF16),
        ),
        [pltpu.VMEM(((rows + 4) * c, width), BF16)],
        40,
        10 * row_macs,
    )(pos, x, low, high, st1, norm_gains[0], time_shift, w1t, conv_second[0], zero_conv)
    st2 = spread(st2)
    branches = [(0, 1)]
    pieces = []
    for begin, end in ((0, EARLY), (EARLY, rows)):
        n = end - begin
        block, residual = call(
            functools.partial(second_kernel, begin, end),
            "conv_second",
            6,
            (
                jax.ShapeDtypeStruct((n, c, width), F32),
                jax.ShapeDtypeStruct((n, c, width), BF16),
            ),
            [pltpu.VMEM(((n + 2) * c, width), BF16)],
            32,
            n * row_macs,
        )(pos, x, mid, st2, norm_gains[0], w2t, zt)
        pieces.append((begin, block, lax.ppermute(residual, "branch", branches)))
    whole = jax.ShapeDtypeStruct((rows, c, width), BF16)
    out = None
    for begin, block, arrived in pieces:
        out = mix(pos, block, arrived, begin, whole, out)
    return jnp.transpose(out, (0, 2, 1))[None]


def solution(mesh):
    placed = (
        P("branch", "strip", None, None),
        P("branch", None, None, None, None),
        P("branch", None, None, None, None),
        P("branch", None),
        P("branch", None, None),
        P(),
    )
    return jax.shard_map(
        on_device,
        mesh=mesh,
        in_specs=placed,
        out_specs=P("branch", "strip", None, None),
        check_vma=False,
    )
```

time: 1240 us -> 112 us (0.09); the launches traced: 1220 us -> 111 us
  blocking collectives: 1120 us -> 43 us
  Pallas kernels: 0 us -> 27.6 us
  other arithmetic: 22.1 us -> 0.08 us
  local copies, waits for them, and re-layouts: 24.9 us -> 6.7 us
  matrix products: 17.8 us -> 0 us
    psum x4 -> x0, blocking collectives: 1120 us -> none  [the longest x2 565 us: group_stats(): total = lax.psum(part_sums(values, groups), 'strip')]
    all_to_all x0 -> x2, blocking collectives: none -> 43 us  [spread(): return lax.all_to_all(st, 'strip', 0, 0)]
    pallas_call x0 -> x6, Pallas kernels: none -> 27.6 us  [the longest x2 12.8 us: on_device(): call(functools.partial(second_kernel, begin, end), 'conv_second', 6, (jax...]
    conv_general_dilated x2 -> x0, matrix products: 16 us -> none  [conv_rows(): lax.conv_general_dilated(inputs[None], kernel, (1, 1), ((0, 0), (1, 1)),...]
    ppermute x5 -> x4, waiting for transfers between devices: 33.8 us -> 26.8 us  [the longest x2 26.8 us: on_device(): pieces.append((begin, block, lax.ppermute(residual, 'branch', branches)))]
  transfers between devices with their start and end apart: 5 -> 4, of which waited for: 3 -> 1; matrix products, arithmetic and copies ran while one was open for 0% -> 0% of each run, Pallas kernels for 0% -> 7%
where the time goes in v1:
time: 112 us; the launch traced here: 111 us
  blocking collectives  43 us (38%)
  Pallas kernels  27.6 us (25%)
  waiting for transfers between devices  26.8 us (24%)
  starting transfers between devices  6.9 us (6%)
  local copies, waits for them, and re-layouts  6.7 us (6%)
    all_to_all x2, blocking collectives, spread(): return lax.all_to_all(st, 'strip', 0, 0)  43 us
    ppermute x2, waiting for transfers between devices, on_device(): pieces.append((begin, block, lax.ppermute(residual, 'branch', branches)))  26.8 us
    pallas_call x2, Pallas kernels, on_device(): call(functools.partial(second_kernel, begin, end), 'conv_second', 6, (jax...  12.8 us
    pallas_call x1, Pallas kernels, on_device(): call(first_kernel, 'conv_first', 9, (jax.ShapeDtypeStruct((rows + 2, c, w...  7.25 us
    pallas_call x2, Pallas kernels, mix(): pl.pallas_call(mix_kernel, out_shape=whole, grid=(n // EARLY,), in_specs=...  5.52 us
    unnamed x22, local copies, waits for them, and re-layouts  5.48 us
    ppermute x1, starting transfers between devices, on_device(): low = lax.ppermute(x[rows - 2:], 'strip', down)  3.05 us
    ppermute x2, starting transfers between devices, on_device(): pieces.append((begin, block, lax.ppermute(residual, 'branch', branches)))  2.56 us
  transfers between devices with their start and end apart: 4, of which 1 were waited for; matrix products, arithmetic and copies ran while one was open for 0% of the time, Pallas kernels for 7%

profile of v1, /device:TPU:16, one launch (start us, length us, event | category | flops | bytes accessed | tf_op | source)
XLA Modules:
  0.0 111.2 jit_solution(15128259005109062682)
XLA Ops:
  0.0 1.2 %fusion = (bf16[2,320,256]{2,1,0:T(8,128)(2,1)S(1)}, bf16[2,320,256]{2,1,0:T(8,128)(2,1)S(1)}) fusion(bf16[8,320,256]{2,1,0:T(8,128)(2,1)} %bitcast.19), kind=kLoop, calls=%fused_computation.1 | loop fusion | bytes 1310720 | tf_op jit(solution)/shard_map/slice | solution.py:197
  1.2 0.0 copy-start.5
  1.2 0.0 copy-start.8
  1.2 1.3 %collective-permute-start.1 = (bf16[2,320,256]{2,1,0:T(8,128)(2,1)S(1)}, bf16[2,320,256]{2,1,0:T(8,128)(2,1)S(1)}, u32[]{:S(2)}, u32[]{:S(2)}) collective-permute-start(bf16[2,320,256]{2,1,0:T(8,128)(2,1)S(1)} %get-tuple-element.25), channel_id=1, source_target_pairs={{1,0},{2,1},{3,2},{4,3},{5,4},{6,5},{7,6},{8,7},{9,8},{10,9},{11,1... | collective-permute-start | bytes 983048 | tf_op jit(solution)/shard_map/ppermute | solution.py:197
  2.5 3.1 %collective-permute-start = (bf16[2,320,256]{2,1,0:T(8,128)(2,1)S(1)}, bf16[2,320,256]{2,1,0:T(8,128)(2,1)S(1)}, u32[]{:S(2)}, u32[]{:S(2)}) collective-permute-start(bf16[2,320,256]{2,1,0:T(8,128)(2,1)S(1)} %get-tuple-element.26), channel_id=1, source_target_pairs={{0,1},{1,2},{2,3},{3,4},{4,5},{5,6},{6,7},{7,8},{8,9},{9,10},{10,1... | collective-permute-start | bytes 983048 | tf_op jit(solution)/shard_map/ppermute | solution.py:196
  5.6 0.1 pad_add_fusion.pos
  5.7 1.6 %copy-done.1 = bf16[1,3,3,320,320]{4,3,2,1,0:T(8,128)(2,1)S(1)} copy-done((bf16[1,3,3,320,320]{4,3,2,1,0:T(8,128)(2,1)S(1)}, bf16[1,3,3,320,320]{4,3,2,1,0:T(8,128)(2,1)}, u32[]{:S(2)}) %copy-start.1) | copy-done | bytes 1843224
  7.3 2.0 %stats_first.1 = (f32[128,128]{1,0:T(8,128)S(1)}, bf16[960,960]{1,0:T(8,128)(2,1)S(1)}) custom-call(s32[3]{0:T(128)S(1)} %pad_add_fusion.pos, bf16[8,320,256]{2,1,0:T(8,128)(2,1)S(1)} %bitcast.20, bf16[3,3,320,320]{3,2,1,0:T(8,128)(2,1)S(1)} %bitcast.24), custom_call_target="tpu_custom_call" | custom-call | flops 10000000 | bytes 4194304 | tf_op jit(solution)/shard_map/stats_first/pallas_call | solution.py:205
  9.3 26.8 %all_to_all.22 = f32[128,1,128]{2,1,0:T(1,128)S(1)} all-to-all(f32[128,1,128]{2,1,0:T(1,128)S(1)} %bitcast.29), channel_id=1, replica_groups=mesh['branch'=2,'strip'=128] {'strip'}, dimensions={0} | all-to-all | bytes 131072 | tf_op jit(solution)/shard_map/all_to_all | solution.py:203
  36.2 0.0 collective-permute-done.1.high
  36.2 0.0 collective-permute-done.low
  36.2 7.3 %conv_first.1 = (f32[10,320,256]{2,1,0:T(8,128)S(1)}, f32[128,128]{1,0:T(8,128)S(1)}, bf16[960,960]{1,0:T(8,128)(2,1)S(1)}, bf16[320,320]{1,0:T(8,128)(2,1)S(1)}) custom-call(s32[3]{0:T(128)S(1)} %pad_add_fusion.pos, bf16[8,320,256]{2,1,0:T(8,128)(2,1)S(1)} %bitcast.21, bf16[2,320,256]{2,1,0:T(8,128)(2,1)S(1)} %collective-permute-done.low, ...), custom_call_target="tpu_custom_call" | custom-call | flops 4718592000 | bytes 4194304 | tf_op jit(solution)/shard_map/conv_first/pallas_call | solution.py:209
  43.5 16.1 %all_to_all.23 = f32[128,1,128]{2,1,0:T(1,128)S(1)} all-to-all(f32[128,1,128]{2,1,0:T(1,128)S(1)} %bitcast.28), channel_id=1, replica_groups=mesh['branch'=2,'strip'=128] {'strip'}, dimensions={0} | all-to-all | bytes 131072 | tf_op jit(solution)/shard_map/all_to_all | solution.py:203
  59.6 9.1 %conv_second.2 = (f32[6,320,256]{2,1,0:T(8,128)S(1)}, bf16[6,320,256]{2,1,0:T(8,128)(2,1)S(1)}) custom-call(s32[3]{0:T(128)S(1)} %pad_add_fusion.pos, bf16[8,320,256]{2,1,0:T(8,128)(2,1)S(1)} %bitcast.22, f32[10,320,256]{2,1,0:T(8,128)S(1)} %get-tuple-element.17.mid, f32[128,128]{1,0:T(8,128)S(1)} %bitcast.25, f32[2,320]{1,0:T(2,128)S(1)} %bitcast.31, ...), custom_call_target="tpu_custom_call" | custom-call | flops 2831155200 | bytes 4194304 | tf_op jit(solution)/shard_map/conv_second/pallas_call | solution.py:228
  68.8 1.3 %copy-done.2 = f32[6,320,256]{2,1,0:T(8,128)} copy-done((f32[6,320,256]{2,1,0:T(8,128)}, f32[6,320,256]{2,1,0:T(8,128)S(1)}, u32[]{:S(2)}) %copy-start.2) | copy-done | bytes 1966104
  70.1 1.3 %collective-permute-start.2 = (bf16[6,320,256]{2,1,0:T(8,128)(2,1)S(1)}, bf16[6,320,256]{2,1,0:T(8,128)(2,1)S(1)}, u32[]{:S(2)}, u32[]{:S(2)}) collective-permute-start(bf16[6,320,256]{2,1,0:T(8,128)(2,1)S(1)} %get-tuple-element.22), channel_id=1, source_target_pairs={{0,128},{1,129},{2,130},{3,131},{4,132},{5,133},{6,134},{7,135},{8... | collective-permute-start | bytes 2949128 | tf_op jit(solution)/shard_map/ppermute | solution.py:240
  71.4 3.7 %conv_second.3 = (f32[2,320,256]{2,1,0:T(8,128)S(1)}, bf16[2,320,256]{2,1,0:T(8,128)(2,1)S(1)}) custom-call(s32[3]{0:T(128)S(1)} %pad_add_fusion.pos, bf16[8,320,256]{2,1,0:T(8,128)(2,1)S(1)} %bitcast.23, f32[10,320,256]{2,1,0:T(8,128)S(1)} %get-tuple-element.17.mid, f32[128,128]{1,0:T(8,128)S(1)} %bitcast.26, f32[2,320]{1,0:T(2,128)S(1)} %bitcast.32, ...), custom_call_target="tpu_custom_call" | custom-call | flops 943718400 | bytes 4194304 | tf_op jit(solution)/shard_map/conv_second/pallas_call | solution.py:228
  75.0 0.8 copy-done.3
  75.9 1.3 %collective-permute-start.3 = (bf16[2,320,256]{2,1,0:T(8,128)(2,1)S(1)}, bf16[2,320,256]{2,1,0:T(8,128)(2,1)S(1)}, u32[]{:S(2)}, u32[]{:S(2)}) collective-permute-start(bf16[2,320,256]{2,1,0:T(8,128)(2,1)S(1)} %get-tuple-element.24), channel_id=1, source_target_pairs={{0,128},{1,129},{2,130},{3,131},{4,132},{5,133},{6,134},{7,135},{8... | collective-permute-start | bytes 983048 | tf_op jit(solution)/shard_map/ppermute | solution.py:240
  77.2 26.8 %collective-permute-done.3.arrived = bf16[2,320,256]{2,1,0:T(8,128)(2,1)S(1)} collective-permute-done((bf16[2,320,256]{2,1,0:T(8,128)(2,1)S(1)}, bf16[2,320,256]{2,1,0:T(8,128)(2,1)S(1)}, u32[]{:S(2)}, u32[]{:S(2)}) %collective-permute-start.3) | collective-permute-done | bytes 327712 | tf_op jit(solution)/shard_map/ppermute | solution.py:240
  104.0 0.7 copy-done.10
  104.7 2.0 %mix.2.rest_0_ = bf16[8,320,256]{2,1,0:T(8,128)(2,1)} custom-call(s32[3]{0:T(128)} %copy-done.4, f32[2,320,256]{2,1,0:T(8,128)} %copy-done.3, bf16[2,320,256]{2,1,0:T(8,128)(2,1)} %copy-done.10), custom_call_target="tpu_custom_call" | custom-call | flops 1000000 | bytes 2097152 | tf_op jit(solution)/shard_map/mix/pallas_call | solution.py:176
  106.7 1.0 copy-done.9
  107.7 3.5 %mix.3 = bf16[8,320,256]{2,1,0:T(8,128)(2,1)} custom-call(s32[3]{0:T(128)} %copy-done.4, f32[6,320,256]{2,1,0:T(8,128)} %copy-done.2, bf16[6,320,256]{2,1,0:T(8,128)(2,1)} %copy-done.9, bf16[8,320,256]{2,1,0:T(8,128)(2,1)} %mix.2.rest_0_), custom_call_target="tpu_custom_call", output_to_operand_aliasing={{}: (3, {})} | custom-call | flops 1000000 | bytes 2097152 | tf_op jit(solution)/shard_map/mix/pallas_call | solution.py:176
  (16 shorter events, 0.0 us)
Async XLA Ops:
  0.0 5.7 %copy-start = (bf16[1,8,256,320]{2,3,1,0:T(8,128)(2,1)S(1)}, bf16[1,8,256,320]{2,3,1,0:T(8,128)(2,1)}, u32[]{:S(2)}) copy-start(bf16[1,8,256,320]{2,3,1,0:T(8,128)(2,1)} %param.6) | copy-start | bytes 3932164
  1.2 35.0 %copy-start.5 = (f32[1,2,320]{2,1,0:T(2,128)S(1)}, f32[1,2,320]{2,1,0:T(2,128)}, u32[]{:S(2)}) copy-start(f32[1,2,320]{2,1,0:T(2,128)} %param.10) | copy-start | bytes 7684
  1.2 35.0 %copy-start.8 = (f32[1,320]{1,0:T(1,128)S(1)}, f32[1,320]{1,0:T(1,128)}, u32[]{:S(2)}) copy-start(f32[1,320]{1,0:T(1,128)} %shift.1) | copy-start | bytes 3844
  1.2 34.9 %collective-permute-start.1 = (bf16[2,320,256]{2,1,0:T(8,128)(2,1)S(1)}, bf16[2,320,256]{2,1,0:T(8,128)(2,1)S(1)}, u32[]{:S(2)}, u32[]{:S(2)}) collective-permute-start(bf16[2,320,256]{2,1,0:T(8,128)(2,1)S(1)} %get-tuple-element.25), channel_id=1, source_target_pairs={{1,0},{2,1},{3,2},{4,3},{5,4},{6,5},{7,6},{8,7},{9,8},{10,9},{11,1... | collective-permute-start | bytes 983048 | tf_op jit(solution)/shard_map/ppermute | solution.py:197
  2.5 33.6 %collective-permute-start = (bf16[2,320,256]{2,1,0:T(8,128)(2,1)S(1)}, bf16[2,320,256]{2,1,0:T(8,128)(2,1)S(1)}, u32[]{:S(2)}, u32[]{:S(2)}) collective-permute-start(bf16[2,320,256]{2,1,0:T(8,128)(2,1)S(1)} %get-tuple-element.26), channel_id=1, source_target_pairs={{0,1},{1,2},{2,3},{3,4},{4,5},{5,6},{6,7},{7,8},{8,9},{9,10},{10,1... | collective-permute-start | bytes 983048 | tf_op jit(solution)/shard_map/ppermute | solution.py:196
  5.7 65.7 %copy-start.4 = (s32[3]{0:T(128)}, s32[3]{0:T(128)S(1)}, u32[]{:S(2)}) copy-start(s32[3]{0:T(128)S(1)} %pad_add_fusion.pos) | copy-start | bytes 40
  5.7 1.6 %copy-start.1 = (bf16[1,3,3,320,320]{4,3,2,1,0:T(8,128)(2,1)S(1)}, bf16[1,3,3,320,320]{4,3,2,1,0:T(8,128)(2,1)}, u32[]{:S(2)}) copy-start(bf16[1,3,3,320,320]{4,3,2,1,0:T(8,128)(2,1)} %param.7) | copy-start | bytes 5529604
  7.3 28.9 %copy-start.6 = (bf16[1,3,3,320,320]{4,3,2,1,0:T(8,128)(2,1)S(1)}, bf16[1,3,3,320,320]{4,3,2,1,0:T(8,128)(2,1)}, u32[]{:S(2)}) copy-start(bf16[1,3,3,320,320]{4,3,2,1,0:T(8,128)(2,1)} %param.8) | copy-start | bytes 5529604
  7.3 28.9 %copy-start.7 = (bf16[320,320]{1,0:T(8,128)(2,1)S(1)}, bf16[320,320]{1,0:T(8,128)(2,1)}, u32[]{:S(2)}) copy-start(bf16[320,320]{1,0:T(8,128)(2,1)} %z.1) | copy-start | bytes 614404
  68.8 1.3 %copy-start.2 = (f32[6,320,256]{2,1,0:T(8,128)}, f32[6,320,256]{2,1,0:T(8,128)S(1)}, u32[]{:S(2)}) copy-start(f32[6,320,256]{2,1,0:T(8,128)S(1)} %get-tuple-element.21.block) | copy-start | bytes 5898244
  70.1 36.6 %collective-permute-start.2 = (bf16[6,320,256]{2,1,0:T(8,128)(2,1)S(1)}, bf16[6,320,256]{2,1,0:T(8,128)(2,1)S(1)}, u32[]{:S(2)}, u32[]{:S(2)}) collective-permute-start(bf16[6,320,256]{2,1,0:T(8,128)(2,1)S(1)} %get-tuple-element.22), channel_id=1, source_target_pairs={{0,128},{1,129},{2,130},{3,131},{4,132},{5,133},{6,134},{7,135},{8... | collective-permute-start | bytes 2949128 | tf_op jit(solution)/shard_map/ppermute | solution.py:240
  75.0 0.8 copy-start.3
  75.9 28.1 %collective-permute-start.3 = (bf16[2,320,256]{2,1,0:T(8,128)(2,1)S(1)}, bf16[2,320,256]{2,1,0:T(8,128)(2,1)S(1)}, u32[]{:S(2)}, u32[]{:S(2)}) collective-permute-start(bf16[2,320,256]{2,1,0:T(8,128)(2,1)S(1)} %get-tuple-element.24), channel_id=1, source_target_pairs={{0,128},{1,129},{2,130},{3,131},{4,132},{5,133},{6,134},{7,135},{8... | collective-permute-start | bytes 983048 | tf_op jit(solution)/shard_map/ppermute | solution.py:240
  104.0 0.7 copy-start.10
  106.7 1.0 copy-start.9

commit v2 on v1

--- a/solution.py
+++ b/solution.py
@@ -12,15 +12,15 @@
 BF16 = jnp.bfloat16
 VMEM = pl.BlockSpec(memory_space=pltpu.VMEM)
 SMEM = pl.BlockSpec(memory_space=pltpu.SMEM)
+ANYWHERE = pl.BlockSpec(memory_space=pl.ANY)
 LANES = 128
-EARLY = 2
-
-
-def call(kernel, name, ins, outs, scratch, mib, flops):
+
+
+def call(kernel, name, ins, outs, scratch, mib, flops, unread=0):
     return pl.pallas_call(
         kernel,
         out_shape=outs,
-        in_specs=[SMEM] + [VMEM] * ins,
+        in_specs=[SMEM] + [VMEM] * ins + [ANYWHERE] * unread,
         out_specs=[VMEM] * len(outs),
         scratch_shapes=scratch,
         compiler_params=pltpu.CompilerParams(vmem_limit_bytes=mib * 2**20),
@@ -96,20 +96,25 @@
     return y[c : 2 * c] + left + right
 
 
-def stats_kernel(pos, x, w, out, wt):
+def stats_kernel(pos, x, out, first_rows, last_rows):
     rows, c, width = x.shape
     st = strip_stats(lambda r: x[r].astype(F32), rows, c, width)
     out[...] = jnp.broadcast_to(st, out.shape)
-    turned(w, wt)
-
-
-def first_kernel(pos, x, low, high, st, gains, shift, wt, w2, z, mid, out, w2t, zt, acts):
+    first_rows[...] = x[:2]
+    last_rows[...] = x[rows - 2 :]
+
+
+def edge_flags(pos):
+    return jnp.where(pos[0] == 0, 0.0, 1.0), jnp.where(pos[0] == pos[1] - 1, 0.0, 1.0)
+
+
+def first_kernel(
+    pos, x, low, high, st, gains, shift, w1, w2, z, mid, out, edges, w1t, w2t, zt, cols, acts
+):
     rows, c, width = x.shape
     mean, scale = whole_stats(st[...], c, rows * width * (c // G))
     scale = scale * column(gains[0:1, :])
-    shift_c = column(shift[...])
-    top = jnp.where(pos[0] == 0, 0.0, 1.0)
-    bottom = jnp.where(pos[0] == pos[1] - 1, 0.0, 1.0)
+    top, bottom = edge_flags(pos)
 
     def put(at):
         if at < 2:
@@ -123,63 +128,111 @@
             a = a * keep
         acts[at * c : (at + 1) * c, :] = a.astype(BF16)
 
-    for at in range(3):
+    for at in (1, 2, 3):
         put(at)
-    for r in range(rows + 2):
-        mid[r] = conv_row(wt[...], acts[r * c : (r + 3) * c, :]) + shift_c
-        if r + 3 < rows + 4:
+    turned(w1, w1t)
+    shift_c = column(shift[...])
+    cols[...] = jnp.broadcast_to(
+        jnp.concatenate([shift_c, column(gains[1:2, :])], axis=0), cols.shape
+    )
+    first, second = group_masks(c)
+    per_row = width * (c // G)
+    for r in range(1, rows + 1):
+        y = conv_row(w1t[...], acts[r * c : (r + 3) * c, :]) + shift_c
+        mid[r - 1] = y
+        if r == 1:
+            total = fold(y)
+            row_sum = jnp.sum(first * jnp.sum(total, axis=1, keepdims=True), axis=0, keepdims=True)
+            about = row_sum / per_row
+            about_c = jnp.sum(first * about, axis=1, keepdims=True)
+            squares = fold((y - about_c) * (y - about_c))
+        else:
+            total = total + fold(y)
+            squares = squares + fold((y - about_c) * (y - about_c))
+        if r < rows:
             put(r + 3)
+    count = rows * per_row
+    total = jnp.sum(total, axis=1, keepdims=True)
+    squares = jnp.sum(squares, axis=1, keepdims=True)
+    own_mean = jnp.sum(first * total, axis=0, keepdims=True) / count
+    off = jnp.sum(first * (own_mean - about), axis=1, keepdims=True)
+    squares = squares - off * off * (rows * width)
+    st2 = own_mean + jnp.sum(second * squares, axis=0, keepdims=True)
+    out[...] = jnp.broadcast_to(st2, out.shape)
+    put(0)
+    put(rows + 3)
     turned(w2, w2t)
     zt[...] = z[...].T
-    st2 = strip_stats(lambda r: mid[r + 1], rows, c, width)
-    out[...] = jnp.broadcast_to(st2, out.shape)
-
-
-def second_kernel(begin, end, pos, x, mid, st, gains, w2t, zt, block, residual, acts):
+    edges[: 3 * c, :] = acts[: 3 * c, :]
+    edges[3 * c :, :] = acts[(rows + 1) * c :, :]
+
+
+def second_kernel(wanted, pos, x, mid, st, cols, w2t, zt, edges, w1t, after, *outs):
+    block, residual, acts, control = outs
     rows, c, width = x.shape
     mean, scale = whole_stats(st[...], c, rows * width * (c // G))
-    scale = scale * column(gains[1:2, :])
-    top = jnp.where(pos[0] == 0, 0.0, 1.0)
-    bottom = jnp.where(pos[0] == pos[1] - 1, 0.0, 1.0)
-
-    def put(at):
-        a = silu((mid[begin + at] - mean) * scale)
-        if begin + at == 0:
+    scale = scale * cols[c:, :1]
+    top, bottom = edge_flags(pos)
+
+    def put(at, slot):
+        if at == 0:
+            v = conv_row(w1t[...], edges[: 3 * c, :]) + cols[:c, :1]
+        elif at == rows + 1:
+            v = conv_row(w1t[...], edges[3 * c :, :]) + cols[:c, :1]
+        else:
+            v = mid[at - 1]
+        a = silu((v - mean) * scale)
+        if at == 0:
             a = a * top
-        if begin + at == rows + 1:
+        if at == rows + 1:
             a = a * bottom
-        acts[at * c : (at + 1) * c, :] = a.astype(BF16)
-
-    for at in range(3):
-        put(at)
-    for r in range(end - begin):
-        y = x[begin + r].astype(F32) + conv_row(w2t[...], acts[r * c : (r + 3) * c, :])
-        block[r] = y
-        control = y.astype(BF16)
-        residual[r] = jnp.dot(zt[...], control, preferred_element_type=F32).astype(BF16)
-        if r + 3 < end - begin + 2:
-            put(r + 3)
-
-
-def mix_kernel(pos, block, arrived, *rest):
-    out = rest[-1]
+        acts[slot * c : (slot + 1) * c, :] = a.astype(BF16)
+
+    done = 0
+    slot = 0
+    for begin, end in wanted:
+        base = slot
+        for at in range(begin, end + 2):
+            put(at, slot)
+            slot += 1
+        for r in range(begin, end):
+            at = (base + r - begin) * c
+            y = x[r].astype(F32) + conv_row(w2t[...], acts[at : at + 3 * c, :])
+            block[done] = y
+            control[done * c : (done + 1) * c, :] = y.astype(BF16)
+            done += 1
+    for r in range(done):
+        residual[r] = jnp.dot(
+            zt[...], control[r * c : (r + 1) * c, :], preferred_element_type=F32
+        ).astype(BF16)
+
+
+def mix_kernel(wanted, pos, block, arrived, *rest):
+    whole, held, sem = rest[-3:]
     unet = pos[2] == 1
-    for r in range(block.shape[0]):
+    copies = []
+    for r, to in enumerate(wanted):
         add = jnp.where(unet, arrived[r].astype(F32), 0.0)
-        out[r] = (block[r] + add).astype(BF16)
-
-
-def mix(pos, block, arrived, begin, whole, old):
-    n, c, width = block.shape
-    piece = pl.BlockSpec((EARLY, c, width), lambda i: (i, 0, 0))
+        held[r] = (block[r] + add).astype(BF16)
+        copies.append(pltpu.make_async_copy(held.at[r], whole.at[to], sem.at[r]))
+        copies[-1].start()
+    for copy in copies:
+        copy.wait()
+
+
+def mix(pos, block, arrived, wanted, whole, old):
     held = [] if old is None else [old]
     return pl.pallas_call(
-        mix_kernel,
+        functools.partial(mix_kernel, wanted),
         out_shape=whole,
-        grid=(n // EARLY,),
-        in_specs=[SMEM, piece, piece] + [pl.BlockSpec(memory_space=pl.ANY)] * len(held),
-        out_specs=pl.BlockSpec((EARLY, c, width), lambda i: (i + begin // EARLY, 0, 0)),
+        in_specs=[SMEM, VMEM, VMEM] + [ANYWHERE] * len(held),
+        out_specs=ANYWHERE,
+        scratch_shapes=[
+            pltpu.VMEM(arrived.shape, BF16),
+            pltpu.SemaphoreType.DMA((len(wanted),)),
+        ],
         input_output_aliases={3: 0} if held else {},
+        compiler_params=pltpu.CompilerParams(vmem_limit_bytes=16 * 2**20),
         cost_estimate=pl.CostEstimate(flops=10**6, bytes_accessed=2**21, transcendentals=0),
         name="mix",
     )(pos, block, arrived, *held)
@@ -193,55 +246,63 @@
     rows, c, width = x.shape
     down = [(i, i + 1) for i in range(strips - 1)]
     up = [(i + 1, i) for i in range(strips - 1)]
-    low = lax.ppermute(x[rows - 2 :], "strip", down)
-    high = lax.ppermute(x[:2], "strip", up)
-    stat = jax.ShapeDtypeStruct((strips, LANES), F32)
-    wide = jax.ShapeDtypeStruct((3 * c, 3 * c), BF16)
+    shaped = jax.ShapeDtypeStruct
+    stat = shaped((strips, LANES), F32)
+    wide = shaped((3 * c, 3 * c), BF16)
+    halo = shaped((2, c, width), BF16)
     row_macs = 2 * 9 * c * c * width
 
     def spread(st):
         return lax.all_to_all(st, "strip", 0, 0)
 
-    st1, w1t = call(stats_kernel, "stats_first", 2, (stat, wide), [], 24, 10**7)(
-        pos, x, conv_first[0]
-    )
+    st1, first_rows, last_rows = call(
+        stats_kernel, "stats_first", 1, (stat, halo, halo), [], 16, 2 * 10**10
+    )(pos, x)
+    low = lax.ppermute(last_rows, "strip", down)
+    high = lax.ppermute(first_rows, "strip", up)
     st1 = spread(st1)
-    mid, st2, w2t, zt = call(
+    mid, st2, edges, w1t, w2t, zt, cols = call(
         first_kernel,
         "conv_first",
         9,
         (
-            jax.ShapeDtypeStruct((rows + 2, c, width), F32),
+            shaped((rows, c, width), F32),
             stat,
+            shaped((6 * c, width), BF16),
             wide,
-            jax.ShapeDtypeStruct((c, c), BF16),
+            wide,
+            shaped((c, c), BF16),
+            shaped((2 * c, LANES), F32),
         ),
         [pltpu.VMEM(((rows + 4) * c, width), BF16)],
-        40,
-        10 * row_macs,
-    )(pos, x, low, high, st1, norm_gains[0], time_shift, w1t, conv_second[0], zero_conv)
+        36,
+        rows * row_macs,
+    )(pos, x, low, high, st1, norm_gains[0], time_shift, conv_first[0], conv_second[0], zero_conv)
     st2 = spread(st2)
-    branches = [(0, 1)]
     pieces = []
-    for begin, end in ((0, EARLY), (EARLY, rows)):
-        n = end - begin
+    after = zt
+    for wanted in (((3, 6),), ((0, 3),), ((6, rows),)):
+        n = sum(end - begin for begin, end in wanted)
         block, residual = call(
-            functools.partial(second_kernel, begin, end),
+            functools.partial(second_kernel, wanted),
             "conv_second",
-            6,
-            (
-                jax.ShapeDtypeStruct((n, c, width), F32),
-                jax.ShapeDtypeStruct((n, c, width), BF16),
-            ),
-            [pltpu.VMEM(((n + 2) * c, width), BF16)],
+            8,
+            (shaped((n, c, width), F32), shaped((n, c, width), BF16)),
+            [
+                pltpu.VMEM(((n + 2 * len(wanted)) * c, width), BF16),
+                pltpu.VMEM((n * c, width), BF16),
+            ],
             32,
             n * row_macs,
-        )(pos, x, mid, st2, norm_gains[0], w2t, zt)
-        pieces.append((begin, block, lax.ppermute(residual, "branch", branches)))
-    whole = jax.ShapeDtypeStruct((rows, c, width), BF16)
+            unread=1,
+        )(pos, x, mid, st2, cols, w2t, zt, edges, w1t, after)
+        after = residual
+        listed = [r for begin, end in wanted for r in range(begin, end)]
+        pieces.append((listed, block, lax.ppermute(residual, "branch", [(0, 1)])))
+    whole = shaped((rows, c, width), BF16)
     out = None
-    for begin, block, arrived in pieces:
-        out = mix(pos, block, arrived, begin, whole, out)
+    for listed, block, arrived in pieces:
+        out = mix(pos, block, arrived, listed, whole, out)
     return jnp.transpose(out, (0, 2, 1))[None]
 
 

time: 112 us -> 95.7 us (0.85)
  waiting for transfers between devices: 26.8 us -> 19.9 us
  local copies, waits for them, and re-layouts: 6.7 us -> 1.34 us
  Pallas kernels: 27.6 us -> 22.9 us
    ppermute x4 -> x5, waiting for transfers between devices: 26.8 us -> 19.9 us  [the longest x3 19.9 us: on_device(): pieces.append((listed, block, lax.ppermute(residual, 'branch', [(0, 1)])))]
    pallas_call x6 -> x8, Pallas kernels: 27.6 us -> 22.9 us  [the longest x3 10.6 us: on_device(): call(functools.partial(second_kernel, wanted), 'conv_second', 8, (shaped(...]
    unnamed x22 -> x14, local copies, waits for them, and re-layouts: 5.48 us -> 1.34 us
    slice x1 -> x0, local copies, waits for them, and re-layouts: 1.22 us -> none  [on_device(): high = lax.ppermute(x[:2], 'strip', up)]
    ppermute x4 -> x5, starting transfers between devices: 6.9 us -> 7.06 us  [the longest x3 3.88 us: on_device(): pieces.append((listed, block, lax.ppermute(residual, 'branch', [(0, 1)])))]
  transfers between devices with their start and end apart: 4 -> 5, of which waited for: 1 -> 3; matrix products, arithmetic and copies ran while one was open for 0% -> 0% of each run, Pallas kernels for 7% -> 11%
where the time goes in v2:
time: 95.7 us; the launch traced here: 95.4 us
  blocking collectives  43.8 us (46%)
  Pallas kernels  22.9 us (24%)
  waiting for transfers between devices  19.9 us (21%)
  starting transfers between devices  7.06 us (7%)
  local copies, waits for them, and re-layouts  1.34 us (1%)
    all_to_all x2, blocking collectives, spread(): return lax.all_to_all(st, 'strip', 0, 0)  43.8 us
    ppermute x3, waiting for transfers between devices, on_device(): pieces.append((listed, block, lax.ppermute(residual, 'branch', [(0, 1)])))  19.9 us
    pallas_call x3, Pallas kernels, on_device(): call(functools.partial(second_kernel, wanted), 'conv_second', 8, (shaped(...  10.6 us
    pallas_call x1, Pallas kernels, on_device(): call(first_kernel, 'conv_first', 9, (shaped((rows, c, width), F32), stat,...  6.9 us
    pallas_call x3, Pallas kernels, mix(): pl.pallas_call(functools.partial(mix_kernel, wanted), out_shape=whole, in...  4.08 us
    ppermute x3, starting transfers between devices, on_device(): pieces.append((listed, block, lax.ppermute(residual, 'branch', [(0, 1)])))  3.88 us
  transfers between devices with their start and end apart: 5, of which 3 were waited for; matrix products, arithmetic and copies ran while one was open for 0% of the time, Pallas kernels for 11%

profile of v2, /device:TPU:16, one launch (start us, length us, event | category | flops | bytes accessed | tf_op | source)
XLA Modules:
  0.0 95.4 jit_solution(2305028651401407061)
XLA Ops:
  0.0 0.1 pad_add_fusion.pos
  0.1 1.3 %copy-done = bf16[1,8,256,320]{2,3,1,0:T(8,128)(2,1)S(1)} copy-done((bf16[1,8,256,320]{2,3,1,0:T(8,128)(2,1)S(1)}, bf16[1,8,256,320]{2,3,1,0:T(8,128)(2,1)}, u32[]{:S(2)}) %copy-start) | copy-done | bytes 1310744
  1.4 0.0 copy-start.5
  1.4 0.0 copy-start.6
  1.4 1.3 %stats_first.1 = (f32[128,128]{1,0:T(8,128)S(1)}, bf16[2,320,256]{2,1,0:T(8,128)(2,1)S(1)}, bf16[2,320,256]{2,1,0:T(8,128)(2,1)S(1)}) custom-call(s32[3]{0:T(128)S(1)} %pad_add_fusion.pos, bf16[8,320,256]{2,1,0:T(8,128)(2,1)S(1)} %bitcast.19), custom_call_target="tpu_custom_call" | custom-call | flops 20000000000 | bytes 4194304 | tf_op jit(solution)/shard_map/stats_first/pallas_call | solution.py:258
  2.7 1.9 %collective-permute-start = (bf16[2,320,256]{2,1,0:T(8,128)(2,1)S(1)}, bf16[2,320,256]{2,1,0:T(8,128)(2,1)S(1)}, u32[]{:S(2)}, u32[]{:S(2)}) collective-permute-start(bf16[2,320,256]{2,1,0:T(8,128)(2,1)S(1)} %get-tuple-element.21), channel_id=1, source_target_pairs={{0,1},{1,2},{2,3},{3,4},{4,5},{5,6},{6,7},{7,8},{8,9},{9,10},{10,1... | collective-permute-start | bytes 983048 | tf_op jit(solution)/shard_map/ppermute | solution.py:261
  4.6 1.3 %collective-permute-start.1 = (bf16[2,320,256]{2,1,0:T(8,128)(2,1)S(1)}, bf16[2,320,256]{2,1,0:T(8,128)(2,1)S(1)}, u32[]{:S(2)}, u32[]{:S(2)}) collective-permute-start(bf16[2,320,256]{2,1,0:T(8,128)(2,1)S(1)} %get-tuple-element.22), channel_id=1, source_target_pairs={{1,0},{2,1},{3,2},{4,3},{5,4},{6,5},{7,6},{8,7},{9,8},{10,9},{11,1... | collective-permute-start | bytes 983048 | tf_op jit(solution)/shard_map/ppermute | solution.py:262
  5.9 27.7 %all_to_all.22 = f32[128,1,128]{2,1,0:T(1,128)S(1)} all-to-all(f32[128,1,128]{2,1,0:T(1,128)S(1)} %bitcast.28), channel_id=1, replica_groups=mesh['branch'=2,'strip'=128] {'strip'}, dimensions={0} | all-to-all | bytes 131072 | tf_op jit(solution)/shard_map/all_to_all | solution.py:256
  33.6 0.0 collective-permute-done.low
  33.6 0.0 collective-permute-done.1.high
  33.6 6.9 %conv_first.1 = (f32[8,320,256]{2,1,0:T(8,128)S(1)}, f32[128,128]{1,0:T(8,128)S(1)}, bf16[1920,256]{1,0:T(8,128)(2,1)S(1)}, bf16[960,960]{1,0:T(8,128)(2,1)S(1)}...) custom-call(s32[3]{0:T(128)S(1)} %pad_add_fusion.pos, ...), custom_call_target="tpu_custom_call" | custom-call | flops 3774873600 | bytes 4194304 | tf_op jit(solution)/shard_map/conv_first/pallas_call | solution.py:264
  40.6 16.1 %all_to_all.23 = f32[128,1,128]{2,1,0:T(1,128)S(1)} all-to-all(f32[128,1,128]{2,1,0:T(1,128)S(1)} %bitcast.29), channel_id=1, replica_groups=mesh['branch'=2,'strip'=128] {'strip'}, dimensions={0} | all-to-all | bytes 131072 | tf_op jit(solution)/shard_map/all_to_all | solution.py:256
  56.7 3.3 %conv_second.3 = (f32[3,320,256]{2,1,0:T(8,128)S(1)}, bf16[3,320,256]{2,1,0:T(8,128)(2,1)S(1)}) custom-call(s32[3]{0:T(128)S(1)} %pad_add_fusion.pos, bf16[8,320,256]{2,1,0:T(8,128)(2,1)S(1)} %bitcast.21, f32[8,320,256]{2,1,0:T(8,128)S(1)} %get-tuple-element.24.mid, f32[128,128]{1,0:T(8,128)S(1)} %bitcast.24, f32[640,128]{1,0:T(8,128)S(1)} %get-tuple-element.26.cols, ...), custom_call_target="tpu_custom_call" | custom-call | flops 1415577600 | bytes 4194304 | tf_op jit(solution)/shard_map/conv_second/pallas_call | solution.py:286
  60.0 1.3 %collective-permute-start.4 = (bf16[3,320,256]{2,1,0:T(8,128)(2,1)S(1)}, bf16[3,320,256]{2,1,0:T(8,128)(2,1)S(1)}, u32[]{:S(2)}, u32[]{:S(2)}) collective-permute-start(bf16[3,320,256]{2,1,0:T(8,128)(2,1)S(1)} %get-tuple-element.31.after), channel_id=1, source_target_pairs={{0,128},{1,129},{2,130},{3,131},{4,132},{5,133},{6,134},{7,135},{8... | collective-permute-start | bytes 1474568 | tf_op jit(solution)/shard_map/ppermute | solution.py:301
  61.3 4.3 %conv_second.4 = (f32[3,320,256]{2,1,0:T(8,128)S(1)}, bf16[3,320,256]{2,1,0:T(8,128)(2,1)S(1)}) custom-call(s32[3]{0:T(128)S(1)} %pad_add_fusion.pos, bf16[8,320,256]{2,1,0:T(8,128)(2,1)S(1)} %bitcast.22, f32[8,320,256]{2,1,0:T(8,128)S(1)} %get-tuple-element.24.mid, f32[128,128]{1,0:T(8,128)S(1)} %bitcast.25, f32[640,128]{1,0:T(8,128)S(1)} %get-tuple-element.26.cols, ...), custom_call_target="tpu_custom_call" | custom-call | flops 1415577600 | bytes 4194304 | tf_op jit(solution)/shard_map/conv_second/pallas_call | solution.py:286
  65.6 1.3 %collective-permute-start.3 = (bf16[3,320,256]{2,1,0:T(8,128)(2,1)S(1)}, bf16[3,320,256]{2,1,0:T(8,128)(2,1)S(1)}, u32[]{:S(2)}, u32[]{:S(2)}) collective-permute-start(bf16[3,320,256]{2,1,0:T(8,128)(2,1)S(1)} %get-tuple-element.32.after), channel_id=1, source_target_pairs={{0,128},{1,129},{2,130},{3,131},{4,132},{5,133},{6,134},{7,135},{8... | collective-permute-start | bytes 1474568 | tf_op jit(solution)/shard_map/ppermute | solution.py:301
  66.9 3.0 %conv_second.5 = (f32[2,320,256]{2,1,0:T(8,128)S(1)}, bf16[2,320,256]{2,1,0:T(8,128)(2,1)S(1)}) custom-call(s32[3]{0:T(128)S(1)} %pad_add_fusion.pos, bf16[8,320,256]{2,1,0:T(8,128)(2,1)S(1)} %bitcast.23, f32[8,320,256]{2,1,0:T(8,128)S(1)} %get-tuple-element.24.mid, f32[128,128]{1,0:T(8,128)S(1)} %bitcast.26, f32[640,128]{1,0:T(8,128)S(1)} %get-tuple-element.26.cols, ...), custom_call_target="tpu_custom_call" | custom-call | flops 943718400 | bytes 4194304 | tf_op jit(solution)/shard_map/conv_second/pallas_call | solution.py:286
  69.9 1.3 %collective-permute-start.2 = (bf16[2,320,256]{2,1,0:T(8,128)(2,1)S(1)}, bf16[2,320,256]{2,1,0:T(8,128)(2,1)S(1)}, u32[]{:S(2)}, u32[]{:S(2)}) collective-permute-start(bf16[2,320,256]{2,1,0:T(8,128)(2,1)S(1)} %get-tuple-element.34), channel_id=1, source_target_pairs={{0,128},{1,129},{2,130},{3,131},{4,132},{5,133},{6,134},{7,135},{8... | collective-permute-start | bytes 983048 | tf_op jit(solution)/shard_map/ppermute | solution.py:301
  71.2 6.3 %collective-permute-done.4.arrived = bf16[3,320,256]{2,1,0:T(8,128)(2,1)S(1)} collective-permute-done((bf16[3,320,256]{2,1,0:T(8,128)(2,1)S(1)}, bf16[3,320,256]{2,1,0:T(8,128)(2,1)S(1)}, u32[]{:S(2)}, u32[]{:S(2)}) %collective-permute-start.4) | collective-permute-done | bytes 491552 | tf_op jit(solution)/shard_map/ppermute | solution.py:301
  77.5 1.4 %mix.3.rest_0_ = bf16[8,320,256]{2,1,0:T(8,128)(2,1)} custom-call(s32[3]{0:T(128)S(1)} %pad_add_fusion.pos, f32[3,320,256]{2,1,0:T(8,128)S(1)} %get-tuple-element.36.block, bf16[3,320,256]{2,1,0:T(8,128)(2,1)S(1)} %collective-permute-done.4.arrived), custom_call_target="tpu_custom_call" | custom-call | flops 1000000 | bytes 2097152 | tf_op jit(solution)/shard_map/mix/pallas_call | solution.py:225
  78.9 9.1 %collective-permute-done.3.arrived = bf16[3,320,256]{2,1,0:T(8,128)(2,1)S(1)} collective-permute-done((bf16[3,320,256]{2,1,0:T(8,128)(2,1)S(1)}, bf16[3,320,256]{2,1,0:T(8,128)(2,1)S(1)}, u32[]{:S(2)}, u32[]{:S(2)}) %collective-permute-start.3) | collective-permute-done | bytes 491552 | tf_op jit(solution)/shard_map/ppermute | solution.py:301
  88.0 1.4 %mix.4.rest_0_ = bf16[8,320,256]{2,1,0:T(8,128)(2,1)} custom-call(s32[3]{0:T(128)S(1)} %pad_add_fusion.pos, f32[3,320,256]{2,1,0:T(8,128)S(1)} %get-tuple-element.35.block, bf16[3,320,256]{2,1,0:T(8,128)(2,1)S(1)} %collective-permute-done.3.arrived, bf16[8,320,256]{2,1,0:T(8,128)(2,1)} %mix.3.rest_0_), custom_call_target="tpu_custom_call", output_to_operand_aliasing={{}: (3, {})} | custom-call | flops 1000000 | bytes 2097152 | tf_op jit(solution)/shard_map/mix/pallas_call | solution.py:225
  89.4 4.5 %collective-permute-done.2.arrived = bf16[2,320,256]{2,1,0:T(8,128)(2,1)S(1)} collective-permute-done((bf16[2,320,256]{2,1,0:T(8,128)(2,1)S(1)}, bf16[2,320,256]{2,1,0:T(8,128)(2,1)S(1)}, u32[]{:S(2)}, u32[]{:S(2)}) %collective-permute-start.2) | collective-permute-done | bytes 327712 | tf_op jit(solution)/shard_map/ppermute | solution.py:301
  93.9 1.3 %mix.5 = bf16[8,320,256]{2,1,0:T(8,128)(2,1)} custom-call(s32[3]{0:T(128)S(1)} %pad_add_fusion.pos, f32[2,320,256]{2,1,0:T(8,128)S(1)} %get-tuple-element.33.block, bf16[2,320,256]{2,1,0:T(8,128)(2,1)S(1)} %collective-permute-done.2.arrived, bf16[8,320,256]{2,1,0:T(8,128)(2,1)} %mix.4.rest_0_), custom_call_target="tpu_custom_call", output_to_operand_aliasing={{}: (3, {})} | custom-call | flops 1000000 | bytes 2097152 | tf_op jit(solution)/shard_map/mix/pallas_call | solution.py:225
  (11 shorter events, 0.0 us)
Async XLA Ops:
  0.1 1.3 %copy-start = (bf16[1,8,256,320]{2,3,1,0:T(8,128)(2,1)S(1)}, bf16[1,8,256,320]{2,3,1,0:T(8,128)(2,1)}, u32[]{:S(2)}) copy-start(bf16[1,8,256,320]{2,3,1,0:T(8,128)(2,1)} %param.6) | copy-start | bytes 3932164
  1.4 32.2 %copy-start.1 = (bf16[1,8,256,320]{2,3,1,0:T(8,128)(2,1)S(1)}, bf16[1,8,256,320]{2,3,1,0:T(8,128)(2,1)}, u32[]{:S(2)}) copy-start(bf16[1,8,256,320]{2,3,1,0:T(8,128)(2,1)} %param.6) | copy-start | bytes 3932164
  1.4 32.2 %copy-start.2 = (bf16[1,3,3,320,320]{4,3,2,1,0:T(8,128)(2,1)S(1)}, bf16[1,3,3,320,320]{4,3,2,1,0:T(8,128)(2,1)}, u32[]{:S(2)}) copy-start(bf16[1,3,3,320,320]{4,3,2,1,0:T(8,128)(2,1)} %param.7) | copy-start | bytes 5529604
  1.4 32.2 %copy-start.3 = (bf16[1,3,3,320,320]{4,3,2,1,0:T(8,128)(2,1)S(1)}, bf16[1,3,3,320,320]{4,3,2,1,0:T(8,128)(2,1)}, u32[]{:S(2)}) copy-start(bf16[1,3,3,320,320]{4,3,2,1,0:T(8,128)(2,1)} %param.8) | copy-start | bytes 5529604
  1.4 32.2 %copy-start.4 = (bf16[320,320]{1,0:T(8,128)(2,1)S(1)}, bf16[320,320]{1,0:T(8,128)(2,1)}, u32[]{:S(2)}) copy-start(bf16[320,320]{1,0:T(8,128)(2,1)} %z.1) | copy-start | bytes 614404
  1.4 32.2 %copy-start.5 = (f32[1,2,320]{2,1,0:T(2,128)S(1)}, f32[1,2,320]{2,1,0:T(2,128)}, u32[]{:S(2)}) copy-start(f32[1,2,320]{2,1,0:T(2,128)} %param.10) | copy-start | bytes 7684
  1.4 32.2 %copy-start.6 = (f32[1,320]{1,0:T(1,128)S(1)}, f32[1,320]{1,0:T(1,128)}, u32[]{:S(2)}) copy-start(f32[1,320]{1,0:T(1,128)} %shift.1) | copy-start | bytes 3844
  2.7 30.9 %collective-permute-start = (bf16[2,320,256]{2,1,0:T(8,128)(2,1)S(1)}, bf16[2,320,256]{2,1,0:T(8,128)(2,1)S(1)}, u32[]{:S(2)}, u32[]{:S(2)}) collective-permute-start(bf16[2,320,256]{2,1,0:T(8,128)(2,1)S(1)} %get-tuple-element.21), channel_id=1, source_target_pairs={{0,1},{1,2},{2,3},{3,4},{4,5},{5,6},{6,7},{7,8},{8,9},{9,10},{10,1... | collective-permute-start | bytes 983048 | tf_op jit(solution)/shard_map/ppermute | solution.py:261
  4.6 29.0 %collective-permute-start.1 = (bf16[2,320,256]{2,1,0:T(8,128)(2,1)S(1)}, bf16[2,320,256]{2,1,0:T(8,128)(2,1)S(1)}, u32[]{:S(2)}, u32[]{:S(2)}) collective-permute-start(bf16[2,320,256]{2,1,0:T(8,128)(2,1)S(1)} %get-tuple-element.22), channel_id=1, source_target_pairs={{1,0},{2,1},{3,2},{4,3},{5,4},{6,5},{7,6},{8,7},{9,8},{10,9},{11,1... | collective-permute-start | bytes 983048 | tf_op jit(solution)/shard_map/ppermute | solution.py:262
  60.0 17.5 %collective-permute-start.4 = (bf16[3,320,256]{2,1,0:T(8,128)(2,1)S(1)}, bf16[3,320,256]{2,1,0:T(8,128)(2,1)S(1)}, u32[]{:S(2)}, u32[]{:S(2)}) collective-permute-start(bf16[3,320,256]{2,1,0:T(8,128)(2,1)S(1)} %get-tuple-element.31.after), channel_id=1, source_target_pairs={{0,128},{1,129},{2,130},{3,131},{4,132},{5,133},{6,134},{7,135},{8... | collective-permute-start | bytes 1474568 | tf_op jit(solution)/shard_map/ppermute | solution.py:301
  65.6 22.4 %collective-permute-start.3 = (bf16[3,320,256]{2,1,0:T(8,128)(2,1)S(1)}, bf16[3,320,256]{2,1,0:T(8,128)(2,1)S(1)}, u32[]{:S(2)}, u32[]{:S(2)}) collective-permute-start(bf16[3,320,256]{2,1,0:T(8,128)(2,1)S(1)} %get-tuple-element.32.after), channel_id=1, source_target_pairs={{0,128},{1,129},{2,130},{3,131},{4,132},{5,133},{6,134},{7,135},{8... | collective-permute-start | bytes 1474568 | tf_op jit(solution)/shard_map/ppermute | solution.py:301
  69.9 24.0 %collective-permute-start.2 = (bf16[2,320,256]{2,1,0:T(8,128)(2,1)S(1)}, bf16[2,320,256]{2,1,0:T(8,128)(2,1)S(1)}, u32[]{:S(2)}, u32[]{:S(2)}) collective-permute-start(bf16[2,320,256]{2,1,0:T(8,128)(2,1)S(1)} %get-tuple-element.34), channel_id=1, source_target_pairs={{0,128},{1,129},{2,130},{3,131},{4,132},{5,133},{6,134},{7,135},{8... | collective-permute-start | bytes 983048 | tf_op jit(solution)/shard_map/ppermute | solution.py:301

commit v3 on v2

--- a/solution.py
+++ b/solution.py
@@ -11,7 +11,6 @@
 F32 = jnp.float32
 BF16 = jnp.bfloat16
 VMEM = pl.BlockSpec(memory_space=pltpu.VMEM)
-SMEM = pl.BlockSpec(memory_space=pltpu.SMEM)
 ANYWHERE = pl.BlockSpec(memory_space=pl.ANY)
 LANES = 128
 
@@ -20,7 +19,7 @@
     return pl.pallas_call(
         kernel,
         out_shape=outs,
-        in_specs=[SMEM] + [VMEM] * ins + [ANYWHERE] * unread,
+        in_specs=[VMEM] * ins + [ANYWHERE] * unread,
         out_specs=[VMEM] * len(outs),
         scratch_shapes=scratch,
         compiler_params=pltpu.CompilerParams(vmem_limit_bytes=mib * 2**20),
@@ -96,34 +95,45 @@
     return y[c : 2 * c] + left + right
 
 
-def stats_kernel(pos, x, out, first_rows, last_rows):
+def stats_kernel(flags, x, out, inner, outer):
     rows, c, width = x.shape
     st = strip_stats(lambda r: x[r].astype(F32), rows, c, width)
     out[...] = jnp.broadcast_to(st, out.shape)
-    first_rows[...] = x[:2]
-    last_rows[...] = x[rows - 2 :]
-
-
-def edge_flags(pos):
-    return jnp.where(pos[0] == 0, 0.0, 1.0), jnp.where(pos[0] == pos[1] - 1, 0.0, 1.0)
+    even = flags[3:4, :1] > 0.5
+    for i in range(2):
+        begin, end = x[i].astype(F32), x[rows - 2 + i].astype(F32)
+        inner[i] = jnp.where(even, end, begin).astype(BF16)
+        outer[i] = jnp.where(even, begin, end).astype(BF16)
+
+
+def strip_flags(strips):
+    here = lax.axis_index("strip")
+    values = [here > 0, here < strips - 1, lax.axis_index("branch") == 1, here % 2 == 0]
+    at = lax.broadcasted_iota(jnp.int32, (8, LANES), 0)
+    return functools.reduce(
+        jnp.add, [jnp.where((at == i) & v, 1.0, 0.0) for i, v in enumerate(values)]
+    )
 
 
 def first_kernel(
-    pos, x, low, high, st, gains, shift, w1, w2, z, mid, out, edges, w1t, w2t, zt, cols, acts
+    flags, x, inner, outer, st, gains, shift, w1, w2, z, mid, out, edges, w1t, w2t, zt, cols, acts
 ):
     rows, c, width = x.shape
     mean, scale = whole_stats(st[...], c, rows * width * (c // G))
     scale = scale * column(gains[0:1, :])
-    top, bottom = edge_flags(pos)
+    top, bottom = flags[0:1, :1], flags[1:2, :1]
+    even = flags[3:4, :1] > 0.5
 
     def put(at):
         if at < 2:
-            v, keep = low[at], top
+            v, keep = jnp.where(even, outer[at].astype(F32), inner[at].astype(F32)), top
         elif at < rows + 2:
-            v, keep = x[at - 2], None
+            v, keep = x[at - 2].astype(F32), None
         else:
-            v, keep = high[at - rows - 2], bottom
-        a = silu((v.astype(F32) - mean) * scale)
+            at_high = at - rows - 2
+            v = jnp.where(even, inner[at_high].astype(F32), outer[at_high].astype(F32))
+            keep = bottom
+        a = silu((v - mean) * scale)
         if keep is not None:
             a = a * keep
         acts[at * c : (at + 1) * c, :] = a.astype(BF16)
@@ -167,12 +177,12 @@
     edges[3 * c :, :] = acts[(rows + 1) * c :, :]
 
 
-def second_kernel(wanted, pos, x, mid, st, cols, w2t, zt, edges, w1t, after, *outs):
+def second_kernel(wanted, flags, x, mid, st, cols, w2t, zt, edges, w1t, after, *outs):
     block, residual, acts, control = outs
     rows, c, width = x.shape
     mean, scale = whole_stats(st[...], c, rows * width * (c // G))
     scale = scale * cols[c:, :1]
-    top, bottom = edge_flags(pos)
+    top, bottom = flags[0:1, :1], flags[1:2, :1]
 
     def put(at, slot):
         if at == 0:
@@ -207,9 +217,9 @@
         ).astype(BF16)
 
 
-def mix_kernel(wanted, pos, block, arrived, *rest):
+def mix_kernel(wanted, flags, block, arrived, *rest):
     whole, held, sem = rest[-3:]
-    unet = pos[2] == 1
+    unet = flags[2:3, :1] > 0.5
     copies = []
     for r, to in enumerate(wanted):
         add = jnp.where(unet, arrived[r].astype(F32), 0.0)
@@ -220,12 +230,12 @@
         copy.wait()
 
 
-def mix(pos, block, arrived, wanted, whole, old):
+def mix(flags, block, arrived, wanted, whole, old):
     held = [] if old is None else [old]
     return pl.pallas_call(
         functools.partial(mix_kernel, wanted),
         out_shape=whole,
-        in_specs=[SMEM, VMEM, VMEM] + [ANYWHERE] * len(held),
+        in_specs=[VMEM, VMEM, VMEM] + [ANYWHERE] * len(held),
         out_specs=ANYWHERE,
         scratch_shapes=[
             pltpu.VMEM(arrived.shape, BF16),
@@ -235,17 +245,17 @@
         compiler_params=pltpu.CompilerParams(vmem_limit_bytes=16 * 2**20),
         cost_estimate=pl.CostEstimate(flops=10**6, bytes_accessed=2**21, transcendentals=0),
         name="mix",
-    )(pos, block, arrived, *held)
+    )(flags, block, arrived, *held)
 
 
 def on_device(feats, conv_first, conv_second, time_shift, norm_gains, zero_conv):
     strips = lax.axis_size("strip")
-    here = lax.axis_index("strip")
-    pos = jnp.stack([here, strips, lax.axis_index("branch")]).astype(jnp.int32)
+    flags = strip_flags(strips)
     x = jnp.transpose(feats[0], (0, 2, 1))
     rows, c, width = x.shape
-    down = [(i, i + 1) for i in range(strips - 1)]
-    up = [(i + 1, i) for i in range(strips - 1)]
+    same_chip = [(i, i ^ 1) for i in range(strips)]
+    next_chip = [(i, i + 1) for i in range(1, strips - 1, 2)]
+    next_chip += [(target, source) for source, target in next_chip]
     shaped = jax.ShapeDtypeStruct
     stat = shaped((strips, LANES), F32)
     wide = shaped((3 * c, 3 * c), BF16)
@@ -255,16 +265,16 @@
     def spread(st):
         return lax.all_to_all(st, "strip", 0, 0)
 
-    st1, first_rows, last_rows = call(
-        stats_kernel, "stats_first", 1, (stat, halo, halo), [], 16, 2 * 10**10
-    )(pos, x)
-    low = lax.ppermute(last_rows, "strip", down)
-    high = lax.ppermute(first_rows, "strip", up)
+    st1, inner, outer = call(
+        stats_kernel, "stats_first", 2, (stat, halo, halo), [], 16, 2 * 10**10
+    )(flags, x)
+    outer = lax.ppermute(outer, "strip", next_chip)
+    inner = lax.ppermute(inner, "strip", same_chip)
     st1 = spread(st1)
     mid, st2, edges, w1t, w2t, zt, cols = call(
         first_kernel,
         "conv_first",
-        9,
+        10,
         (
             shaped((rows, c, width), F32),
             stat,
@@ -277,16 +287,16 @@
         [pltpu.VMEM(((rows + 4) * c, width), BF16)],
         36,
         rows * row_macs,
-    )(pos, x, low, high, st1, norm_gains[0], time_shift, conv_first[0], conv_second[0], zero_conv)
+    )(flags, x, inner, outer, st1, norm_gains[0], time_shift, conv_first[0], conv_second[0], zero_conv)
     st2 = spread(st2)
     pieces = []
     after = zt
-    for wanted in (((3, 6),), ((0, 3),), ((6, rows),)):
+    for wanted in (((3, 5),), ((1, 3),), ((5, 7),), ((0, 1), (7, rows))):
         n = sum(end - begin for begin, end in wanted)
         block, residual = call(
             functools.partial(second_kernel, wanted),
             "conv_second",
-            8,
+            9,
             (shaped((n, c, width), F32), shaped((n, c, width), BF16)),
             [
                 pltpu.VMEM(((n + 2 * len(wanted)) * c, width), BF16),
@@ -295,14 +305,14 @@
             32,
             n * row_macs,
             unread=1,
-        )(pos, x, mid, st2, cols, w2t, zt, edges, w1t, after)
+        )(flags, x, mid, st2, cols, w2t, zt, edges, w1t, after)
         after = residual
         listed = [r for begin, end in wanted for r in range(begin, end)]
         pieces.append((listed, block, lax.ppermute(residual, "branch", [(0, 1)])))
     whole = shaped((rows, c, width), BF16)
     out = None
     for listed, block, arrived in pieces:
-        out = mix(pos, block, arrived, listed, whole, out)
+        out = mix(flags, block, arrived, listed, whole, out)
     return jnp.transpose(out, (0, 2, 1))[None]
 
 

time: 95.7 us -> 89.5 us (0.935)
  Pallas kernels: 22.9 us -> 20.7 us
  waiting for transfers between devices: 19.9 us -> 18.1 us
  blocking collectives: 43.8 us -> 42.6 us
  starting transfers between devices: 7.06 us -> 6.07 us
    ppermute x2, starting transfers between devices: 3.18 us -> 0.91 us  [the longest x1 0.81 us: on_device(): outer = lax.ppermute(outer, 'strip', next_chip)]
    ppermute x3 -> x4, waiting for transfers between devices: 19.9 us -> 18.1 us  [on_device(): pieces.append((listed, block, lax.ppermute(residual, 'branch', [(0, 1)])))]
    pallas_call x5 -> x6, Pallas kernels: 18.8 us -> 17.4 us  [the longest x4 10.1 us: on_device(): call(functools.partial(second_kernel, wanted), 'conv_second', 9, (shaped(...]
    ppermute x3 -> x4, starting transfers between devices: 3.88 us -> 5.17 us  [on_device(): pieces.append((listed, block, lax.ppermute(residual, 'branch', [(0, 1)])))]
    all_to_all x2, blocking collectives: 43.8 us -> 42.6 us  [spread(): return lax.all_to_all(st, 'strip', 0, 0)]
    pallas_call x3 -> x4, Pallas kernels: 4.08 us -> 3.36 us  [mix(): pl.pallas_call(functools.partial(mix_kernel, wanted), out_shape=whole, in...]
  transfers between devices with their start and end apart: 5 -> 6, of which waited for: 3 -> 4; matrix products, arithmetic and copies ran while one was open for 0% -> 0% of each run, Pallas kernels for 11% -> 12%
where the time goes in v3:
time: 89.5 us; the launch traced here: 89.2 us
  blocking collectives  42.6 us (48%)
  Pallas kernels  20.7 us (23%)
  waiting for transfers between devices  18.1 us (20%)
  starting transfers between devices  6.07 us (7%)
  local copies, waits for them, and re-layouts  1.42 us (2%)
    all_to_all x2, blocking collectives, spread(): return lax.all_to_all(st, 'strip', 0, 0)  42.6 us
    ppermute x4, waiting for transfers between devices, on_device(): pieces.append((listed, block, lax.ppermute(residual, 'branch', [(0, 1)])))  18.1 us
    pallas_call x4, Pallas kernels, on_device(): call(functools.partial(second_kernel, wanted), 'conv_second', 9, (shaped(...  10.1 us
    pallas_call x1, Pallas kernels, on_device(): call(first_kernel, 'conv_first', 10, (shaped((rows, c, width), F32), stat...  6.38 us
    ppermute x4, starting transfers between devices, on_device(): pieces.append((listed, block, lax.ppermute(residual, 'branch', [(0, 1)])))  5.17 us
    pallas_call x4, Pallas kernels, mix(): pl.pallas_call(functools.partial(mix_kernel, wanted), out_shape=whole, in...  3.36 us
  transfers between devices with their start and end apart: 6, of which 4 were waited for; matrix products, arithmetic and copies ran while one was open for 0% of the time, Pallas kernels for 12%

profile of v3, /device:TPU:16, one launch (start us, length us, event | category | flops | bytes accessed | tf_op | source)
XLA Modules:
  0.0 89.2 jit_solution(12394878576874859132)
XLA Ops:
  0.0 0.1 iota.16.flags
  0.1 1.3 %copy-done = bf16[1,8,256,320]{2,3,1,0:T(8,128)(2,1)S(1)} copy-done((bf16[1,8,256,320]{2,3,1,0:T(8,128)(2,1)S(1)}, bf16[1,8,256,320]{2,3,1,0:T(8,128)(2,1)}, u32[]{:S(2)}) %copy-start) | copy-done | bytes 1310744
  1.4 0.9 %stats_first.1 = (f32[128,128]{1,0:T(8,128)S(1)}, bf16[2,320,256]{2,1,0:T(8,128)(2,1)S(1)}, bf16[2,320,256]{2,1,0:T(8,128)(2,1)S(1)}) custom-call(f32[8,128]{1,0:T(8,128)S(1)} %iota.16.flags, bf16[8,320,256]{2,1,0:T(8,128)(2,1)S(1)} %bitcast.17), custom_call_target="tpu_custom_call" | custom-call | flops 20000000000 | bytes 4194304 | tf_op jit(solution)/shard_map/stats_first/pallas_call | solution.py:268
  2.4 0.1 collective-permute-start
  2.5 0.8 collective-permute-start.1
  3.3 26.4 %all_to_all.22 = f32[128,1,128]{2,1,0:T(1,128)S(1)} all-to-all(f32[128,1,128]{2,1,0:T(1,128)S(1)} %bitcast.28), channel_id=1, replica_groups=mesh['branch'=2,'strip'=128] {'strip'}, dimensions={0} | all-to-all | bytes 131072 | tf_op jit(solution)/shard_map/all_to_all | solution.py:266
  29.8 6.4 %conv_first.1 = (f32[8,320,256]{2,1,0:T(8,128)S(1)}, f32[128,128]{1,0:T(8,128)S(1)}, bf16[1920,256]{1,0:T(8,128)(2,1)S(1)}, bf16[960,960]{1,0:T(8,128)(2,1)S(1)}...) custom-call(f32[8,128]{1,0:T(8,128)S(1)} %iota.16.flags, ...), custom_call_target="tpu_custom_call" | custom-call | flops 3774873600 | bytes 4194304 | tf_op jit(solution)/shard_map/conv_first/pallas_call | solution.py:274
  36.2 16.1 %all_to_all.23 = f32[128,1,128]{2,1,0:T(1,128)S(1)} all-to-all(f32[128,1,128]{2,1,0:T(1,128)S(1)} %bitcast.29), channel_id=1, replica_groups=mesh['branch'=2,'strip'=128] {'strip'}, dimensions={0} | all-to-all | bytes 131072 | tf_op jit(solution)/shard_map/all_to_all | solution.py:266
  52.3 2.0 %conv_second.4 = (f32[2,320,256]{2,1,0:T(8,128)S(1)}, bf16[2,320,256]{2,1,0:T(8,128)(2,1)S(1)}) custom-call(f32[8,128]{1,0:T(8,128)S(1)} %iota.16.flags, bf16[8,320,256]{2,1,0:T(8,128)(2,1)S(1)} %bitcast.19, f32[8,320,256]{2,1,0:T(8,128)S(1)} %get-tuple-element.26.mid, f32[128,128]{1,0:T(8,128)S(1)} %bitcast.23, f32[640,128]{1,0:T(8,128)S(1)} %get-tuple-element.28.cols, ...), custom_call_target="tpu_custom_call" | custom-call | flops 943718400 | bytes 4194304 | tf_op jit(solution)/shard_map/conv_second/pallas_call | solution.py:296
  54.3 1.3 %collective-permute-start.5 = (bf16[2,320,256]{2,1,0:T(8,128)(2,1)S(1)}, bf16[2,320,256]{2,1,0:T(8,128)(2,1)S(1)}, u32[]{:S(2)}, u32[]{:S(2)}) collective-permute-start(bf16[2,320,256]{2,1,0:T(8,128)(2,1)S(1)} %get-tuple-element.33.after), channel_id=1, source_target_pairs={{0,128},{1,129},{2,130},{3,131},{4,132},{5,133},{6,134},{7,135},{8... | collective-permute-start | bytes 983048 | tf_op jit(solution)/shard_map/ppermute | solution.py:311
  55.6 2.0 %conv_second.5 = (f32[2,320,256]{2,1,0:T(8,128)S(1)}, bf16[2,320,256]{2,1,0:T(8,128)(2,1)S(1)}) custom-call(f32[8,128]{1,0:T(8,128)S(1)} %iota.16.flags, bf16[8,320,256]{2,1,0:T(8,128)(2,1)S(1)} %bitcast.20, f32[8,320,256]{2,1,0:T(8,128)S(1)} %get-tuple-element.26.mid, f32[128,128]{1,0:T(8,128)S(1)} %bitcast.24, f32[640,128]{1,0:T(8,128)S(1)} %get-tuple-element.28.cols, ...), custom_call_target="tpu_custom_call" | custom-call | flops 943718400 | bytes 4194304 | tf_op jit(solution)/shard_map/conv_second/pallas_call | solution.py:296
  57.6 1.3 %collective-permute-start.4 = (bf16[2,320,256]{2,1,0:T(8,128)(2,1)S(1)}, bf16[2,320,256]{2,1,0:T(8,128)(2,1)S(1)}, u32[]{:S(2)}, u32[]{:S(2)}) collective-permute-start(bf16[2,320,256]{2,1,0:T(8,128)(2,1)S(1)} %get-tuple-element.34.after), channel_id=1, source_target_pairs={{0,128},{1,129},{2,130},{3,131},{4,132},{5,133},{6,134},{7,135},{8... | collective-permute-start | bytes 983048 | tf_op jit(solution)/shard_map/ppermute | solution.py:311
  58.9 2.0 %conv_second.6 = (f32[2,320,256]{2,1,0:T(8,128)S(1)}, bf16[2,320,256]{2,1,0:T(8,128)(2,1)S(1)}) custom-call(f32[8,128]{1,0:T(8,128)S(1)} %iota.16.flags, bf16[8,320,256]{2,1,0:T(8,128)(2,1)S(1)} %bitcast.21, f32[8,320,256]{2,1,0:T(8,128)S(1)} %get-tuple-element.26.mid, f32[128,128]{1,0:T(8,128)S(1)} %bitcast.25, f32[640,128]{1,0:T(8,128)S(1)} %get-tuple-element.28.cols, ...), custom_call_target="tpu_custom_call" | custom-call | flops 943718400 | bytes 4194304 | tf_op jit(solution)/shard_map/conv_second/pallas_call | solution.py:296
  61.0 1.3 %collective-permute-start.3 = (bf16[2,320,256]{2,1,0:T(8,128)(2,1)S(1)}, bf16[2,320,256]{2,1,0:T(8,128)(2,1)S(1)}, u32[]{:S(2)}, u32[]{:S(2)}) collective-permute-start(bf16[2,320,256]{2,1,0:T(8,128)(2,1)S(1)} %get-tuple-element.35.after), channel_id=1, source_target_pairs={{0,128},{1,129},{2,130},{3,131},{4,132},{5,133},{6,134},{7,135},{8... | collective-permute-start | bytes 983048 | tf_op jit(solution)/shard_map/ppermute | solution.py:311
  62.3 4.0 %conv_second.7 = (f32[2,320,256]{2,1,0:T(8,128)S(1)}, bf16[2,320,256]{2,1,0:T(8,128)(2,1)S(1)}) custom-call(f32[8,128]{1,0:T(8,128)S(1)} %iota.16.flags, bf16[8,320,256]{2,1,0:T(8,128)(2,1)S(1)} %bitcast.22, f32[8,320,256]{2,1,0:T(8,128)S(1)} %get-tuple-element.26.mid, f32[128,128]{1,0:T(8,128)S(1)} %bitcast.26, f32[640,128]{1,0:T(8,128)S(1)} %get-tuple-element.28.cols, ...), custom_call_target="tpu_custom_call" | custom-call | flops 943718400 | bytes 4194304 | tf_op jit(solution)/shard_map/conv_second/pallas_call | solution.py:296
  66.3 1.3 %collective-permute-start.2 = (bf16[2,320,256]{2,1,0:T(8,128)(2,1)S(1)}, bf16[2,320,256]{2,1,0:T(8,128)(2,1)S(1)}, u32[]{:S(2)}, u32[]{:S(2)}) collective-permute-start(bf16[2,320,256]{2,1,0:T(8,128)(2,1)S(1)} %get-tuple-element.37), channel_id=1, source_target_pairs={{0,128},{1,129},{2,130},{3,131},{4,132},{5,133},{6,134},{7,135},{8... | collective-permute-start | bytes 983048 | tf_op jit(solution)/shard_map/ppermute | solution.py:311
  67.6 0.7 collective-permute-done.5.arrived
  68.3 0.8 mix.4.rest_0_
  69.2 6.2 %collective-permute-done.4.arrived = bf16[2,320,256]{2,1,0:T(8,128)(2,1)S(1)} collective-permute-done((bf16[2,320,256]{2,1,0:T(8,128)(2,1)S(1)}, bf16[2,320,256]{2,1,0:T(8,128)(2,1)S(1)}, u32[]{:S(2)}, u32[]{:S(2)}) %collective-permute-start.4) | collective-permute-done | bytes 327712 | tf_op jit(solution)/shard_map/ppermute | solution.py:311
  75.3 0.8 mix.5.rest_0_
  76.2 6.2 %collective-permute-done.3.arrived = bf16[2,320,256]{2,1,0:T(8,128)(2,1)S(1)} collective-permute-done((bf16[2,320,256]{2,1,0:T(8,128)(2,1)S(1)}, bf16[2,320,256]{2,1,0:T(8,128)(2,1)S(1)}, u32[]{:S(2)}, u32[]{:S(2)}) %collective-permute-start.3) | collective-permute-done | bytes 327712 | tf_op jit(solution)/shard_map/ppermute | solution.py:311
  82.4 0.8 mix.6.rest_0_
  83.2 5.0 %collective-permute-done.2.arrived = bf16[2,320,256]{2,1,0:T(8,128)(2,1)S(1)} collective-permute-done((bf16[2,320,256]{2,1,0:T(8,128)(2,1)S(1)}, bf16[2,320,256]{2,1,0:T(8,128)(2,1)S(1)}, u32[]{:S(2)}, u32[]{:S(2)}) %collective-permute-start.2) | collective-permute-done | bytes 327712 | tf_op jit(solution)/shard_map/ppermute | solution.py:311
  88.2 0.8 mix.7
  (16 shorter events, 0.0 us)
Async XLA Ops:
  0.1 1.3 %copy-start = (bf16[1,8,256,320]{2,3,1,0:T(8,128)(2,1)S(1)}, bf16[1,8,256,320]{2,3,1,0:T(8,128)(2,1)}, u32[]{:S(2)}) copy-start(bf16[1,8,256,320]{2,3,1,0:T(8,128)(2,1)} %param.6) | copy-start | bytes 3932164
  1.4 28.3 %copy-start.1 = (bf16[1,8,256,320]{2,3,1,0:T(8,128)(2,1)S(1)}, bf16[1,8,256,320]{2,3,1,0:T(8,128)(2,1)}, u32[]{:S(2)}) copy-start(bf16[1,8,256,320]{2,3,1,0:T(8,128)(2,1)} %param.6) | copy-start | bytes 3932164
  1.4 28.3 %copy-start.2 = (bf16[1,3,3,320,320]{4,3,2,1,0:T(8,128)(2,1)S(1)}, bf16[1,3,3,320,320]{4,3,2,1,0:T(8,128)(2,1)}, u32[]{:S(2)}) copy-start(bf16[1,3,3,320,320]{4,3,2,1,0:T(8,128)(2,1)} %param.7) | copy-start | bytes 5529604
  1.4 28.3 %copy-start.3 = (bf16[1,3,3,320,320]{4,3,2,1,0:T(8,128)(2,1)S(1)}, bf16[1,3,3,320,320]{4,3,2,1,0:T(8,128)(2,1)}, u32[]{:S(2)}) copy-start(bf16[1,3,3,320,320]{4,3,2,1,0:T(8,128)(2,1)} %param.8) | copy-start | bytes 5529604
  1.4 28.3 %copy-start.4 = (bf16[320,320]{1,0:T(8,128)(2,1)S(1)}, bf16[320,320]{1,0:T(8,128)(2,1)}, u32[]{:S(2)}) copy-start(bf16[320,320]{1,0:T(8,128)(2,1)} %z.1) | copy-start | bytes 614404
  1.4 28.3 %copy-start.5 = (f32[1,2,320]{2,1,0:T(2,128)S(1)}, f32[1,2,320]{2,1,0:T(2,128)}, u32[]{:S(2)}) copy-start(f32[1,2,320]{2,1,0:T(2,128)} %param.10) | copy-start | bytes 7684
  1.4 28.3 %copy-start.6 = (f32[1,320]{1,0:T(1,128)S(1)}, f32[1,320]{1,0:T(1,128)}, u32[]{:S(2)}) copy-start(f32[1,320]{1,0:T(1,128)} %shift.1) | copy-start | bytes 3844
  2.4 27.4 %collective-permute-start = (bf16[2,320,256]{2,1,0:T(8,128)(2,1)S(1)}, bf16[2,320,256]{2,1,0:T(8,128)(2,1)S(1)}, u32[]{:S(2)}, u32[]{:S(2)}) collective-permute-start(bf16[2,320,256]{2,1,0:T(8,128)(2,1)S(1)} %get-tuple-element.23), channel_id=1, source_target_pairs={{0,1},{1,0},{2,3},{3,2},{4,5},{5,4},{6,7},{7,6},{8,9},{9,8},{10,11... | collective-permute-start | bytes 983048 | tf_op jit(solution)/shard_map/ppermute | solution.py:272
  2.5 27.3 %collective-permute-start.1 = (bf16[2,320,256]{2,1,0:T(8,128)(2,1)S(1)}, bf16[2,320,256]{2,1,0:T(8,128)(2,1)S(1)}, u32[]{:S(2)}, u32[]{:S(2)}) collective-permute-start(bf16[2,320,256]{2,1,0:T(8,128)(2,1)S(1)} %get-tuple-element.24), channel_id=1, source_target_pairs={{1,2},{3,4},{5,6},{7,8},{9,10},{11,12},{13,14},{15,16},{17,18},{19... | collective-permute-start | bytes 983048 | tf_op jit(solution)/shard_map/ppermute | solution.py:271
  54.3 14.0 %collective-permute-start.5 = (bf16[2,320,256]{2,1,0:T(8,128)(2,1)S(1)}, bf16[2,320,256]{2,1,0:T(8,128)(2,1)S(1)}, u32[]{:S(2)}, u32[]{:S(2)}) collective-permute-start(bf16[2,320,256]{2,1,0:T(8,128)(2,1)S(1)} %get-tuple-element.33.after), channel_id=1, source_target_pairs={{0,128},{1,129},{2,130},{3,131},{4,132},{5,133},{6,134},{7,135},{8... | collective-permute-start | bytes 983048 | tf_op jit(solution)/shard_map/ppermute | solution.py:311
  57.6 17.7 %collective-permute-start.4 = (bf16[2,320,256]{2,1,0:T(8,128)(2,1)S(1)}, bf16[2,320,256]{2,1,0:T(8,128)(2,1)S(1)}, u32[]{:S(2)}, u32[]{:S(2)}) collective-permute-start(bf16[2,320,256]{2,1,0:T(8,128)(2,1)S(1)} %get-tuple-element.34.after), channel_id=1, source_target_pairs={{0,128},{1,129},{2,130},{3,131},{4,132},{5,133},{6,134},{7,135},{8... | collective-permute-start | bytes 983048 | tf_op jit(solution)/shard_map/ppermute | solution.py:311
  61.0 21.4 %collective-permute-start.3 = (bf16[2,320,256]{2,1,0:T(8,128)(2,1)S(1)}, bf16[2,320,256]{2,1,0:T(8,128)(2,1)S(1)}, u32[]{:S(2)}, u32[]{:S(2)}) collective-permute-start(bf16[2,320,256]{2,1,0:T(8,128)(2,1)S(1)} %get-tuple-element.35.after), channel_id=1, source_target_pairs={{0,128},{1,129},{2,130},{3,131},{4,132},{5,133},{6,134},{7,135},{8... | collective-permute-start | bytes 983048 | tf_op jit(solution)/shard_map/ppermute | solution.py:311
  66.3 22.0 %collective-permute-start.2 = (bf16[2,320,256]{2,1,0:T(8,128)(2,1)S(1)}, bf16[2,320,256]{2,1,0:T(8,128)(2,1)S(1)}, u32[]{:S(2)}, u32[]{:S(2)}) collective-permute-start(bf16[2,320,256]{2,1,0:T(8,128)(2,1)S(1)} %get-tuple-element.37), channel_id=1, source_target_pairs={{0,128},{1,129},{2,130},{3,131},{4,132},{5,133},{6,134},{7,135},{8... | collective-permute-start | bytes 983048 | tf_op jit(solution)/shard_map/ppermute | solution.py:311

commit v4 on v3

--- a/solution.py
+++ b/solution.py
@@ -80,10 +80,9 @@
     return half + half * jnp.tanh(half)
 
 
-def turned(w, out):
+def turned(w, out, kx):
     c = w.shape[2]
-    for kx in range(3):
-        out[kx * c : (kx + 1) * c, :] = jnp.concatenate([w[ky, kx].T for ky in range(3)], axis=1)
+    out[kx * c : (kx + 1) * c, :] = jnp.concatenate([w[ky, kx].T for ky in range(3)], axis=1)
 
 
 def conv_row(wt, rows):
@@ -136,17 +135,37 @@
         a = silu((v - mean) * scale)
         if keep is not None:
             a = a * keep
-        acts[at * c : (at + 1) * c, :] = a.astype(BF16)
-
+        a = a.astype(BF16)
+        acts[at * c : (at + 1) * c, :] = a
+        if at < 3:
+            edges[at * c : (at + 1) * c, :] = a
+        if at > rows:
+            edges[(at - rows + 2) * c : (at - rows + 3) * c, :] = a
+
+    for kx in range(3):
+        turned(w1, w1t, kx)
     for at in (1, 2, 3):
         put(at)
-    turned(w1, w1t)
     shift_c = column(shift[...])
-    cols[...] = jnp.broadcast_to(
-        jnp.concatenate([shift_c, column(gains[1:2, :])], axis=0), cols.shape
-    )
     first, second = group_masks(c)
     per_row = width * (c // G)
+
+    def turn_z():
+        zt[...] = z[...].T
+
+    def keep_columns():
+        both = jnp.concatenate([shift_c, column(gains[1:2, :])], axis=0)
+        cols[...] = jnp.broadcast_to(both, cols.shape)
+
+    beside = {
+        1: keep_columns,
+        2: lambda: turned(w2, w2t, 0),
+        3: lambda: turned(w2, w2t, 1),
+        4: lambda: turned(w2, w2t, 2),
+        5: turn_z,
+        6: lambda: put(0),
+        7: lambda: put(rows + 3),
+    }
     for r in range(1, rows + 1):
         y = conv_row(w1t[...], acts[r * c : (r + 3) * c, :]) + shift_c
         mid[r - 1] = y
@@ -161,20 +180,16 @@
             squares = squares + fold((y - about_c) * (y - about_c))
         if r < rows:
             put(r + 3)
+        if r in beside:
+            beside[r]()
     count = rows * per_row
     total = jnp.sum(total, axis=1, keepdims=True)
     squares = jnp.sum(squares, axis=1, keepdims=True)
     own_mean = jnp.sum(first * total, axis=0, keepdims=True) / count
-    off = jnp.sum(first * (own_mean - about), axis=1, keepdims=True)
-    squares = squares - off * off * (rows * width)
-    st2 = own_mean + jnp.sum(second * squares, axis=0, keepdims=True)
+    moved = (own_mean - about) * (own_mean - about) * count
+    moved = pltpu.roll(jnp.broadcast_to(moved, (8, LANES)), G, 1)[:1]
+    st2 = own_mean + jnp.sum(second * squares, axis=0, keepdims=True) - moved
     out[...] = jnp.broadcast_to(st2, out.shape)
-    put(0)
-    put(rows + 3)
-    turned(w2, w2t)
-    zt[...] = z[...].T
-    edges[: 3 * c, :] = acts[: 3 * c, :]
-    edges[3 * c :, :] = acts[(rows + 1) * c :, :]
 
 
 def second_kernel(wanted, flags, x, mid, st, cols, w2t, zt, edges, w1t, after, *outs):
@@ -308,7 +323,7 @@
         )(flags, x, mid, st2, cols, w2t, zt, edges, w1t, after)
         after = residual
         listed = [r for begin, end in wanted for r in range(begin, end)]
-        pieces.append((listed, block, lax.ppermute(residual, "branch", [(0, 1)])))
+        pieces.append((listed, block, lax.ppermute(residual, "branch", [(0, 1), (1, 0)])))
     whole = shaped((rows, c, width), BF16)
     out = None
     for listed, block, arrived in pieces:

time: 89.5 us -> 87.8 us (0.981)
  waiting for transfers between devices: 18.1 us -> 14.1 us
  starting transfers between devices: 6.07 us -> 8.31 us
    ppermute x4, waiting for transfers between devices: 18.1 us -> 14.1 us  [on_device(): lax.ppermute(residual, 'branch', [(0, 1), (1, 0)])]
    ppermute x4, starting transfers between devices: 5.17 us -> 7.4 us  [on_device(): lax.ppermute(residual, 'branch', [(0, 1), (1, 0)])]
  transfers between devices with their start and end apart: 6 -> 6, of which waited for: 4 -> 3; matrix products, arithmetic and copies ran while one was open for 0% -> 0% of each run, Pallas kernels for 12% -> 12%
where the time goes in v4:
time: 87.8 us; the launch traced here: 87.3 us
  blocking collectives  42.6 us (49%)
  Pallas kernels  20.6 us (23%)
  waiting for transfers between devices  14.1 us (16%)
  starting transfers between devices  8.31 us (9%)
  local copies, waits for them, and re-layouts  1.42 us (2%)
    all_to_all x2, blocking collectives, spread(): return lax.all_to_all(st, 'strip', 0, 0)  42.6 us
    ppermute x4, waiting for transfers between devices, on_device(): lax.ppermute(residual, 'branch', [(0, 1), (1, 0)])  14.1 us
    pallas_call x4, Pallas kernels, on_device(): call(functools.partial(second_kernel, wanted), 'conv_second', 9, (shaped(...  10.1 us
    ppermute x4, starting transfers between devices, on_device(): lax.ppermute(residual, 'branch', [(0, 1), (1, 0)])  7.4 us
    pallas_call x1, Pallas kernels, on_device(): call(first_kernel, 'conv_first', 10, (shaped((rows, c, width), F32), stat...  6.27 us
    pallas_call x4, Pallas kernels, mix(): pl.pallas_call(functools.partial(mix_kernel, wanted), out_shape=whole, in...  3.36 us
  transfers between devices with their start and end apart: 6, of which 3 were waited for; matrix products, arithmetic and copies ran while one was open for 0% of the time, Pallas kernels for 12%

profile of v4, /device:TPU:16, one launch (start us, length us, event | category | flops | bytes accessed | tf_op | source)
XLA Modules:
  0.0 87.3 jit_solution(10550383289147526244)
XLA Ops:
  0.0 0.1 iota.16.flags
  0.1 1.3 %copy-done = bf16[1,8,256,320]{2,3,1,0:T(8,128)(2,1)S(1)} copy-done((bf16[1,8,256,320]{2,3,1,0:T(8,128)(2,1)S(1)}, bf16[1,8,256,320]{2,3,1,0:T(8,128)(2,1)}, u32[]{:S(2)}) %copy-start) | copy-done | bytes 1310744
  1.4 0.0 copy-start.5
  1.4 0.9 %stats_first.1 = (f32[128,128]{1,0:T(8,128)S(1)}, bf16[2,320,256]{2,1,0:T(8,128)(2,1)S(1)}, bf16[2,320,256]{2,1,0:T(8,128)(2,1)S(1)}) custom-call(f32[8,128]{1,0:T(8,128)S(1)} %iota.16.flags, bf16[8,320,256]{2,1,0:T(8,128)(2,1)S(1)} %bitcast.17), custom_call_target="tpu_custom_call" | custom-call | flops 20000000000 | bytes 4194304 | tf_op jit(solution)/shard_map/stats_first/pallas_call | solution.py:283
  2.4 0.1 collective-permute-start
  2.5 0.8 collective-permute-start.1
  3.3 26.4 %all_to_all.22 = f32[128,1,128]{2,1,0:T(1,128)S(1)} all-to-all(f32[128,1,128]{2,1,0:T(1,128)S(1)} %bitcast.28), channel_id=1, replica_groups=mesh['branch'=2,'strip'=128] {'strip'}, dimensions={0} | all-to-all | bytes 131072 | tf_op jit(solution)/shard_map/all_to_all | solution.py:281
  29.8 6.3 %conv_first.1 = (f32[8,320,256]{2,1,0:T(8,128)S(1)}, f32[128,128]{1,0:T(8,128)S(1)}, bf16[1920,256]{1,0:T(8,128)(2,1)S(1)}, bf16[960,960]{1,0:T(8,128)(2,1)S(1)}...) custom-call(f32[8,128]{1,0:T(8,128)S(1)} %iota.16.flags, ...), custom_call_target="tpu_custom_call" | custom-call | flops 3774873600 | bytes 4194304 | tf_op jit(solution)/shard_map/conv_first/pallas_call | solution.py:289
  36.0 16.1 %all_to_all.23 = f32[128,1,128]{2,1,0:T(1,128)S(1)} all-to-all(f32[128,1,128]{2,1,0:T(1,128)S(1)} %bitcast.29), channel_id=1, replica_groups=mesh['branch'=2,'strip'=128] {'strip'}, dimensions={0} | all-to-all | bytes 131072 | tf_op jit(solution)/shard_map/all_to_all | solution.py:281
  52.2 2.0 %conv_second.4 = (f32[2,320,256]{2,1,0:T(8,128)S(1)}, bf16[2,320,256]{2,1,0:T(8,128)(2,1)S(1)}) custom-call(f32[8,128]{1,0:T(8,128)S(1)} %iota.16.flags, bf16[8,320,256]{2,1,0:T(8,128)(2,1)S(1)} %bitcast.19, f32[8,320,256]{2,1,0:T(8,128)S(1)} %get-tuple-element.26.mid, f32[128,128]{1,0:T(8,128)S(1)} %bitcast.23, f32[640,128]{1,0:T(8,128)S(1)} %get-tuple-element.28.cols, ...), custom_call_target="tpu_custom_call" | custom-call | flops 943718400 | bytes 4194304 | tf_op jit(solution)/shard_map/conv_second/pallas_call | solution.py:311
  54.2 0.7 collective-permute-start.5
  54.9 2.0 %conv_second.5 = (f32[2,320,256]{2,1,0:T(8,128)S(1)}, bf16[2,320,256]{2,1,0:T(8,128)(2,1)S(1)}) custom-call(f32[8,128]{1,0:T(8,128)S(1)} %iota.16.flags, bf16[8,320,256]{2,1,0:T(8,128)(2,1)S(1)} %bitcast.20, f32[8,320,256]{2,1,0:T(8,128)S(1)} %get-tuple-element.26.mid, f32[128,128]{1,0:T(8,128)S(1)} %bitcast.24, f32[640,128]{1,0:T(8,128)S(1)} %get-tuple-element.28.cols, ...), custom_call_target="tpu_custom_call" | custom-call | flops 943718400 | bytes 4194304 | tf_op jit(solution)/shard_map/conv_second/pallas_call | solution.py:311
  56.9 3.0 %collective-permute-start.4 = (bf16[2,320,256]{2,1,0:T(8,128)(2,1)S(1)}, bf16[2,320,256]{2,1,0:T(8,128)(2,1)S(1)}, u32[]{:S(2)}, u32[]{:S(2)}) collective-permute-start(bf16[2,320,256]{2,1,0:T(8,128)(2,1)S(1)} %get-tuple-element.34.after), channel_id=1, source_target_pairs={{0,128},{128,0},{1,129},{129,1},{2,130},{130,2},{3,131},{131,3},{4... | collective-permute-start | bytes 983048 | tf_op jit(solution)/shard_map/ppermute | solution.py:326
  59.9 2.0 %conv_second.6 = (f32[2,320,256]{2,1,0:T(8,128)S(1)}, bf16[2,320,256]{2,1,0:T(8,128)(2,1)S(1)}) custom-call(f32[8,128]{1,0:T(8,128)S(1)} %iota.16.flags, bf16[8,320,256]{2,1,0:T(8,128)(2,1)S(1)} %bitcast.21, f32[8,320,256]{2,1,0:T(8,128)S(1)} %get-tuple-element.26.mid, f32[128,128]{1,0:T(8,128)S(1)} %bitcast.25, f32[640,128]{1,0:T(8,128)S(1)} %get-tuple-element.28.cols, ...), custom_call_target="tpu_custom_call" | custom-call | flops 943718400 | bytes 4194304 | tf_op jit(solution)/shard_map/conv_second/pallas_call | solution.py:311
  62.0 0.7 collective-permute-start.3
  62.7 4.0 %conv_second.7 = (f32[2,320,256]{2,1,0:T(8,128)S(1)}, bf16[2,320,256]{2,1,0:T(8,128)(2,1)S(1)}) custom-call(f32[8,128]{1,0:T(8,128)S(1)} %iota.16.flags, bf16[8,320,256]{2,1,0:T(8,128)(2,1)S(1)} %bitcast.22, f32[8,320,256]{2,1,0:T(8,128)S(1)} %get-tuple-element.26.mid, f32[128,128]{1,0:T(8,128)S(1)} %bitcast.26, f32[640,128]{1,0:T(8,128)S(1)} %get-tuple-element.28.cols, ...), custom_call_target="tpu_custom_call" | custom-call | flops 943718400 | bytes 4194304 | tf_op jit(solution)/shard_map/conv_second/pallas_call | solution.py:311
  66.7 3.0 %collective-permute-start.2 = (bf16[2,320,256]{2,1,0:T(8,128)(2,1)S(1)}, bf16[2,320,256]{2,1,0:T(8,128)(2,1)S(1)}, u32[]{:S(2)}, u32[]{:S(2)}) collective-permute-start(bf16[2,320,256]{2,1,0:T(8,128)(2,1)S(1)} %get-tuple-element.37), channel_id=1, source_target_pairs={{0,128},{128,0},{1,129},{129,1},{2,130},{130,2},{3,131},{131,3},{4... | collective-permute-start | bytes 983048 | tf_op jit(solution)/shard_map/ppermute | solution.py:326
  69.7 0.8 mix.4.rest_0_
  70.5 2.9 %collective-permute-done.4.arrived = bf16[2,320,256]{2,1,0:T(8,128)(2,1)S(1)} collective-permute-done((bf16[2,320,256]{2,1,0:T(8,128)(2,1)S(1)}, bf16[2,320,256]{2,1,0:T(8,128)(2,1)S(1)}, u32[]{:S(2)}, u32[]{:S(2)}) %collective-permute-start.4) | collective-permute-done | bytes 327712 | tf_op jit(solution)/shard_map/ppermute | solution.py:326
  73.4 0.8 mix.5.rest_0_
  74.3 6.2 %collective-permute-done.3.arrived = bf16[2,320,256]{2,1,0:T(8,128)(2,1)S(1)} collective-permute-done((bf16[2,320,256]{2,1,0:T(8,128)(2,1)S(1)}, bf16[2,320,256]{2,1,0:T(8,128)(2,1)S(1)}, u32[]{:S(2)}, u32[]{:S(2)}) %collective-permute-start.3) | collective-permute-done | bytes 327712 | tf_op jit(solution)/shard_map/ppermute | solution.py:326
  80.4 0.8 mix.6.rest_0_
  81.3 5.0 %collective-permute-done.2.arrived = bf16[2,320,256]{2,1,0:T(8,128)(2,1)S(1)} collective-permute-done((bf16[2,320,256]{2,1,0:T(8,128)(2,1)S(1)}, bf16[2,320,256]{2,1,0:T(8,128)(2,1)S(1)}, u32[]{:S(2)}, u32[]{:S(2)}) %collective-permute-start.2) | collective-permute-done | bytes 327712 | tf_op jit(solution)/shard_map/ppermute | solution.py:326
  86.3 0.8 mix.7
  (16 shorter events, 0.0 us)
Async XLA Ops:
  0.1 1.3 %copy-start = (bf16[1,8,256,320]{2,3,1,0:T(8,128)(2,1)S(1)}, bf16[1,8,256,320]{2,3,1,0:T(8,128)(2,1)}, u32[]{:S(2)}) copy-start(bf16[1,8,256,320]{2,3,1,0:T(8,128)(2,1)} %param.6) | copy-start | bytes 3932164
  1.4 28.3 %copy-start.1 = (bf16[1,8,256,320]{2,3,1,0:T(8,128)(2,1)S(1)}, bf16[1,8,256,320]{2,3,1,0:T(8,128)(2,1)}, u32[]{:S(2)}) copy-start(bf16[1,8,256,320]{2,3,1,0:T(8,128)(2,1)} %param.6) | copy-start | bytes 3932164
  1.4 28.3 %copy-start.2 = (bf16[1,3,3,320,320]{4,3,2,1,0:T(8,128)(2,1)S(1)}, bf16[1,3,3,320,320]{4,3,2,1,0:T(8,128)(2,1)}, u32[]{:S(2)}) copy-start(bf16[1,3,3,320,320]{4,3,2,1,0:T(8,128)(2,1)} %param.7) | copy-start | bytes 5529604
  1.4 28.3 %copy-start.3 = (bf16[1,3,3,320,320]{4,3,2,1,0:T(8,128)(2,1)S(1)}, bf16[1,3,3,320,320]{4,3,2,1,0:T(8,128)(2,1)}, u32[]{:S(2)}) copy-start(bf16[1,3,3,320,320]{4,3,2,1,0:T(8,128)(2,1)} %param.8) | copy-start | bytes 5529604
  1.4 28.3 %copy-start.4 = (bf16[320,320]{1,0:T(8,128)(2,1)S(1)}, bf16[320,320]{1,0:T(8,128)(2,1)}, u32[]{:S(2)}) copy-start(bf16[320,320]{1,0:T(8,128)(2,1)} %z.1) | copy-start | bytes 614404
  1.4 28.3 %copy-start.5 = (f32[1,2,320]{2,1,0:T(2,128)S(1)}, f32[1,2,320]{2,1,0:T(2,128)}, u32[]{:S(2)}) copy-start(f32[1,2,320]{2,1,0:T(2,128)} %param.10) | copy-start | bytes 7684
  1.4 28.3 %copy-start.6 = (f32[1,320]{1,0:T(1,128)S(1)}, f32[1,320]{1,0:T(1,128)}, u32[]{:S(2)}) copy-start(f32[1,320]{1,0:T(1,128)} %shift.1) | copy-start | bytes 3844
  2.4 27.4 %collective-permute-start = (bf16[2,320,256]{2,1,0:T(8,128)(2,1)S(1)}, bf16[2,320,256]{2,1,0:T(8,128)(2,1)S(1)}, u32[]{:S(2)}, u32[]{:S(2)}) collective-permute-start(bf16[2,320,256]{2,1,0:T(8,128)(2,1)S(1)} %get-tuple-element.23), channel_id=1, source_target_pairs={{0,1},{1,0},{2,3},{3,2},{4,5},{5,4},{6,7},{7,6},{8,9},{9,8},{10,11... | collective-permute-start | bytes 983048 | tf_op jit(solution)/shard_map/ppermute | solution.py:287
  2.5 27.3 %collective-permute-start.1 = (bf16[2,320,256]{2,1,0:T(8,128)(2,1)S(1)}, bf16[2,320,256]{2,1,0:T(8,128)(2,1)S(1)}, u32[]{:S(2)}, u32[]{:S(2)}) collective-permute-start(bf16[2,320,256]{2,1,0:T(8,128)(2,1)S(1)} %get-tuple-element.24), channel_id=1, source_target_pairs={{1,2},{3,4},{5,6},{7,8},{9,10},{11,12},{13,14},{15,16},{17,18},{19... | collective-permute-start | bytes 983048 | tf_op jit(solution)/shard_map/ppermute | solution.py:286
  54.2 15.5 %collective-permute-start.5 = (bf16[2,320,256]{2,1,0:T(8,128)(2,1)S(1)}, bf16[2,320,256]{2,1,0:T(8,128)(2,1)S(1)}, u32[]{:S(2)}, u32[]{:S(2)}) collective-permute-start(bf16[2,320,256]{2,1,0:T(8,128)(2,1)S(1)} %get-tuple-element.33.after), channel_id=1, source_target_pairs={{0,128},{128,0},{1,129},{129,1},{2,130},{130,2},{3,131},{131,3},{4... | collective-permute-start | bytes 983048 | tf_op jit(solution)/shard_map/ppermute | solution.py:326
  56.9 16.5 %collective-permute-start.4 = (bf16[2,320,256]{2,1,0:T(8,128)(2,1)S(1)}, bf16[2,320,256]{2,1,0:T(8,128)(2,1)S(1)}, u32[]{:S(2)}, u32[]{:S(2)}) collective-permute-start(bf16[2,320,256]{2,1,0:T(8,128)(2,1)S(1)} %get-tuple-element.34.after), channel_id=1, source_target_pairs={{0,128},{128,0},{1,129},{129,1},{2,130},{130,2},{3,131},{131,3},{4... | collective-permute-start | bytes 983048 | tf_op jit(solution)/shard_map/ppermute | solution.py:326
  62.0 18.5 %collective-permute-start.3 = (bf16[2,320,256]{2,1,0:T(8,128)(2,1)S(1)}, bf16[2,320,256]{2,1,0:T(8,128)(2,1)S(1)}, u32[]{:S(2)}, u32[]{:S(2)}) collective-permute-start(bf16[2,320,256]{2,1,0:T(8,128)(2,1)S(1)} %get-tuple-element.35.after), channel_id=1, source_target_pairs={{0,128},{128,0},{1,129},{129,1},{2,130},{130,2},{3,131},{131,3},{4... | collective-permute-start | bytes 983048 | tf_op jit(solution)/shard_map/ppermute | solution.py:326
  66.7 19.7 %collective-permute-start.2 = (bf16[2,320,256]{2,1,0:T(8,128)(2,1)S(1)}, bf16[2,320,256]{2,1,0:T(8,128)(2,1)S(1)}, u32[]{:S(2)}, u32[]{:S(2)}) collective-permute-start(bf16[2,320,256]{2,1,0:T(8,128)(2,1)S(1)} %get-tuple-element.37), channel_id=1, source_target_pairs={{0,128},{128,0},{1,129},{129,1},{2,130},{130,2},{3,131},{131,3},{4... | collective-permute-start | bytes 983048 | tf_op jit(solution)/shard_map/ppermute | solution.py:326

commit v5 on v4

--- a/solution.py
+++ b/solution.py
@@ -75,8 +75,7 @@
     return mean_c, lax.rsqrt(variance + 1e-5)
 
 
-def silu(v):
-    half = 0.5 * v
+def silu_of_twice(half):
     return half + half * jnp.tanh(half)
 
 
@@ -119,7 +118,7 @@
 ):
     rows, c, width = x.shape
     mean, scale = whole_stats(st[...], c, rows * width * (c // G))
-    scale = scale * column(gains[0:1, :])
+    scale = 0.5 * scale * column(gains[0:1, :])
     top, bottom = flags[0:1, :1], flags[1:2, :1]
     even = flags[3:4, :1] > 0.5
 
@@ -132,7 +131,7 @@
             at_high = at - rows - 2
             v = jnp.where(even, inner[at_high].astype(F32), outer[at_high].astype(F32))
             keep = bottom
-        a = silu((v - mean) * scale)
+        a = silu_of_twice((v - mean) * scale)
         if keep is not None:
             a = a * keep
         a = a.astype(BF16)
@@ -196,7 +195,7 @@
     block, residual, acts, control = outs
     rows, c, width = x.shape
     mean, scale = whole_stats(st[...], c, rows * width * (c // G))
-    scale = scale * cols[c:, :1]
+    scale = 0.5 * scale * cols[c:, :1]
     top, bottom = flags[0:1, :1], flags[1:2, :1]
 
     def put(at, slot):
@@ -206,7 +205,7 @@
             v = conv_row(w1t[...], edges[3 * c :, :]) + cols[:c, :1]
         else:
             v = mid[at - 1]
-        a = silu((v - mean) * scale)
+        a = silu_of_twice((v - mean) * scale)
         if at == 0:
             a = a * top
         if at == rows + 1:
@@ -272,20 +271,28 @@
     next_chip = [(i, i + 1) for i in range(1, strips - 1, 2)]
     next_chip += [(target, source) for source, target in next_chip]
     shaped = jax.ShapeDtypeStruct
-    stat = shaped((strips, LANES), F32)
+    stat = shaped((8, LANES), F32)
     wide = shaped((3 * c, 3 * c), BF16)
     halo = shaped((2, c, width), BF16)
     row_macs = 2 * 9 * c * c * width
 
-    def spread(st):
-        return lax.all_to_all(st, "strip", 0, 0)
+    chips = [list(range(core, strips, 2)) for core in range(2)]
+
+    def paired(st):
+        return jnp.concatenate([st[:1], lax.ppermute(st[:1], "strip", same_chip)], axis=0)
+
+    def spread(pair):
+        sent = jnp.broadcast_to(pair[None], (strips // 2, 2, LANES))
+        rows_of_all = lax.all_to_all(sent, "strip", 0, 0, axis_index_groups=chips)
+        return rows_of_all.reshape(strips, LANES)
 
     st1, inner, outer = call(
         stats_kernel, "stats_first", 2, (stat, halo, halo), [], 16, 2 * 10**10
     )(flags, x)
+    pair, inner, outer = lax.optimization_barrier((paired(st1), inner, outer))
     outer = lax.ppermute(outer, "strip", next_chip)
     inner = lax.ppermute(inner, "strip", same_chip)
-    st1 = spread(st1)
+    st1 = spread(pair)
     mid, st2, edges, w1t, w2t, zt, cols = call(
         first_kernel,
         "conv_first",
@@ -303,7 +310,7 @@
         36,
         rows * row_macs,
     )(flags, x, inner, outer, st1, norm_gains[0], time_shift, conv_first[0], conv_second[0], zero_conv)
-    st2 = spread(st2)
+    st2 = spread(paired(st2))
     pieces = []
     after = zt
     for wanted in (((3, 5),), ((1, 3),), ((5, 7),), ((0, 1), (7, rows))):

time: 87.8 us -> 86 us (0.979)
  blocking collectives: 42.6 us -> 39.7 us
  waiting for transfers between devices: 14.1 us -> 15.8 us
    all_to_all x2, blocking collectives: 42.6 us -> 39.7 us  [spread(): rows_of_all = lax.all_to_all(sent, 'strip', 0, 0, axis_index_groups=chips)]
    ppermute x0 -> x2, waiting for transfers between devices: none -> 2.22 us  [paired(): lax.ppermute(st[:1], 'strip', same_chip)]
  transfers between devices with their start and end apart: 6 -> 8, of which waited for: 3 -> 5; matrix products, arithmetic and copies ran while one was open for 0% -> 0% of each run, Pallas kernels for 12% -> 12%
where the time goes in v5:
time: 86 us; the launch traced here: 85.9 us
  blocking collectives  39.7 us (46%)
  Pallas kernels  19.9 us (23%)
  waiting for transfers between devices  15.8 us (18%)
  starting transfers between devices  8.62 us (10%)
  local copies, waits for them, and re-layouts  1.46 us (2%)
    all_to_all x2, blocking collectives, spread(): rows_of_all = lax.all_to_all(sent, 'strip', 0, 0, axis_index_groups=chips)  39.7 us
    ppermute x4, waiting for transfers between devices, on_device(): lax.ppermute(residual, 'branch', [(0, 1), (1, 0)])  13.6 us
    pallas_call x4, Pallas kernels, on_device(): call(functools.partial(second_kernel, wanted), 'conv_second', 9, (shaped(...  9.68 us
    ppermute x4, starting transfers between devices, on_device(): lax.ppermute(residual, 'branch', [(0, 1), (1, 0)])  7.58 us
    pallas_call x1, Pallas kernels, on_device(): call(first_kernel, 'conv_first', 10, (shaped((rows, c, width), F32), stat...  5.92 us
    pallas_call x4, Pallas kernels, mix(): pl.pallas_call(functools.partial(mix_kernel, wanted), out_shape=whole, in...  3.36 us
    ppermute x2, waiting for transfers between devices, paired(): lax.ppermute(st[:1], 'strip', same_chip)  2.22 us
  transfers between devices with their start and end apart: 8, of which 5 were waited for; matrix products, arithmetic and copies ran while one was open for 0% of the time, Pallas kernels for 12%

profile of v5, /device:TPU:16, one launch (start us, length us, event | category | flops | bytes accessed | tf_op | source)
XLA Modules:
  0.0 85.9 jit_solution(16136381509610487593)
XLA Ops:
  0.1 1.3 %copy-done = bf16[1,8,256,320]{2,3,1,0:T(8,128)(2,1)S(1)} copy-done((bf16[1,8,256,320]{2,3,1,0:T(8,128)(2,1)S(1)}, bf16[1,8,256,320]{2,3,1,0:T(8,128)(2,1)}, u32[]{:S(2)}) %copy-start) | copy-done | bytes 1310744
  1.4 0.9 %stats_first.1 = (f32[8,128]{1,0:T(8,128)S(1)}, bf16[2,320,256]{2,1,0:T(8,128)(2,1)S(1)}, bf16[2,320,256]{2,1,0:T(8,128)(2,1)S(1)}) custom-call(f32[8,128]{1,0:T(8,128)S(1)} %iota.16.flags, bf16[8,320,256]{2,1,0:T(8,128)(2,1)S(1)} %bitcast.11), custom_call_target="tpu_custom_call" | custom-call | flops 20000000000 | bytes 4194304 | tf_op jit(solution)/shard_map/stats_first/pallas_call | solution.py:289
  2.5 1.1 %collective-permute-done = f32[1,128]{1,0:T(1,128)S(1)} collective-permute-done((f32[1,128]{1,0:T(1,128)S(1)}, f32[1,128]{1,0:T(1,128)S(1)}, u32[]{:S(2)}, u32[]{:S(2)}) %collective-permute-start) | collective-permute-done | bytes 544 | tf_op jit(solution)/shard_map/ppermute | solution.py:282
  3.6 0.2 collective-permute-start.1
  3.8 0.7 collective-permute-start.2
  4.5 25.1 %all_to_all.10 = f32[64,2,128]{2,1,0:T(2,128)S(1)} all-to-all(f32[64,2,128]{2,1,0:T(2,128)S(1)} %broadcast_in_dim.31), channel_id=1, replica_groups={{0,2,4,6,8,10,12,14,16,18,20,22,24,26,28,30,32,34,36,38,40,42,44,46,48,..., dimensions={0} | all-to-all | bytes 131072 | tf_op jit(solution)/shard_map/all_to_all | solution.py:286
  29.7 5.9 %conv_first.1 = (f32[8,320,256]{2,1,0:T(8,128)S(1)}, f32[8,128]{1,0:T(8,128)S(1)}, bf16[1920,256]{1,0:T(8,128)(2,1)S(1)}, bf16[960,960]{1,0:T(8,128)(2,1)S(1)}, ...) custom-call(f32[8,128]{1,0:T(8,128)S(1)} %iota.16.flags, ...), custom_call_target="tpu_custom_call" | custom-call | flops 3774873600 | bytes 4194304 | tf_op jit(solution)/shard_map/conv_first/pallas_call | solution.py:296
  35.7 1.1 %collective-permute-done.3 = f32[1,128]{1,0:T(1,128)S(1)} collective-permute-done((f32[1,128]{1,0:T(1,128)S(1)}, f32[1,128]{1,0:T(1,128)S(1)}, u32[]{:S(2)}, u32[]{:S(2)}) %collective-permute-start.3) | collective-permute-done | bytes 544 | tf_op jit(solution)/shard_map/ppermute | solution.py:282
  36.8 14.6 %all_to_all.11 = f32[64,2,128]{2,1,0:T(2,128)S(1)} all-to-all(f32[64,2,128]{2,1,0:T(2,128)S(1)} %broadcast_in_dim.32), channel_id=1, replica_groups={{0,2,4,6,8,10,12,14,16,18,20,22,24,26,28,30,32,34,36,38,40,42,44,46,48,..., dimensions={0} | all-to-all | bytes 131072 | tf_op jit(solution)/shard_map/all_to_all | solution.py:286
  51.4 1.9 %conv_second.4 = (f32[2,320,256]{2,1,0:T(8,128)S(1)}, bf16[2,320,256]{2,1,0:T(8,128)(2,1)S(1)}) custom-call(f32[8,128]{1,0:T(8,128)S(1)} %iota.16.flags, bf16[8,320,256]{2,1,0:T(8,128)(2,1)S(1)} %bitcast.13, f32[8,320,256]{2,1,0:T(8,128)S(1)} %get-tuple-element.32.mid, f32[128,128]{1,0:T(8,128)S(1)} %bitcast.17, f32[640,128]{1,0:T(8,128)S(1)} %get-tuple-element.34.cols, ...), custom_call_target="tpu_custom_call" | custom-call | flops 943718400 | bytes 4194304 | tf_op jit(solution)/shard_map/conv_second/pallas_call | solution.py:318
  53.3 0.9 %collective-permute-start.7 = (bf16[2,320,256]{2,1,0:T(8,128)(2,1)S(1)}, bf16[2,320,256]{2,1,0:T(8,128)(2,1)S(1)}, u32[]{:S(2)}, u32[]{:S(2)}) collective-permute-start(bf16[2,320,256]{2,1,0:T(8,128)(2,1)S(1)} %get-tuple-element.39.after), channel_id=1, source_target_pairs={{0,128},{128,0},{1,129},{129,1},{2,130},{130,2},{3,131},{131,3},{4... | collective-permute-start | bytes 983048 | tf_op jit(solution)/shard_map/ppermute | solution.py:333
  54.2 1.9 %conv_second.5 = (f32[2,320,256]{2,1,0:T(8,128)S(1)}, bf16[2,320,256]{2,1,0:T(8,128)(2,1)S(1)}) custom-call(f32[8,128]{1,0:T(8,128)S(1)} %iota.16.flags, bf16[8,320,256]{2,1,0:T(8,128)(2,1)S(1)} %bitcast.14, f32[8,320,256]{2,1,0:T(8,128)S(1)} %get-tuple-element.32.mid, f32[128,128]{1,0:T(8,128)S(1)} %bitcast.18, f32[640,128]{1,0:T(8,128)S(1)} %get-tuple-element.34.cols, ...), custom_call_target="tpu_custom_call" | custom-call | flops 943718400 | bytes 4194304 | tf_op jit(solution)/shard_map/conv_second/pallas_call | solution.py:318
  56.2 3.0 %collective-permute-start.6 = (bf16[2,320,256]{2,1,0:T(8,128)(2,1)S(1)}, bf16[2,320,256]{2,1,0:T(8,128)(2,1)S(1)}, u32[]{:S(2)}, u32[]{:S(2)}) collective-permute-start(bf16[2,320,256]{2,1,0:T(8,128)(2,1)S(1)} %get-tuple-element.40.after), channel_id=1, source_target_pairs={{0,128},{128,0},{1,129},{129,1},{2,130},{130,2},{3,131},{131,3},{4... | collective-permute-start | bytes 983048 | tf_op jit(solution)/shard_map/ppermute | solution.py:333
  59.2 1.9 %conv_second.6 = (f32[2,320,256]{2,1,0:T(8,128)S(1)}, bf16[2,320,256]{2,1,0:T(8,128)(2,1)S(1)}) custom-call(f32[8,128]{1,0:T(8,128)S(1)} %iota.16.flags, bf16[8,320,256]{2,1,0:T(8,128)(2,1)S(1)} %bitcast.15, f32[8,320,256]{2,1,0:T(8,128)S(1)} %get-tuple-element.32.mid, f32[128,128]{1,0:T(8,128)S(1)} %bitcast.19, f32[640,128]{1,0:T(8,128)S(1)} %get-tuple-element.34.cols, ...), custom_call_target="tpu_custom_call" | custom-call | flops 943718400 | bytes 4194304 | tf_op jit(solution)/shard_map/conv_second/pallas_call | solution.py:318
  61.1 0.7 collective-permute-start.5
  61.8 3.9 %conv_second.7 = (f32[2,320,256]{2,1,0:T(8,128)S(1)}, bf16[2,320,256]{2,1,0:T(8,128)(2,1)S(1)}) custom-call(f32[8,128]{1,0:T(8,128)S(1)} %iota.16.flags, bf16[8,320,256]{2,1,0:T(8,128)(2,1)S(1)} %bitcast.16, f32[8,320,256]{2,1,0:T(8,128)S(1)} %get-tuple-element.32.mid, f32[128,128]{1,0:T(8,128)S(1)} %bitcast.20, f32[640,128]{1,0:T(8,128)S(1)} %get-tuple-element.34.cols, ...), custom_call_target="tpu_custom_call" | custom-call | flops 943718400 | bytes 4194304 | tf_op jit(solution)/shard_map/conv_second/pallas_call | solution.py:318
  65.7 3.0 %collective-permute-start.4 = (bf16[2,320,256]{2,1,0:T(8,128)(2,1)S(1)}, bf16[2,320,256]{2,1,0:T(8,128)(2,1)S(1)}, u32[]{:S(2)}, u32[]{:S(2)}) collective-permute-start(bf16[2,320,256]{2,1,0:T(8,128)(2,1)S(1)} %get-tuple-element.43), channel_id=1, source_target_pairs={{0,128},{128,0},{1,129},{129,1},{2,130},{130,2},{3,131},{131,3},{4... | collective-permute-start | bytes 983048 | tf_op jit(solution)/shard_map/ppermute | solution.py:333
  68.7 0.8 mix.4.rest_0_
  69.5 3.2 %collective-permute-done.6.arrived = bf16[2,320,256]{2,1,0:T(8,128)(2,1)S(1)} collective-permute-done((bf16[2,320,256]{2,1,0:T(8,128)(2,1)S(1)}, bf16[2,320,256]{2,1,0:T(8,128)(2,1)S(1)}, u32[]{:S(2)}, u32[]{:S(2)}) %collective-permute-start.6) | collective-permute-done | bytes 327712 | tf_op jit(solution)/shard_map/ppermute | solution.py:333
  72.8 0.8 mix.5.rest_0_
  73.6 6.2 %collective-permute-done.5.arrived = bf16[2,320,256]{2,1,0:T(8,128)(2,1)S(1)} collective-permute-done((bf16[2,320,256]{2,1,0:T(8,128)(2,1)S(1)}, bf16[2,320,256]{2,1,0:T(8,128)(2,1)S(1)}, u32[]{:S(2)}, u32[]{:S(2)}) %collective-permute-start.5) | collective-permute-done | bytes 327712 | tf_op jit(solution)/shard_map/ppermute | solution.py:333
  79.8 0.8 mix.6.rest_0_
  80.7 4.2 %collective-permute-done.4.arrived = bf16[2,320,256]{2,1,0:T(8,128)(2,1)S(1)} collective-permute-done((bf16[2,320,256]{2,1,0:T(8,128)(2,1)S(1)}, bf16[2,320,256]{2,1,0:T(8,128)(2,1)S(1)}, u32[]{:S(2)}, u32[]{:S(2)}) %collective-permute-start.4) | collective-permute-done | bytes 327712 | tf_op jit(solution)/shard_map/ppermute | solution.py:333
  84.9 0.8 mix.7
  (26 shorter events, 0.3 us)
Async XLA Ops:
  0.1 1.3 %copy-start = (bf16[1,8,256,320]{2,3,1,0:T(8,128)(2,1)S(1)}, bf16[1,8,256,320]{2,3,1,0:T(8,128)(2,1)}, u32[]{:S(2)}) copy-start(bf16[1,8,256,320]{2,3,1,0:T(8,128)(2,1)} %param.6) | copy-start | bytes 3932164
  1.4 28.2 %copy-start.1 = (bf16[1,8,256,320]{2,3,1,0:T(8,128)(2,1)S(1)}, bf16[1,8,256,320]{2,3,1,0:T(8,128)(2,1)}, u32[]{:S(2)}) copy-start(bf16[1,8,256,320]{2,3,1,0:T(8,128)(2,1)} %param.6) | copy-start | bytes 3932164
  1.4 28.2 %copy-start.2 = (bf16[1,3,3,320,320]{4,3,2,1,0:T(8,128)(2,1)S(1)}, bf16[1,3,3,320,320]{4,3,2,1,0:T(8,128)(2,1)}, u32[]{:S(2)}) copy-start(bf16[1,3,3,320,320]{4,3,2,1,0:T(8,128)(2,1)} %param.7) | copy-start | bytes 5529604
  1.4 28.2 %copy-start.3 = (bf16[1,3,3,320,320]{4,3,2,1,0:T(8,128)(2,1)S(1)}, bf16[1,3,3,320,320]{4,3,2,1,0:T(8,128)(2,1)}, u32[]{:S(2)}) copy-start(bf16[1,3,3,320,320]{4,3,2,1,0:T(8,128)(2,1)} %param.8) | copy-start | bytes 5529604
  1.4 28.2 %copy-start.4 = (bf16[320,320]{1,0:T(8,128)(2,1)S(1)}, bf16[320,320]{1,0:T(8,128)(2,1)}, u32[]{:S(2)}) copy-start(bf16[320,320]{1,0:T(8,128)(2,1)} %z.1) | copy-start | bytes 614404
  1.4 28.3 %copy-start.5 = (f32[1,2,320]{2,1,0:T(2,128)S(1)}, f32[1,2,320]{2,1,0:T(2,128)}, u32[]{:S(2)}) copy-start(f32[1,2,320]{2,1,0:T(2,128)} %param.10) | copy-start | bytes 7684
  1.4 28.3 %copy-start.6 = (f32[1,320]{1,0:T(1,128)S(1)}, f32[1,320]{1,0:T(1,128)}, u32[]{:S(2)}) copy-start(f32[1,320]{1,0:T(1,128)} %shift.1) | copy-start | bytes 3844
  2.4 1.2 %collective-permute-start = (f32[1,128]{1,0:T(1,128)S(1)}, f32[1,128]{1,0:T(1,128)S(1)}, u32[]{:S(2)}, u32[]{:S(2)}) collective-permute-start(f32[1,128]{1,0:T(1,128)S(1)} %slice.8), channel_id=1, source_target_pairs={{0,1},{1,0},{2,3},{3,2},{4,5},{5,4},{6,7},{7,6},{8,9},{9,8},{10,11... | collective-permute-start | bytes 1544 | tf_op jit(solution)/shard_map/ppermute | solution.py:282
  3.6 26.0 %collective-permute-start.1 = (bf16[2,320,256]{2,1,0:T(8,128)(2,1)S(1)}, bf16[2,320,256]{2,1,0:T(8,128)(2,1)S(1)}, u32[]{:S(2)}, u32[]{:S(2)}) collective-permute-start(bf16[2,320,256]{2,1,0:T(8,128)(2,1)S(1)} %get-tuple-element.29), channel_id=1, source_target_pairs={{0,1},{1,0},{2,3},{3,2},{4,5},{5,4},{6,7},{7,6},{8,9},{9,8},{10,11... | collective-permute-start | bytes 983048 | tf_op jit(solution)/shard_map/ppermute | solution.py:294
  3.8 25.8 %collective-permute-start.2 = (bf16[2,320,256]{2,1,0:T(8,128)(2,1)S(1)}, bf16[2,320,256]{2,1,0:T(8,128)(2,1)S(1)}, u32[]{:S(2)}, u32[]{:S(2)}) collective-permute-start(bf16[2,320,256]{2,1,0:T(8,128)(2,1)S(1)} %get-tuple-element.30), channel_id=1, source_target_pairs={{1,2},{3,4},{5,6},{7,8},{9,10},{11,12},{13,14},{15,16},{17,18},{19... | collective-permute-start | bytes 983048 | tf_op jit(solution)/shard_map/ppermute | solution.py:293
  35.6 1.2 %collective-permute-start.3 = (f32[1,128]{1,0:T(1,128)S(1)}, f32[1,128]{1,0:T(1,128)S(1)}, u32[]{:S(2)}, u32[]{:S(2)}) collective-permute-start(f32[1,128]{1,0:T(1,128)S(1)} %slice.9), channel_id=1, source_target_pairs={{0,1},{1,0},{2,3},{3,2},{4,5},{5,4},{6,7},{7,6},{8,9},{9,8},{10,11... | collective-permute-start | bytes 1544 | tf_op jit(solution)/shard_map/ppermute | solution.py:282
  53.3 15.3 %collective-permute-start.7 = (bf16[2,320,256]{2,1,0:T(8,128)(2,1)S(1)}, bf16[2,320,256]{2,1,0:T(8,128)(2,1)S(1)}, u32[]{:S(2)}, u32[]{:S(2)}) collective-permute-start(bf16[2,320,256]{2,1,0:T(8,128)(2,1)S(1)} %get-tuple-element.39.after), channel_id=1, source_target_pairs={{0,128},{128,0},{1,129},{129,1},{2,130},{130,2},{3,131},{131,3},{4... | collective-permute-start | bytes 983048 | tf_op jit(solution)/shard_map/ppermute | solution.py:333
  56.2 16.6 %collective-permute-start.6 = (bf16[2,320,256]{2,1,0:T(8,128)(2,1)S(1)}, bf16[2,320,256]{2,1,0:T(8,128)(2,1)S(1)}, u32[]{:S(2)}, u32[]{:S(2)}) collective-permute-start(bf16[2,320,256]{2,1,0:T(8,128)(2,1)S(1)} %get-tuple-element.40.after), channel_id=1, source_target_pairs={{0,128},{128,0},{1,129},{129,1},{2,130},{130,2},{3,131},{131,3},{4... | collective-permute-start | bytes 983048 | tf_op jit(solution)/shard_map/ppermute | solution.py:333
  61.1 18.7 %collective-permute-start.5 = (bf16[2,320,256]{2,1,0:T(8,128)(2,1)S(1)}, bf16[2,320,256]{2,1,0:T(8,128)(2,1)S(1)}, u32[]{:S(2)}, u32[]{:S(2)}) collective-permute-start(bf16[2,320,256]{2,1,0:T(8,128)(2,1)S(1)} %get-tuple-element.41.after), channel_id=1, source_target_pairs={{0,128},{128,0},{1,129},{129,1},{2,130},{130,2},{3,131},{131,3},{4... | collective-permute-start | bytes 983048 | tf_op jit(solution)/shard_map/ppermute | solution.py:333
  65.7 19.1 %collective-permute-start.4 = (bf16[2,320,256]{2,1,0:T(8,128)(2,1)S(1)}, bf16[2,320,256]{2,1,0:T(8,128)(2,1)S(1)}, u32[]{:S(2)}, u32[]{:S(2)}) collective-permute-start(bf16[2,320,256]{2,1,0:T(8,128)(2,1)S(1)} %get-tuple-element.43), channel_id=1, source_target_pairs={{0,128},{128,0},{1,129},{129,1},{2,130},{130,2},{3,131},{131,3},{4... | collective-permute-start | bytes 983048 | tf_op jit(solution)/shard_map/ppermute | solution.py:333

commit v6 on v5

--- a/solution.py
+++ b/solution.py
@@ -44,6 +44,10 @@
     return jnp.sum(jnp.where(eye, row, 0.0), axis=1, keepdims=True)
 
 
+def widened(v, width):
+    return jnp.concatenate([v] * (width // LANES), axis=1)
+
+
 def fold(x):
     parts = [x[:, i : i + LANES] for i in range(0, x.shape[1], LANES)]
     return functools.reduce(jnp.add, parts)
@@ -93,10 +97,14 @@
     return y[c : 2 * c] + left + right
 
 
-def stats_kernel(flags, x, out, inner, outer):
+def stats_kernel(flags, x, out):
     rows, c, width = x.shape
     st = strip_stats(lambda r: x[r].astype(F32), rows, c, width)
     out[...] = jnp.broadcast_to(st, out.shape)
+
+
+def halo_kernel(flags, x, after, inner, outer):
+    rows = x.shape[0]
     even = flags[3:4, :1] > 0.5
     for i in range(2):
         begin, end = x[i].astype(F32), x[rows - 2 + i].astype(F32)
@@ -114,7 +122,7 @@
 
 
 def first_kernel(
-    flags, x, inner, outer, st, gains, shift, w1, w2, z, mid, out, edges, w1t, w2t, zt, cols, acts
+    flags, x, inner, outer, st, gains, shift, w1, mid, out, edges, w1t, cols, acts
 ):
     rows, c, width = x.shape
     mean, scale = whole_stats(st[...], c, rows * width * (c // G))
@@ -149,22 +157,11 @@
     first, second = group_masks(c)
     per_row = width * (c // G)
 
-    def turn_z():
-        zt[...] = z[...].T
-
     def keep_columns():
         both = jnp.concatenate([shift_c, column(gains[1:2, :])], axis=0)
         cols[...] = jnp.broadcast_to(both, cols.shape)
 
-    beside = {
-        1: keep_columns,
-        2: lambda: turned(w2, w2t, 0),
-        3: lambda: turned(w2, w2t, 1),
-        4: lambda: turned(w2, w2t, 2),
-        5: turn_z,
-        6: lambda: put(0),
-        7: lambda: put(rows + 3),
-    }
+    beside = {1: keep_columns, 4: lambda: put(0), 6: lambda: put(rows + 3)}
     for r in range(1, rows + 1):
         y = conv_row(w1t[...], acts[r * c : (r + 3) * c, :]) + shift_c
         mid[r - 1] = y
@@ -191,18 +188,24 @@
     out[...] = jnp.broadcast_to(st2, out.shape)
 
 
+def prepare_kernel(w2, z, after, w2t, zt):
+    for kx in range(3):
+        turned(w2, w2t, kx)
+    zt[...] = z[...].T
+
+
 def second_kernel(wanted, flags, x, mid, st, cols, w2t, zt, edges, w1t, after, *outs):
     block, residual, acts, control = outs
     rows, c, width = x.shape
     mean, scale = whole_stats(st[...], c, rows * width * (c // G))
-    scale = 0.5 * scale * cols[c:, :1]
+    scale = scale * widened(0.5 * cols[c:, :], width)
     top, bottom = flags[0:1, :1], flags[1:2, :1]
 
     def put(at, slot):
         if at == 0:
-            v = conv_row(w1t[...], edges[: 3 * c, :]) + cols[:c, :1]
+            v = conv_row(w1t[...], edges[: 3 * c, :]) + widened(cols[:c, :], width)
         elif at == rows + 1:
-            v = conv_row(w1t[...], edges[3 * c :, :]) + cols[:c, :1]
+            v = conv_row(w1t[...], edges[3 * c :, :]) + widened(cols[:c, :], width)
         else:
             v = mid[at - 1]
         a = silu_of_twice((v - mean) * scale)
@@ -286,31 +289,34 @@
         rows_of_all = lax.all_to_all(sent, "strip", 0, 0, axis_index_groups=chips)
         return rows_of_all.reshape(strips, LANES)
 
-    st1, inner, outer = call(
-        stats_kernel, "stats_first", 2, (stat, halo, halo), [], 16, 2 * 10**10
-    )(flags, x)
+    (st1,) = call(stats_kernel, "stats_first", 2, (stat,), [], 16, 2 * 10**10)(flags, x)
+    inner, outer = call(halo_kernel, "halo", 2, (halo, halo), [], 16, 10**8, unread=1)(
+        flags, x, st1
+    )
     pair, inner, outer = lax.optimization_barrier((paired(st1), inner, outer))
     outer = lax.ppermute(outer, "strip", next_chip)
     inner = lax.ppermute(inner, "strip", same_chip)
     st1 = spread(pair)
-    mid, st2, edges, w1t, w2t, zt, cols = call(
+    mid, st2, edges, w1t, cols = call(
         first_kernel,
         "conv_first",
-        10,
+        8,
         (
             shaped((rows, c, width), F32),
             stat,
             shaped((6 * c, width), BF16),
             wide,
-            wide,
-            shaped((c, c), BF16),
             shaped((2 * c, LANES), F32),
         ),
         [pltpu.VMEM(((rows + 4) * c, width), BF16)],
         36,
         rows * row_macs,
-    )(flags, x, inner, outer, st1, norm_gains[0], time_shift, conv_first[0], conv_second[0], zero_conv)
-    st2 = spread(paired(st2))
+    )(flags, x, inner, outer, st1, norm_gains[0], time_shift, conv_first[0])
+    w2t, zt = call(
+        prepare_kernel, "prepare", 2, (wide, shaped((c, c), BF16)), [], 16, 10**9, unread=1
+    )(conv_second[0], zero_conv, st2)
+    pair, w2t, zt = lax.optimization_barrier((paired(st2), w2t, zt))
+    st2 = spread(pair)
     pieces = []
     after = zt
     for wanted in (((3, 5),), ((1, 3),), ((5, 7),), ((0, 1), (7, rows))):

time: 86 us -> 85.6 us (level)
  waiting for transfers between devices: 15.8 us -> 14.9 us
    ppermute x2, waiting for transfers between devices: 2.22 us -> 0.97 us  [paired(): lax.ppermute(st[:1], 'strip', same_chip)]
    pallas_call x2 -> x4, Pallas kernels: 6.84 us -> 7.7 us  [the longest x1 5.73 us: on_device(): call(first_kernel, 'conv_first', 8, (shaped((rows, c, width), F32), stat,...]
  transfers between devices with their start and end apart: 8 -> 8, of which waited for: 5 -> 5; matrix products, arithmetic and copies ran while one was open for 0% -> 0% of each run, Pallas kernels for 12% -> 13%
where the time goes in v6:
time: 85.6 us; the launch traced here: 85.4 us
  blocking collectives  39.8 us (46%)
  Pallas kernels  20.5 us (24%)
  waiting for transfers between devices  14.9 us (17%)
  starting transfers between devices  8.43 us (10%)
  local copies, waits for them, and re-layouts  1.47 us (2%)
    all_to_all x2, blocking collectives, spread(): rows_of_all = lax.all_to_all(sent, 'strip', 0, 0, axis_index_groups=chips)  39.8 us
    ppermute x4, waiting for transfers between devices, on_device(): lax.ppermute(residual, 'branch', [(0, 1), (1, 0)])  13.9 us
    pallas_call x4, Pallas kernels, on_device(): call(functools.partial(second_kernel, wanted), 'conv_second', 9, (shaped(...  9.48 us
    ppermute x4, starting transfers between devices, on_device(): lax.ppermute(residual, 'branch', [(0, 1), (1, 0)])  7.41 us
    pallas_call x1, Pallas kernels, on_device(): call(first_kernel, 'conv_first', 8, (shaped((rows, c, width), F32), stat,...  5.73 us
    pallas_call x4, Pallas kernels, mix(): pl.pallas_call(functools.partial(mix_kernel, wanted), out_shape=whole, in...  3.36 us
  transfers between devices with their start and end apart: 8, of which 5 were waited for; matrix products, arithmetic and copies ran while one was open for 0% of the time, Pallas kernels for 13%

profile of v6, /device:TPU:16, one launch (start us, length us, event | category | flops | bytes accessed | tf_op | source)
XLA Modules:
  0.0 85.4 jit_solution(8020162598894282730)
XLA Ops:
  0.1 1.3 %copy-done = bf16[1,8,256,320]{2,3,1,0:T(8,128)(2,1)S(1)} copy-done((bf16[1,8,256,320]{2,3,1,0:T(8,128)(2,1)S(1)}, bf16[1,8,256,320]{2,3,1,0:T(8,128)(2,1)}, u32[]{:S(2)}) %copy-start) | copy-done | bytes 1310744
  1.4 0.8 stats_first.1.after
  2.3 0.2 halo.1
  2.5 0.9 %collective-permute-done = f32[1,128]{1,0:T(1,128)S(1)} collective-permute-done((f32[1,128]{1,0:T(1,128)S(1)}, f32[1,128]{1,0:T(1,128)S(1)}, u32[]{:S(2)}, u32[]{:S(2)}) %collective-permute-start) | collective-permute-done | bytes 544 | tf_op jit(solution)/shard_map/ppermute | solution.py:285
  3.6 0.7 collective-permute-start.2
  4.3 25.1 %all_to_all.10 = f32[64,2,128]{2,1,0:T(2,128)S(1)} all-to-all(f32[64,2,128]{2,1,0:T(2,128)S(1)} %broadcast_in_dim.31), channel_id=1, replica_groups={{0,2,4,6,8,10,12,14,16,18,20,22,24,26,28,30,32,34,36,38,40,42,44,46,48,..., dimensions={0} | all-to-all | bytes 131072 | tf_op jit(solution)/shard_map/all_to_all | solution.py:289
  29.5 5.7 %conv_first.1 = (f32[8,320,256]{2,1,0:T(8,128)S(1)}, f32[8,128]{1,0:T(8,128)S(1)}, bf16[1920,256]{1,0:T(8,128)(2,1)S(1)}, bf16[960,960]{1,0:T(8,128)(2,1)S(1)}, f32[640,128]{1,0:T(8,128)S(1)}) custom-call(f32[8,128]{1,0:T(8,128)S(1)} %iota.16.flags, bf16[8,320,256]{2,1,0:T(8,128)(2,1)S(1)} %bitcast.13, ...), custom_call_target="tpu_custom_call" | custom-call | flops 3774873600 | bytes 4194304 | tf_op jit(solution)/shard_map/conv_first/pallas_call | solution.py:300
  35.3 1.0 %prepare.1 = (bf16[960,960]{1,0:T(8,128)(2,1)S(1)}, bf16[320,320]{1,0:T(8,128)(2,1)S(1)}) custom-call(bf16[3,3,320,320]{3,2,1,0:T(8,128)(2,1)S(1)} %bitcast.24, bf16[320,320]{1,0:T(8,128)(2,1)S(1)} %copy-done.4, f32[8,128]{1,0:T(8,128)S(1)} %get-tuple-element.34.after), custom_call_target="tpu_custom_call" | custom-call | flops 1000000000 | bytes 4194304 | tf_op jit(solution)/shard_map/prepare/pallas_call | solution.py:315
  36.4 14.6 %all_to_all.11 = f32[64,2,128]{2,1,0:T(2,128)S(1)} all-to-all(f32[64,2,128]{2,1,0:T(2,128)S(1)} %broadcast_in_dim.32), channel_id=1, replica_groups={{0,2,4,6,8,10,12,14,16,18,20,22,24,26,28,30,32,34,36,38,40,42,44,46,48,..., dimensions={0} | all-to-all | bytes 131072 | tf_op jit(solution)/shard_map/all_to_all | solution.py:289
  51.1 1.9 %conv_second.4 = (f32[2,320,256]{2,1,0:T(8,128)S(1)}, bf16[2,320,256]{2,1,0:T(8,128)(2,1)S(1)}) custom-call(f32[8,128]{1,0:T(8,128)S(1)} %iota.16.flags, bf16[8,320,256]{2,1,0:T(8,128)(2,1)S(1)} %bitcast.14, f32[8,320,256]{2,1,0:T(8,128)S(1)} %get-tuple-element.33.mid, f32[128,128]{1,0:T(8,128)S(1)} %bitcast.18, f32[640,128]{1,0:T(8,128)S(1)} %get-tuple-element.38.cols, ...), custom_call_target="tpu_custom_call" | custom-call | flops 943718400 | bytes 4194304 | tf_op jit(solution)/shard_map/conv_second/pallas_call | solution.py:324
  52.9 0.7 collective-permute-start.7
  53.6 1.9 %conv_second.5 = (f32[2,320,256]{2,1,0:T(8,128)S(1)}, bf16[2,320,256]{2,1,0:T(8,128)(2,1)S(1)}) custom-call(f32[8,128]{1,0:T(8,128)S(1)} %iota.16.flags, bf16[8,320,256]{2,1,0:T(8,128)(2,1)S(1)} %bitcast.15, f32[8,320,256]{2,1,0:T(8,128)S(1)} %get-tuple-element.33.mid, f32[128,128]{1,0:T(8,128)S(1)} %bitcast.19, f32[640,128]{1,0:T(8,128)S(1)} %get-tuple-element.38.cols, ...), custom_call_target="tpu_custom_call" | custom-call | flops 943718400 | bytes 4194304 | tf_op jit(solution)/shard_map/conv_second/pallas_call | solution.py:324
  55.5 3.0 %collective-permute-start.6 = (bf16[2,320,256]{2,1,0:T(8,128)(2,1)S(1)}, bf16[2,320,256]{2,1,0:T(8,128)(2,1)S(1)}, u32[]{:S(2)}, u32[]{:S(2)}) collective-permute-start(bf16[2,320,256]{2,1,0:T(8,128)(2,1)S(1)} %get-tuple-element.44.after), channel_id=1, source_target_pairs={{0,128},{128,0},{1,129},{129,1},{2,130},{130,2},{3,131},{131,3},{4... | collective-permute-start | bytes 983048 | tf_op jit(solution)/shard_map/ppermute | solution.py:339
  58.5 1.9 %conv_second.6 = (f32[2,320,256]{2,1,0:T(8,128)S(1)}, bf16[2,320,256]{2,1,0:T(8,128)(2,1)S(1)}) custom-call(f32[8,128]{1,0:T(8,128)S(1)} %iota.16.flags, bf16[8,320,256]{2,1,0:T(8,128)(2,1)S(1)} %bitcast.16, f32[8,320,256]{2,1,0:T(8,128)S(1)} %get-tuple-element.33.mid, f32[128,128]{1,0:T(8,128)S(1)} %bitcast.20, f32[640,128]{1,0:T(8,128)S(1)} %get-tuple-element.38.cols, ...), custom_call_target="tpu_custom_call" | custom-call | flops 943718400 | bytes 4194304 | tf_op jit(solution)/shard_map/conv_second/pallas_call | solution.py:324
  60.4 0.7 collective-permute-start.5
  61.1 3.9 %conv_second.7 = (f32[2,320,256]{2,1,0:T(8,128)S(1)}, bf16[2,320,256]{2,1,0:T(8,128)(2,1)S(1)}) custom-call(f32[8,128]{1,0:T(8,128)S(1)} %iota.16.flags, bf16[8,320,256]{2,1,0:T(8,128)(2,1)S(1)} %bitcast.17, f32[8,320,256]{2,1,0:T(8,128)S(1)} %get-tuple-element.33.mid, f32[128,128]{1,0:T(8,128)S(1)} %bitcast.21, f32[640,128]{1,0:T(8,128)S(1)} %get-tuple-element.38.cols, ...), custom_call_target="tpu_custom_call" | custom-call | flops 943718400 | bytes 4194304 | tf_op jit(solution)/shard_map/conv_second/pallas_call | solution.py:324
  65.0 3.0 %collective-permute-start.4 = (bf16[2,320,256]{2,1,0:T(8,128)(2,1)S(1)}, bf16[2,320,256]{2,1,0:T(8,128)(2,1)S(1)}, u32[]{:S(2)}, u32[]{:S(2)}) collective-permute-start(bf16[2,320,256]{2,1,0:T(8,128)(2,1)S(1)} %get-tuple-element.47), channel_id=1, source_target_pairs={{0,128},{128,0},{1,129},{129,1},{2,130},{130,2},{3,131},{131,3},{4... | collective-permute-start | bytes 983048 | tf_op jit(solution)/shard_map/ppermute | solution.py:339
  68.0 0.8 mix.4.rest_0_
  68.8 3.4 %collective-permute-done.6.arrived = bf16[2,320,256]{2,1,0:T(8,128)(2,1)S(1)} collective-permute-done((bf16[2,320,256]{2,1,0:T(8,128)(2,1)S(1)}, bf16[2,320,256]{2,1,0:T(8,128)(2,1)S(1)}, u32[]{:S(2)}, u32[]{:S(2)}) %collective-permute-start.6) | collective-permute-done | bytes 327712 | tf_op jit(solution)/shard_map/ppermute | solution.py:339
  72.2 0.8 mix.5.rest_0_
  73.0 6.2 %collective-permute-done.5.arrived = bf16[2,320,256]{2,1,0:T(8,128)(2,1)S(1)} collective-permute-done((bf16[2,320,256]{2,1,0:T(8,128)(2,1)S(1)}, bf16[2,320,256]{2,1,0:T(8,128)(2,1)S(1)}, u32[]{:S(2)}, u32[]{:S(2)}) %collective-permute-start.5) | collective-permute-done | bytes 327712 | tf_op jit(solution)/shard_map/ppermute | solution.py:339
  79.2 0.8 mix.6.rest_0_
  80.1 4.4 %collective-permute-done.4.arrived = bf16[2,320,256]{2,1,0:T(8,128)(2,1)S(1)} collective-permute-done((bf16[2,320,256]{2,1,0:T(8,128)(2,1)S(1)}, bf16[2,320,256]{2,1,0:T(8,128)(2,1)S(1)}, u32[]{:S(2)}, u32[]{:S(2)}) %collective-permute-start.4) | collective-permute-done | bytes 327712 | tf_op jit(solution)/shard_map/ppermute | solution.py:339
  84.4 0.8 mix.7
  (28 shorter events, 0.6 us)
Async XLA Ops:
  0.1 1.3 %copy-start = (bf16[1,8,256,320]{2,3,1,0:T(8,128)(2,1)S(1)}, bf16[1,8,256,320]{2,3,1,0:T(8,128)(2,1)}, u32[]{:S(2)}) copy-start(bf16[1,8,256,320]{2,3,1,0:T(8,128)(2,1)} %param.6) | copy-start | bytes 3932164
  1.4 28.0 %copy-start.1 = (bf16[1,8,256,320]{2,3,1,0:T(8,128)(2,1)S(1)}, bf16[1,8,256,320]{2,3,1,0:T(8,128)(2,1)}, u32[]{:S(2)}) copy-start(bf16[1,8,256,320]{2,3,1,0:T(8,128)(2,1)} %param.6) | copy-start | bytes 3932164
  1.4 28.0 %copy-start.2 = (bf16[1,3,3,320,320]{4,3,2,1,0:T(8,128)(2,1)S(1)}, bf16[1,3,3,320,320]{4,3,2,1,0:T(8,128)(2,1)}, u32[]{:S(2)}) copy-start(bf16[1,3,3,320,320]{4,3,2,1,0:T(8,128)(2,1)} %param.7) | copy-start | bytes 5529604
  1.4 28.0 %copy-start.5 = (f32[1,2,320]{2,1,0:T(2,128)S(1)}, f32[1,2,320]{2,1,0:T(2,128)}, u32[]{:S(2)}) copy-start(f32[1,2,320]{2,1,0:T(2,128)} %param.10) | copy-start | bytes 7684
  1.4 28.0 %copy-start.6 = (f32[1,320]{1,0:T(1,128)S(1)}, f32[1,320]{1,0:T(1,128)}, u32[]{:S(2)}) copy-start(f32[1,320]{1,0:T(1,128)} %shift.1) | copy-start | bytes 3844
  2.2 1.2 %collective-permute-start = (f32[1,128]{1,0:T(1,128)S(1)}, f32[1,128]{1,0:T(1,128)S(1)}, u32[]{:S(2)}, u32[]{:S(2)}) collective-permute-start(f32[1,128]{1,0:T(1,128)S(1)} %slice.8), channel_id=1, source_target_pairs={{0,1},{1,0},{2,3},{3,2},{4,5},{5,4},{6,7},{7,6},{8,9},{9,8},{10,11... | collective-permute-start | bytes 1544 | tf_op jit(solution)/shard_map/ppermute | solution.py:285
  3.4 26.0 %collective-permute-start.1 = (bf16[2,320,256]{2,1,0:T(8,128)(2,1)S(1)}, bf16[2,320,256]{2,1,0:T(8,128)(2,1)S(1)}, u32[]{:S(2)}, u32[]{:S(2)}) collective-permute-start(bf16[2,320,256]{2,1,0:T(8,128)(2,1)S(1)} %get-tuple-element.30), channel_id=1, source_target_pairs={{0,1},{1,0},{2,3},{3,2},{4,5},{5,4},{6,7},{7,6},{8,9},{9,8},{10,11... | collective-permute-start | bytes 983048 | tf_op jit(solution)/shard_map/ppermute | solution.py:298
  3.6 25.8 %collective-permute-start.2 = (bf16[2,320,256]{2,1,0:T(8,128)(2,1)S(1)}, bf16[2,320,256]{2,1,0:T(8,128)(2,1)S(1)}, u32[]{:S(2)}, u32[]{:S(2)}) collective-permute-start(bf16[2,320,256]{2,1,0:T(8,128)(2,1)S(1)} %get-tuple-element.31), channel_id=1, source_target_pairs={{1,2},{3,4},{5,6},{7,8},{9,10},{11,12},{13,14},{15,16},{17,18},{19... | collective-permute-start | bytes 983048 | tf_op jit(solution)/shard_map/ppermute | solution.py:297
  29.5 5.8 %copy-start.3 = (bf16[1,3,3,320,320]{4,3,2,1,0:T(8,128)(2,1)S(1)}, bf16[1,3,3,320,320]{4,3,2,1,0:T(8,128)(2,1)}, u32[]{:S(2)}) copy-start(bf16[1,3,3,320,320]{4,3,2,1,0:T(8,128)(2,1)} %param.8) | copy-start | bytes 5529604
  29.5 5.8 %copy-start.4 = (bf16[320,320]{1,0:T(8,128)(2,1)S(1)}, bf16[320,320]{1,0:T(8,128)(2,1)}, u32[]{:S(2)}) copy-start(bf16[320,320]{1,0:T(8,128)(2,1)} %z.1) | copy-start | bytes 614404
  35.2 1.2 %collective-permute-start.3 = (f32[1,128]{1,0:T(1,128)S(1)}, f32[1,128]{1,0:T(1,128)S(1)}, u32[]{:S(2)}, u32[]{:S(2)}) collective-permute-start(f32[1,128]{1,0:T(1,128)S(1)} %slice.9), channel_id=1, source_target_pairs={{0,1},{1,0},{2,3},{3,2},{4,5},{5,4},{6,7},{7,6},{8,9},{9,8},{10,11... | collective-permute-start | bytes 1544 | tf_op jit(solution)/shard_map/ppermute | solution.py:285
  52.9 15.1 %collective-permute-start.7 = (bf16[2,320,256]{2,1,0:T(8,128)(2,1)S(1)}, bf16[2,320,256]{2,1,0:T(8,128)(2,1)S(1)}, u32[]{:S(2)}, u32[]{:S(2)}) collective-permute-start(bf16[2,320,256]{2,1,0:T(8,128)(2,1)S(1)} %get-tuple-element.43.after), channel_id=1, source_target_pairs={{0,128},{128,0},{1,129},{129,1},{2,130},{130,2},{3,131},{131,3},{4... | collective-permute-start | bytes 983048 | tf_op jit(solution)/shard_map/ppermute | solution.py:339
  55.5 16.7 %collective-permute-start.6 = (bf16[2,320,256]{2,1,0:T(8,128)(2,1)S(1)}, bf16[2,320,256]{2,1,0:T(8,128)(2,1)S(1)}, u32[]{:S(2)}, u32[]{:S(2)}) collective-permute-start(bf16[2,320,256]{2,1,0:T(8,128)(2,1)S(1)} %get-tuple-element.44.after), channel_id=1, source_target_pairs={{0,128},{128,0},{1,129},{129,1},{2,130},{130,2},{3,131},{131,3},{4... | collective-permute-start | bytes 983048 | tf_op jit(solution)/shard_map/ppermute | solution.py:339
  60.4 18.8 %collective-permute-start.5 = (bf16[2,320,256]{2,1,0:T(8,128)(2,1)S(1)}, bf16[2,320,256]{2,1,0:T(8,128)(2,1)S(1)}, u32[]{:S(2)}, u32[]{:S(2)}) collective-permute-start(bf16[2,320,256]{2,1,0:T(8,128)(2,1)S(1)} %get-tuple-element.45.after), channel_id=1, source_target_pairs={{0,128},{128,0},{1,129},{129,1},{2,130},{130,2},{3,131},{131,3},{4... | collective-permute-start | bytes 983048 | tf_op jit(solution)/shard_map/ppermute | solution.py:339
  65.0 19.4 %collective-permute-start.4 = (bf16[2,320,256]{2,1,0:T(8,128)(2,1)S(1)}, bf16[2,320,256]{2,1,0:T(8,128)(2,1)S(1)}, u32[]{:S(2)}, u32[]{:S(2)}) collective-permute-start(bf16[2,320,256]{2,1,0:T(8,128)(2,1)S(1)} %get-tuple-element.47), channel_id=1, source_target_pairs={{0,128},{128,0},{1,129},{129,1},{2,130},{130,2},{3,131},{131,3},{4... | collective-permute-start | bytes 983048 | tf_op jit(solution)/shard_map/ppermute | solution.py:339

commit v7 on v6

--- a/solution.py
+++ b/solution.py
@@ -293,7 +293,7 @@
     inner, outer = call(halo_kernel, "halo", 2, (halo, halo), [], 16, 10**8, unread=1)(
         flags, x, st1
     )
-    pair, inner, outer = lax.optimization_barrier((paired(st1), inner, outer))
+    pair, inner = lax.optimization_barrier((paired(st1), inner))
     outer = lax.ppermute(outer, "strip", next_chip)
     inner = lax.ppermute(inner, "strip", same_chip)
     st1 = spread(pair)

time: 85.6 us -> 85.3 us (level)
  starting transfers between devices: 8.43 us -> 11 us
  blocking collectives: 39.8 us -> 37.6 us
    ppermute x1, starting transfers between devices: 0.21 us -> 2.75 us  [on_device(): inner = lax.ppermute(inner, 'strip', same_chip)]
    all_to_all x2, blocking collectives: 39.8 us -> 37.6 us  [spread(): rows_of_all = lax.all_to_all(sent, 'strip', 0, 0, axis_index_groups=chips)]
where the time goes in v7:
time: 85.3 us; the launch traced here: 85.1 us
  blocking collectives  37.6 us (44%)
  Pallas kernels  20.5 us (24%)
  waiting for transfers between devices  14.2 us (17%)
  starting transfers between devices  11 us (13%)
  local copies, waits for them, and re-layouts  1.47 us (2%)
    all_to_all x2, blocking collectives, spread(): rows_of_all = lax.all_to_all(sent, 'strip', 0, 0, axis_index_groups=chips)  37.6 us
    ppermute x4, waiting for transfers between devices, on_device(): lax.ppermute(residual, 'branch', [(0, 1), (1, 0)])  13.9 us
    pallas_call x4, Pallas kernels, on_device(): call(functools.partial(second_kernel, wanted), 'conv_second', 9, (shaped(...  9.48 us
    ppermute x4, starting transfers between devices, on_device(): lax.ppermute(residual, 'branch', [(0, 1), (1, 0)])  7.4 us
    pallas_call x1, Pallas kernels, on_device(): call(first_kernel, 'conv_first', 8, (shaped((rows, c, width), F32), stat,...  5.72 us
    pallas_call x4, Pallas kernels, mix(): pl.pallas_call(functools.partial(mix_kernel, wanted), out_shape=whole, in...  3.36 us
    ppermute x1, starting transfers between devices, on_device(): inner = lax.ppermute(inner, 'strip', same_chip)  2.75 us
  transfers between devices with their start and end apart: 8, of which 5 were waited for; matrix products, arithmetic and copies ran while one was open for 0% of the time, Pallas kernels for 13%

profile of v7, /device:TPU:16, one launch (start us, length us, event | category | flops | bytes accessed | tf_op | source)
XLA Modules:
  0.0 85.1 jit_solution(17712270809180364205)
XLA Ops:
  0.1 1.3 %copy-done = bf16[1,8,256,320]{2,3,1,0:T(8,128)(2,1)S(1)} copy-done((bf16[1,8,256,320]{2,3,1,0:T(8,128)(2,1)S(1)}, bf16[1,8,256,320]{2,3,1,0:T(8,128)(2,1)}, u32[]{:S(2)}) %copy-start) | copy-done | bytes 1310744
  1.4 0.8 stats_first.1.after
  2.3 0.2 halo.1
  2.5 0.7 collective-permute-start.2
  3.4 2.7 %collective-permute-start.1 = (bf16[2,320,256]{2,1,0:T(8,128)(2,1)S(1)}, bf16[2,320,256]{2,1,0:T(8,128)(2,1)S(1)}, u32[]{:S(2)}, u32[]{:S(2)}) collective-permute-start(bf16[2,320,256]{2,1,0:T(8,128)(2,1)S(1)} %get-tuple-element.28), channel_id=1, source_target_pairs={{0,1},{1,0},{2,3},{3,2},{4,5},{5,4},{6,7},{7,6},{8,9},{9,8},{10,11... | collective-permute-start | bytes 983048 | tf_op jit(solution)/shard_map/ppermute | solution.py:298
  6.1 22.9 %all_to_all.10 = f32[64,2,128]{2,1,0:T(2,128)S(1)} all-to-all(f32[64,2,128]{2,1,0:T(2,128)S(1)} %broadcast_in_dim.31), channel_id=1, replica_groups={{0,2,4,6,8,10,12,14,16,18,20,22,24,26,28,30,32,34,36,38,40,42,44,46,48,..., dimensions={0} | all-to-all | bytes 131072 | tf_op jit(solution)/shard_map/all_to_all | solution.py:289
  29.1 5.7 %conv_first.1 = (f32[8,320,256]{2,1,0:T(8,128)S(1)}, f32[8,128]{1,0:T(8,128)S(1)}, bf16[1920,256]{1,0:T(8,128)(2,1)S(1)}, bf16[960,960]{1,0:T(8,128)(2,1)S(1)}, f32[640,128]{1,0:T(8,128)S(1)}) custom-call(f32[8,128]{1,0:T(8,128)S(1)} %iota.16.flags, bf16[8,320,256]{2,1,0:T(8,128)(2,1)S(1)} %bitcast.13, ...), custom_call_target="tpu_custom_call" | custom-call | flops 3774873600 | bytes 4194304 | tf_op jit(solution)/shard_map/conv_first/pallas_call | solution.py:300
  35.0 1.0 %prepare.1 = (bf16[960,960]{1,0:T(8,128)(2,1)S(1)}, bf16[320,320]{1,0:T(8,128)(2,1)S(1)}) custom-call(bf16[3,3,320,320]{3,2,1,0:T(8,128)(2,1)S(1)} %bitcast.24, bf16[320,320]{1,0:T(8,128)(2,1)S(1)} %copy-done.4, f32[8,128]{1,0:T(8,128)S(1)} %get-tuple-element.32.after), custom_call_target="tpu_custom_call" | custom-call | flops 1000000000 | bytes 4194304 | tf_op jit(solution)/shard_map/prepare/pallas_call | solution.py:315
  36.1 14.6 %all_to_all.11 = f32[64,2,128]{2,1,0:T(2,128)S(1)} all-to-all(f32[64,2,128]{2,1,0:T(2,128)S(1)} %broadcast_in_dim.32), channel_id=1, replica_groups={{0,2,4,6,8,10,12,14,16,18,20,22,24,26,28,30,32,34,36,38,40,42,44,46,48,..., dimensions={0} | all-to-all | bytes 131072 | tf_op jit(solution)/shard_map/all_to_all | solution.py:289
  50.7 1.9 %conv_second.4 = (f32[2,320,256]{2,1,0:T(8,128)S(1)}, bf16[2,320,256]{2,1,0:T(8,128)(2,1)S(1)}) custom-call(f32[8,128]{1,0:T(8,128)S(1)} %iota.16.flags, bf16[8,320,256]{2,1,0:T(8,128)(2,1)S(1)} %bitcast.14, f32[8,320,256]{2,1,0:T(8,128)S(1)} %get-tuple-element.31.mid, f32[128,128]{1,0:T(8,128)S(1)} %bitcast.18, f32[640,128]{1,0:T(8,128)S(1)} %get-tuple-element.36.cols, ...), custom_call_target="tpu_custom_call" | custom-call | flops 943718400 | bytes 4194304 | tf_op jit(solution)/shard_map/conv_second/pallas_call | solution.py:324
  52.6 0.7 collective-permute-start.7
  53.3 1.9 %conv_second.5 = (f32[2,320,256]{2,1,0:T(8,128)S(1)}, bf16[2,320,256]{2,1,0:T(8,128)(2,1)S(1)}) custom-call(f32[8,128]{1,0:T(8,128)S(1)} %iota.16.flags, bf16[8,320,256]{2,1,0:T(8,128)(2,1)S(1)} %bitcast.15, f32[8,320,256]{2,1,0:T(8,128)S(1)} %get-tuple-element.31.mid, f32[128,128]{1,0:T(8,128)S(1)} %bitcast.19, f32[640,128]{1,0:T(8,128)S(1)} %get-tuple-element.36.cols, ...), custom_call_target="tpu_custom_call" | custom-call | flops 943718400 | bytes 4194304 | tf_op jit(solution)/shard_map/conv_second/pallas_call | solution.py:324
  55.2 3.0 %collective-permute-start.6 = (bf16[2,320,256]{2,1,0:T(8,128)(2,1)S(1)}, bf16[2,320,256]{2,1,0:T(8,128)(2,1)S(1)}, u32[]{:S(2)}, u32[]{:S(2)}) collective-permute-start(bf16[2,320,256]{2,1,0:T(8,128)(2,1)S(1)} %get-tuple-element.42.after), channel_id=1, source_target_pairs={{0,128},{128,0},{1,129},{129,1},{2,130},{130,2},{3,131},{131,3},{4... | collective-permute-start | bytes 983048 | tf_op jit(solution)/shard_map/ppermute | solution.py:339
  58.1 1.9 %conv_second.6 = (f32[2,320,256]{2,1,0:T(8,128)S(1)}, bf16[2,320,256]{2,1,0:T(8,128)(2,1)S(1)}) custom-call(f32[8,128]{1,0:T(8,128)S(1)} %iota.16.flags, bf16[8,320,256]{2,1,0:T(8,128)(2,1)S(1)} %bitcast.16, f32[8,320,256]{2,1,0:T(8,128)S(1)} %get-tuple-element.31.mid, f32[128,128]{1,0:T(8,128)S(1)} %bitcast.20, f32[640,128]{1,0:T(8,128)S(1)} %get-tuple-element.36.cols, ...), custom_call_target="tpu_custom_call" | custom-call | flops 943718400 | bytes 4194304 | tf_op jit(solution)/shard_map/conv_second/pallas_call | solution.py:324
  60.0 0.7 collective-permute-start.5
  60.7 3.9 %conv_second.7 = (f32[2,320,256]{2,1,0:T(8,128)S(1)}, bf16[2,320,256]{2,1,0:T(8,128)(2,1)S(1)}) custom-call(f32[8,128]{1,0:T(8,128)S(1)} %iota.16.flags, bf16[8,320,256]{2,1,0:T(8,128)(2,1)S(1)} %bitcast.17, f32[8,320,256]{2,1,0:T(8,128)S(1)} %get-tuple-element.31.mid, f32[128,128]{1,0:T(8,128)S(1)} %bitcast.21, f32[640,128]{1,0:T(8,128)S(1)} %get-tuple-element.36.cols, ...), custom_call_target="tpu_custom_call" | custom-call | flops 943718400 | bytes 4194304 | tf_op jit(solution)/shard_map/conv_second/pallas_call | solution.py:324
  64.7 3.0 %collective-permute-start.4 = (bf16[2,320,256]{2,1,0:T(8,128)(2,1)S(1)}, bf16[2,320,256]{2,1,0:T(8,128)(2,1)S(1)}, u32[]{:S(2)}, u32[]{:S(2)}) collective-permute-start(bf16[2,320,256]{2,1,0:T(8,128)(2,1)S(1)} %get-tuple-element.45), channel_id=1, source_target_pairs={{0,128},{128,0},{1,129},{129,1},{2,130},{130,2},{3,131},{131,3},{4... | collective-permute-start | bytes 983048 | tf_op jit(solution)/shard_map/ppermute | solution.py:339
  67.6 0.8 mix.4.rest_0_
  68.5 3.4 %collective-permute-done.6.arrived = bf16[2,320,256]{2,1,0:T(8,128)(2,1)S(1)} collective-permute-done((bf16[2,320,256]{2,1,0:T(8,128)(2,1)S(1)}, bf16[2,320,256]{2,1,0:T(8,128)(2,1)S(1)}, u32[]{:S(2)}, u32[]{:S(2)}) %collective-permute-start.6) | collective-permute-done | bytes 327712 | tf_op jit(solution)/shard_map/ppermute | solution.py:339
  71.8 0.8 mix.5.rest_0_
  72.7 6.2 %collective-permute-done.5.arrived = bf16[2,320,256]{2,1,0:T(8,128)(2,1)S(1)} collective-permute-done((bf16[2,320,256]{2,1,0:T(8,128)(2,1)S(1)}, bf16[2,320,256]{2,1,0:T(8,128)(2,1)S(1)}, u32[]{:S(2)}, u32[]{:S(2)}) %collective-permute-start.5) | collective-permute-done | bytes 327712 | tf_op jit(solution)/shard_map/ppermute | solution.py:339
  78.9 0.8 mix.6.rest_0_
  79.7 4.4 %collective-permute-done.4.arrived = bf16[2,320,256]{2,1,0:T(8,128)(2,1)S(1)} collective-permute-done((bf16[2,320,256]{2,1,0:T(8,128)(2,1)S(1)}, bf16[2,320,256]{2,1,0:T(8,128)(2,1)S(1)}, u32[]{:S(2)}, u32[]{:S(2)}) %collective-permute-start.4) | collective-permute-done | bytes 327712 | tf_op jit(solution)/shard_map/ppermute | solution.py:339
  84.1 0.8 mix.7
  (28 shorter events, 0.6 us)
Async XLA Ops:
  0.1 1.3 %copy-start = (bf16[1,8,256,320]{2,3,1,0:T(8,128)(2,1)S(1)}, bf16[1,8,256,320]{2,3,1,0:T(8,128)(2,1)}, u32[]{:S(2)}) copy-start(bf16[1,8,256,320]{2,3,1,0:T(8,128)(2,1)} %param.6) | copy-start | bytes 3932164
  1.4 27.7 %copy-start.1 = (bf16[1,8,256,320]{2,3,1,0:T(8,128)(2,1)S(1)}, bf16[1,8,256,320]{2,3,1,0:T(8,128)(2,1)}, u32[]{:S(2)}) copy-start(bf16[1,8,256,320]{2,3,1,0:T(8,128)(2,1)} %param.6) | copy-start | bytes 3932164
  1.4 27.7 %copy-start.2 = (bf16[1,3,3,320,320]{4,3,2,1,0:T(8,128)(2,1)S(1)}, bf16[1,3,3,320,320]{4,3,2,1,0:T(8,128)(2,1)}, u32[]{:S(2)}) copy-start(bf16[1,3,3,320,320]{4,3,2,1,0:T(8,128)(2,1)} %param.7) | copy-start | bytes 5529604
  1.4 27.7 %copy-start.5 = (f32[1,2,320]{2,1,0:T(2,128)S(1)}, f32[1,2,320]{2,1,0:T(2,128)}, u32[]{:S(2)}) copy-start(f32[1,2,320]{2,1,0:T(2,128)} %param.10) | copy-start | bytes 7684
  1.4 27.7 %copy-start.6 = (f32[1,320]{1,0:T(1,128)S(1)}, f32[1,320]{1,0:T(1,128)}, u32[]{:S(2)}) copy-start(f32[1,320]{1,0:T(1,128)} %shift.1) | copy-start | bytes 3844
  2.2 1.2 %collective-permute-start = (f32[1,128]{1,0:T(1,128)S(1)}, f32[1,128]{1,0:T(1,128)S(1)}, u32[]{:S(2)}, u32[]{:S(2)}) collective-permute-start(f32[1,128]{1,0:T(1,128)S(1)} %slice.8), channel_id=1, source_target_pairs={{0,1},{1,0},{2,3},{3,2},{4,5},{5,4},{6,7},{7,6},{8,9},{9,8},{10,11... | collective-permute-start | bytes 1544 | tf_op jit(solution)/shard_map/ppermute | solution.py:285
  2.5 26.6 %collective-permute-start.2 = (bf16[2,320,256]{2,1,0:T(8,128)(2,1)S(1)}, bf16[2,320,256]{2,1,0:T(8,128)(2,1)S(1)}, u32[]{:S(2)}, u32[]{:S(2)}) collective-permute-start(bf16[2,320,256]{2,1,0:T(8,128)(2,1)S(1)} %get-tuple-element.29), channel_id=1, source_target_pairs={{1,2},{3,4},{5,6},{7,8},{9,10},{11,12},{13,14},{15,16},{17,18},{19... | collective-permute-start | bytes 983048 | tf_op jit(solution)/shard_map/ppermute | solution.py:297
  3.4 25.7 %collective-permute-start.1 = (bf16[2,320,256]{2,1,0:T(8,128)(2,1)S(1)}, bf16[2,320,256]{2,1,0:T(8,128)(2,1)S(1)}, u32[]{:S(2)}, u32[]{:S(2)}) collective-permute-start(bf16[2,320,256]{2,1,0:T(8,128)(2,1)S(1)} %get-tuple-element.28), channel_id=1, source_target_pairs={{0,1},{1,0},{2,3},{3,2},{4,5},{5,4},{6,7},{7,6},{8,9},{9,8},{10,11... | collective-permute-start | bytes 983048 | tf_op jit(solution)/shard_map/ppermute | solution.py:298
  29.1 5.8 %copy-start.3 = (bf16[1,3,3,320,320]{4,3,2,1,0:T(8,128)(2,1)S(1)}, bf16[1,3,3,320,320]{4,3,2,1,0:T(8,128)(2,1)}, u32[]{:S(2)}) copy-start(bf16[1,3,3,320,320]{4,3,2,1,0:T(8,128)(2,1)} %param.8) | copy-start | bytes 5529604
  29.1 5.8 %copy-start.4 = (bf16[320,320]{1,0:T(8,128)(2,1)S(1)}, bf16[320,320]{1,0:T(8,128)(2,1)}, u32[]{:S(2)}) copy-start(bf16[320,320]{1,0:T(8,128)(2,1)} %z.1) | copy-start | bytes 614404
  34.9 1.2 %collective-permute-start.3 = (f32[1,128]{1,0:T(1,128)S(1)}, f32[1,128]{1,0:T(1,128)S(1)}, u32[]{:S(2)}, u32[]{:S(2)}) collective-permute-start(f32[1,128]{1,0:T(1,128)S(1)} %slice.9), channel_id=1, source_target_pairs={{0,1},{1,0},{2,3},{3,2},{4,5},{5,4},{6,7},{7,6},{8,9},{9,8},{10,11... | collective-permute-start | bytes 1544 | tf_op jit(solution)/shard_map/ppermute | solution.py:285
  52.6 15.1 %collective-permute-start.7 = (bf16[2,320,256]{2,1,0:T(8,128)(2,1)S(1)}, bf16[2,320,256]{2,1,0:T(8,128)(2,1)S(1)}, u32[]{:S(2)}, u32[]{:S(2)}) collective-permute-start(bf16[2,320,256]{2,1,0:T(8,128)(2,1)S(1)} %get-tuple-element.41.after), channel_id=1, source_target_pairs={{0,128},{128,0},{1,129},{129,1},{2,130},{130,2},{3,131},{131,3},{4... | collective-permute-start | bytes 983048 | tf_op jit(solution)/shard_map/ppermute | solution.py:339
  55.2 16.7 %collective-permute-start.6 = (bf16[2,320,256]{2,1,0:T(8,128)(2,1)S(1)}, bf16[2,320,256]{2,1,0:T(8,128)(2,1)S(1)}, u32[]{:S(2)}, u32[]{:S(2)}) collective-permute-start(bf16[2,320,256]{2,1,0:T(8,128)(2,1)S(1)} %get-tuple-element.42.after), channel_id=1, source_target_pairs={{0,128},{128,0},{1,129},{129,1},{2,130},{130,2},{3,131},{131,3},{4... | collective-permute-start | bytes 983048 | tf_op jit(solution)/shard_map/ppermute | solution.py:339
  60.0 18.9 %collective-permute-start.5 = (bf16[2,320,256]{2,1,0:T(8,128)(2,1)S(1)}, bf16[2,320,256]{2,1,0:T(8,128)(2,1)S(1)}, u32[]{:S(2)}, u32[]{:S(2)}) collective-permute-start(bf16[2,320,256]{2,1,0:T(8,128)(2,1)S(1)} %get-tuple-element.43.after), channel_id=1, source_target_pairs={{0,128},{128,0},{1,129},{129,1},{2,130},{130,2},{3,131},{131,3},{4... | collective-permute-start | bytes 983048 | tf_op jit(solution)/shard_map/ppermute | solution.py:339
  64.7 19.4 %collective-permute-start.4 = (bf16[2,320,256]{2,1,0:T(8,128)(2,1)S(1)}, bf16[2,320,256]{2,1,0:T(8,128)(2,1)S(1)}, u32[]{:S(2)}, u32[]{:S(2)}) collective-permute-start(bf16[2,320,256]{2,1,0:T(8,128)(2,1)S(1)} %get-tuple-element.45), channel_id=1, source_target_pairs={{0,128},{128,0},{1,129},{129,1},{2,130},{130,2},{3,131},{131,3},{4... | collective-permute-start | bytes 983048 | tf_op jit(solution)/shard_map/ppermute | solution.py:339

commit v8 on v7

--- a/solution.py
+++ b/solution.py
@@ -121,33 +121,35 @@
     )
 
 
+def first_row(flags, x, inner, outer, mean, scale, at):
+    rows = x.shape[0]
+    even = flags[3:4, :1] > 0.5
+    keep = None
+    if at < 2:
+        v = jnp.where(even, outer[at].astype(F32), inner[at].astype(F32))
+        keep = flags[0:1, :1]
+    elif at < rows + 2:
+        v = x[at - 2].astype(F32)
+    else:
+        at_high = at - rows - 2
+        v = jnp.where(even, inner[at_high].astype(F32), outer[at_high].astype(F32))
+        keep = flags[1:2, :1]
+    a = silu_of_twice((v - mean) * scale)
+    if keep is not None:
+        a = a * keep
+    return a.astype(BF16)
+
+
 def first_kernel(
-    flags, x, inner, outer, st, gains, shift, w1, mid, out, edges, w1t, cols, acts
+    flags, x, inner, outer, st, gains, shift, w1, mid, out, w1t, cols, acts
 ):
     rows, c, width = x.shape
     mean, scale = whole_stats(st[...], c, rows * width * (c // G))
     scale = 0.5 * scale * column(gains[0:1, :])
     top, bottom = flags[0:1, :1], flags[1:2, :1]
-    even = flags[3:4, :1] > 0.5
 
     def put(at):
-        if at < 2:
-            v, keep = jnp.where(even, outer[at].astype(F32), inner[at].astype(F32)), top
-        elif at < rows + 2:
-            v, keep = x[at - 2].astype(F32), None
-        else:
-            at_high = at - rows - 2
-            v = jnp.where(even, inner[at_high].astype(F32), outer[at_high].astype(F32))
-            keep = bottom
-        a = silu_of_twice((v - mean) * scale)
-        if keep is not None:
-            a = a * keep
-        a = a.astype(BF16)
-        acts[at * c : (at + 1) * c, :] = a
-        if at < 3:
-            edges[at * c : (at + 1) * c, :] = a
-        if at > rows:
-            edges[(at - rows + 2) * c : (at - rows + 3) * c, :] = a
+        acts[at * c : (at + 1) * c, :] = first_row(flags, x, inner, outer, mean, scale, at)
 
     for kx in range(3):
         turned(w1, w1t, kx)
@@ -161,7 +163,7 @@
         both = jnp.concatenate([shift_c, column(gains[1:2, :])], axis=0)
         cols[...] = jnp.broadcast_to(both, cols.shape)
 
-    beside = {1: keep_columns, 4: lambda: put(0), 6: lambda: put(rows + 3)}
+    beside = {1: keep_columns}
     for r in range(1, rows + 1):
         y = conv_row(w1t[...], acts[r * c : (r + 3) * c, :]) + shift_c
         mid[r - 1] = y
@@ -194,18 +196,29 @@
     zt[...] = z[...].T
 
 
-def second_kernel(wanted, flags, x, mid, st, cols, w2t, zt, edges, w1t, after, *outs):
-    block, residual, acts, control = outs
+def second_kernel(
+    wanted, flags, x, mid, st, cols, w2t, zt, inner, outer, st1, gains, w1t, after, *outs
+):
+    block, residual, acts, control, edges = outs
     rows, c, width = x.shape
     mean, scale = whole_stats(st[...], c, rows * width * (c // G))
     scale = scale * widened(0.5 * cols[c:, :], width)
     top, bottom = flags[0:1, :1], flags[1:2, :1]
 
+    if any(begin == 0 or end == rows for begin, end in wanted):
+        mean_one, scale_one = whole_stats(st1[...], c, rows * width * (c // G))
+        scale_one = 0.5 * scale_one * column(gains[0:1, :])
+
+    def edge_row(begin):
+        for i in range(3):
+            edges[i * c : (i + 1) * c, :] = first_row(
+                flags, x, inner, outer, mean_one, scale_one, begin + i
+            )
+        return conv_row(w1t[...], edges[...]) + widened(cols[:c, :], width)
+
     def put(at, slot):
-        if at == 0:
-            v = conv_row(w1t[...], edges[: 3 * c, :]) + widened(cols[:c, :], width)
-        elif at == rows + 1:
-            v = conv_row(w1t[...], edges[3 * c :, :]) + widened(cols[:c, :], width)
+        if at == 0 or at == rows + 1:
+            v = edge_row(at)
         else:
             v = mid[at - 1]
         a = silu_of_twice((v - mean) * scale)
@@ -297,14 +310,13 @@
     outer = lax.ppermute(outer, "strip", next_chip)
     inner = lax.ppermute(inner, "strip", same_chip)
     st1 = spread(pair)
-    mid, st2, edges, w1t, cols = call(
+    mid, st2, w1t, cols = call(
         first_kernel,
         "conv_first",
         8,
         (
             shaped((rows, c, width), F32),
             stat,
-            shaped((6 * c, width), BF16),
             wide,
             shaped((2 * c, LANES), F32),
         ),
@@ -324,16 +336,17 @@
         block, residual = call(
             functools.partial(second_kernel, wanted),
             "conv_second",
-            9,
+            12,
             (shaped((n, c, width), F32), shaped((n, c, width), BF16)),
             [
                 pltpu.VMEM(((n + 2 * len(wanted)) * c, width), BF16),
                 pltpu.VMEM((n * c, width), BF16),
+                pltpu.VMEM((3 * c, width), BF16),
             ],
             32,
             n * row_macs,
             unread=1,
-        )(flags, x, mid, st2, cols, w2t, zt, edges, w1t, after)
+        )(flags, x, mid, st2, cols, w2t, zt, inner, outer, st1, norm_gains[0], w1t, after)
         after = residual
         listed = [r for begin, end in wanted for r in range(begin, end)]
         pieces.append((listed, block, lax.ppermute(residual, "branch", [(0, 1), (1, 0)])))

time: 85.3 us -> 85.3 us (level)
  transfers between devices with their start and end apart: 8 -> 8, of which waited for: 5 -> 5; matrix products, arithmetic and copies ran while one was open for 0% -> 0% of each run, Pallas kernels for 13% -> 14%
where the time goes in v8:
time: 85.3 us; the launch traced here: 85.1 us
  blocking collectives  37.6 us (44%)
  Pallas kernels  20.6 us (24%)
  waiting for transfers between devices  14 us (16%)
  starting transfers between devices  11.2 us (13%)
  local copies, waits for them, and re-layouts  1.47 us (2%)
    all_to_all x2, blocking collectives, spread(): rows_of_all = lax.all_to_all(sent, 'strip', 0, 0, axis_index_groups=chips)  37.6 us
    ppermute x4, waiting for transfers between devices, on_device(): lax.ppermute(residual, 'branch', [(0, 1), (1, 0)])  13.7 us
    pallas_call x4, Pallas kernels, on_device(): call(functools.partial(second_kernel, wanted), 'conv_second', 12, (shaped...  9.68 us
    ppermute x4, starting transfers between devices, on_device(): lax.ppermute(residual, 'branch', [(0, 1), (1, 0)])  7.59 us
    pallas_call x1, Pallas kernels, on_device(): call(first_kernel, 'conv_first', 8, (shaped((rows, c, width), F32), stat,...  5.54 us
    pallas_call x4, Pallas kernels, mix(): pl.pallas_call(functools.partial(mix_kernel, wanted), out_shape=whole, in...  3.36 us
    ppermute x1, starting transfers between devices, on_device(): inner = lax.ppermute(inner, 'strip', same_chip)  2.75 us
  transfers between devices with their start and end apart: 8, of which 5 were waited for; matrix products, arithmetic and copies ran while one was open for 0% of the time, Pallas kernels for 14%

profile of v8, /device:TPU:16, one launch (start us, length us, event | category | flops | bytes accessed | tf_op | source)
XLA Modules:
  0.0 85.1 jit_solution(15770894531150940572)
XLA Ops:
  0.1 1.3 %copy-done = bf16[1,8,256,320]{2,3,1,0:T(8,128)(2,1)S(1)} copy-done((bf16[1,8,256,320]{2,3,1,0:T(8,128)(2,1)S(1)}, bf16[1,8,256,320]{2,3,1,0:T(8,128)(2,1)}, u32[]{:S(2)}) %copy-start) | copy-done | bytes 1310744
  1.4 0.8 stats_first.1.after
  2.3 0.2 halo.1
  2.5 0.7 collective-permute-start.2
  3.4 2.7 %collective-permute-start.1 = (bf16[2,320,256]{2,1,0:T(8,128)(2,1)S(1)}, bf16[2,320,256]{2,1,0:T(8,128)(2,1)S(1)}, u32[]{:S(2)}, u32[]{:S(2)}) collective-permute-start(bf16[2,320,256]{2,1,0:T(8,128)(2,1)S(1)} %get-tuple-element.27), channel_id=1, source_target_pairs={{0,1},{1,0},{2,3},{3,2},{4,5},{5,4},{6,7},{7,6},{8,9},{9,8},{10,11... | collective-permute-start | bytes 983048 | tf_op jit(solution)/shard_map/ppermute | solution.py:311
  6.1 22.9 %all_to_all.10 = f32[64,2,128]{2,1,0:T(2,128)S(1)} all-to-all(f32[64,2,128]{2,1,0:T(2,128)S(1)} %broadcast_in_dim.31), channel_id=1, replica_groups={{0,2,4,6,8,10,12,14,16,18,20,22,24,26,28,30,32,34,36,38,40,42,44,46,48,..., dimensions={0} | all-to-all | bytes 131072 | tf_op jit(solution)/shard_map/all_to_all | solution.py:302
  29.1 5.5 %conv_first.1 = (f32[8,320,256]{2,1,0:T(8,128)S(1)}, f32[8,128]{1,0:T(8,128)S(1)}, bf16[960,960]{1,0:T(8,128)(2,1)S(1)}, f32[640,128]{1,0:T(8,128)S(1)}) custom-call(f32[8,128]{1,0:T(8,128)S(1)} %iota.16.flags, bf16[8,320,256]{2,1,0:T(8,128)(2,1)S(1)} %bitcast.13, bf16[2,320,256]{2,1,0:T(8,128)(2,1)S(1)} %collective-permute-done.1.inner, ...), custom_call_target="tpu_custom_call" | custom-call | flops 3774873600 | bytes 4194304 | tf_op jit(solution)/shard_map/conv_first/pallas_call | solution.py:313
  34.8 1.0 %prepare.1 = (bf16[960,960]{1,0:T(8,128)(2,1)S(1)}, bf16[320,320]{1,0:T(8,128)(2,1)S(1)}) custom-call(bf16[3,3,320,320]{3,2,1,0:T(8,128)(2,1)S(1)} %bitcast.33, bf16[320,320]{1,0:T(8,128)(2,1)S(1)} %copy-done.5, f32[8,128]{1,0:T(8,128)S(1)} %get-tuple-element.31.after), custom_call_target="tpu_custom_call" | custom-call | flops 1000000000 | bytes 4194304 | tf_op jit(solution)/shard_map/prepare/pallas_call | solution.py:327
  35.9 14.6 %all_to_all.11 = f32[64,2,128]{2,1,0:T(2,128)S(1)} all-to-all(f32[64,2,128]{2,1,0:T(2,128)S(1)} %broadcast_in_dim.32), channel_id=1, replica_groups={{0,2,4,6,8,10,12,14,16,18,20,22,24,26,28,30,32,34,36,38,40,42,44,46,48,..., dimensions={0} | all-to-all | bytes 131072 | tf_op jit(solution)/shard_map/all_to_all | solution.py:302
  50.5 1.9 %conv_second.4 = (f32[2,320,256]{2,1,0:T(8,128)S(1)}, bf16[2,320,256]{2,1,0:T(8,128)(2,1)S(1)}) custom-call(f32[8,128]{1,0:T(8,128)S(1)} %iota.16.flags, bf16[8,320,256]{2,1,0:T(8,128)(2,1)S(1)} %bitcast.14, f32[8,320,256]{2,1,0:T(8,128)S(1)} %get-tuple-element.30.mid, f32[128,128]{1,0:T(8,128)S(1)} %bitcast.23, f32[640,128]{1,0:T(8,128)S(1)} %get-tuple-element.35.cols, ...), custom_call_target="tpu_custom_call" | custom-call | flops 943718400 | bytes 4194304 | tf_op jit(solution)/shard_map/conv_second/pallas_call | solution.py:336
  52.4 0.9 %collective-permute-start.7 = (bf16[2,320,256]{2,1,0:T(8,128)(2,1)S(1)}, bf16[2,320,256]{2,1,0:T(8,128)(2,1)S(1)}, u32[]{:S(2)}, u32[]{:S(2)}) collective-permute-start(bf16[2,320,256]{2,1,0:T(8,128)(2,1)S(1)} %get-tuple-element.39.after), channel_id=1, source_target_pairs={{0,128},{128,0},{1,129},{129,1},{2,130},{130,2},{3,131},{131,3},{4... | collective-permute-start | bytes 983048 | tf_op jit(solution)/shard_map/ppermute | solution.py:352
  53.3 1.9 %conv_second.5 = (f32[2,320,256]{2,1,0:T(8,128)S(1)}, bf16[2,320,256]{2,1,0:T(8,128)(2,1)S(1)}) custom-call(f32[8,128]{1,0:T(8,128)S(1)} %iota.16.flags, bf16[8,320,256]{2,1,0:T(8,128)(2,1)S(1)} %bitcast.15, f32[8,320,256]{2,1,0:T(8,128)S(1)} %get-tuple-element.30.mid, f32[128,128]{1,0:T(8,128)S(1)} %bitcast.24, f32[640,128]{1,0:T(8,128)S(1)} %get-tuple-element.35.cols, ...), custom_call_target="tpu_custom_call" | custom-call | flops 943718400 | bytes 4194304 | tf_op jit(solution)/shard_map/conv_second/pallas_call | solution.py:336
  55.1 3.0 %collective-permute-start.6 = (bf16[2,320,256]{2,1,0:T(8,128)(2,1)S(1)}, bf16[2,320,256]{2,1,0:T(8,128)(2,1)S(1)}, u32[]{:S(2)}, u32[]{:S(2)}) collective-permute-start(bf16[2,320,256]{2,1,0:T(8,128)(2,1)S(1)} %get-tuple-element.40.after), channel_id=1, source_target_pairs={{0,128},{128,0},{1,129},{129,1},{2,130},{130,2},{3,131},{131,3},{4... | collective-permute-start | bytes 983048 | tf_op jit(solution)/shard_map/ppermute | solution.py:352
  58.1 1.9 %conv_second.6 = (f32[2,320,256]{2,1,0:T(8,128)S(1)}, bf16[2,320,256]{2,1,0:T(8,128)(2,1)S(1)}) custom-call(f32[8,128]{1,0:T(8,128)S(1)} %iota.16.flags, bf16[8,320,256]{2,1,0:T(8,128)(2,1)S(1)} %bitcast.16, f32[8,320,256]{2,1,0:T(8,128)S(1)} %get-tuple-element.30.mid, f32[128,128]{1,0:T(8,128)S(1)} %bitcast.25, f32[640,128]{1,0:T(8,128)S(1)} %get-tuple-element.35.cols, ...), custom_call_target="tpu_custom_call" | custom-call | flops 943718400 | bytes 4194304 | tf_op jit(solution)/shard_map/conv_second/pallas_call | solution.py:336
  60.0 0.7 collective-permute-start.5
  60.7 4.1 %conv_second.7 = (f32[2,320,256]{2,1,0:T(8,128)S(1)}, bf16[2,320,256]{2,1,0:T(8,128)(2,1)S(1)}) custom-call(f32[8,128]{1,0:T(8,128)S(1)} %iota.16.flags, bf16[8,320,256]{2,1,0:T(8,128)(2,1)S(1)} %bitcast.17, f32[8,320,256]{2,1,0:T(8,128)S(1)} %get-tuple-element.30.mid, f32[128,128]{1,0:T(8,128)S(1)} %bitcast.26, f32[640,128]{1,0:T(8,128)S(1)} %get-tuple-element.35.cols, ...), custom_call_target="tpu_custom_call" | custom-call | flops 943718400 | bytes 4194304 | tf_op jit(solution)/shard_map/conv_second/pallas_call | solution.py:336
  64.8 3.0 %collective-permute-start.4 = (bf16[2,320,256]{2,1,0:T(8,128)(2,1)S(1)}, bf16[2,320,256]{2,1,0:T(8,128)(2,1)S(1)}, u32[]{:S(2)}, u32[]{:S(2)}) collective-permute-start(bf16[2,320,256]{2,1,0:T(8,128)(2,1)S(1)} %get-tuple-element.43), channel_id=1, source_target_pairs={{0,128},{128,0},{1,129},{129,1},{2,130},{130,2},{3,131},{131,3},{4... | collective-permute-start | bytes 983048 | tf_op jit(solution)/shard_map/ppermute | solution.py:352
  67.8 0.8 mix.4.rest_0_
  68.7 3.2 %collective-permute-done.6.arrived = bf16[2,320,256]{2,1,0:T(8,128)(2,1)S(1)} collective-permute-done((bf16[2,320,256]{2,1,0:T(8,128)(2,1)S(1)}, bf16[2,320,256]{2,1,0:T(8,128)(2,1)S(1)}, u32[]{:S(2)}, u32[]{:S(2)}) %collective-permute-start.6) | collective-permute-done | bytes 327712 | tf_op jit(solution)/shard_map/ppermute | solution.py:352
  71.8 0.8 mix.5.rest_0_
  72.7 6.2 %collective-permute-done.5.arrived = bf16[2,320,256]{2,1,0:T(8,128)(2,1)S(1)} collective-permute-done((bf16[2,320,256]{2,1,0:T(8,128)(2,1)S(1)}, bf16[2,320,256]{2,1,0:T(8,128)(2,1)S(1)}, u32[]{:S(2)}, u32[]{:S(2)}) %collective-permute-start.5) | collective-permute-done | bytes 327712 | tf_op jit(solution)/shard_map/ppermute | solution.py:352
  78.9 0.8 mix.6.rest_0_
  79.7 4.3 %collective-permute-done.4.arrived = bf16[2,320,256]{2,1,0:T(8,128)(2,1)S(1)} collective-permute-done((bf16[2,320,256]{2,1,0:T(8,128)(2,1)S(1)}, bf16[2,320,256]{2,1,0:T(8,128)(2,1)S(1)}, u32[]{:S(2)}, u32[]{:S(2)}) %collective-permute-start.4) | collective-permute-done | bytes 327712 | tf_op jit(solution)/shard_map/ppermute | solution.py:352
  84.1 0.8 mix.7
  (28 shorter events, 0.6 us)
Async XLA Ops:
  0.1 1.3 %copy-start = (bf16[1,8,256,320]{2,3,1,0:T(8,128)(2,1)S(1)}, bf16[1,8,256,320]{2,3,1,0:T(8,128)(2,1)}, u32[]{:S(2)}) copy-start(bf16[1,8,256,320]{2,3,1,0:T(8,128)(2,1)} %param.6) | copy-start | bytes 3932164
  1.4 27.7 %copy-start.1 = (bf16[1,8,256,320]{2,3,1,0:T(8,128)(2,1)S(1)}, bf16[1,8,256,320]{2,3,1,0:T(8,128)(2,1)}, u32[]{:S(2)}) copy-start(bf16[1,8,256,320]{2,3,1,0:T(8,128)(2,1)} %param.6) | copy-start | bytes 3932164
  1.4 27.7 %copy-start.2 = (f32[1,2,320]{2,1,0:T(2,128)S(1)}, f32[1,2,320]{2,1,0:T(2,128)}, u32[]{:S(2)}) copy-start(f32[1,2,320]{2,1,0:T(2,128)} %param.10) | copy-start | bytes 7684
  1.4 27.7 %copy-start.3 = (bf16[1,3,3,320,320]{4,3,2,1,0:T(8,128)(2,1)S(1)}, bf16[1,3,3,320,320]{4,3,2,1,0:T(8,128)(2,1)}, u32[]{:S(2)}) copy-start(bf16[1,3,3,320,320]{4,3,2,1,0:T(8,128)(2,1)} %param.7) | copy-start | bytes 5529604
  1.4 27.7 %copy-start.6 = (f32[1,320]{1,0:T(1,128)S(1)}, f32[1,320]{1,0:T(1,128)}, u32[]{:S(2)}) copy-start(f32[1,320]{1,0:T(1,128)} %shift.1) | copy-start | bytes 3844
  2.2 1.2 %collective-permute-start = (f32[1,128]{1,0:T(1,128)S(1)}, f32[1,128]{1,0:T(1,128)S(1)}, u32[]{:S(2)}, u32[]{:S(2)}) collective-permute-start(f32[1,128]{1,0:T(1,128)S(1)} %slice.8), channel_id=1, source_target_pairs={{0,1},{1,0},{2,3},{3,2},{4,5},{5,4},{6,7},{7,6},{8,9},{9,8},{10,11... | collective-permute-start | bytes 1544 | tf_op jit(solution)/shard_map/ppermute | solution.py:298
  2.5 26.6 %collective-permute-start.2 = (bf16[2,320,256]{2,1,0:T(8,128)(2,1)S(1)}, bf16[2,320,256]{2,1,0:T(8,128)(2,1)S(1)}, u32[]{:S(2)}, u32[]{:S(2)}) collective-permute-start(bf16[2,320,256]{2,1,0:T(8,128)(2,1)S(1)} %get-tuple-element.28), channel_id=1, source_target_pairs={{1,2},{3,4},{5,6},{7,8},{9,10},{11,12},{13,14},{15,16},{17,18},{19... | collective-permute-start | bytes 983048 | tf_op jit(solution)/shard_map/ppermute | solution.py:310
  3.4 25.7 %collective-permute-start.1 = (bf16[2,320,256]{2,1,0:T(8,128)(2,1)S(1)}, bf16[2,320,256]{2,1,0:T(8,128)(2,1)S(1)}, u32[]{:S(2)}, u32[]{:S(2)}) collective-permute-start(bf16[2,320,256]{2,1,0:T(8,128)(2,1)S(1)} %get-tuple-element.27), channel_id=1, source_target_pairs={{0,1},{1,0},{2,3},{3,2},{4,5},{5,4},{6,7},{7,6},{8,9},{9,8},{10,11... | collective-permute-start | bytes 983048 | tf_op jit(solution)/shard_map/ppermute | solution.py:311
  29.1 5.6 %copy-start.4 = (bf16[1,3,3,320,320]{4,3,2,1,0:T(8,128)(2,1)S(1)}, bf16[1,3,3,320,320]{4,3,2,1,0:T(8,128)(2,1)}, u32[]{:S(2)}) copy-start(bf16[1,3,3,320,320]{4,3,2,1,0:T(8,128)(2,1)} %param.8) | copy-start | bytes 5529604
  29.1 5.6 %copy-start.5 = (bf16[320,320]{1,0:T(8,128)(2,1)S(1)}, bf16[320,320]{1,0:T(8,128)(2,1)}, u32[]{:S(2)}) copy-start(bf16[320,320]{1,0:T(8,128)(2,1)} %z.1) | copy-start | bytes 614404
  34.7 1.2 %collective-permute-start.3 = (f32[1,128]{1,0:T(1,128)S(1)}, f32[1,128]{1,0:T(1,128)S(1)}, u32[]{:S(2)}, u32[]{:S(2)}) collective-permute-start(f32[1,128]{1,0:T(1,128)S(1)} %slice.9), channel_id=1, source_target_pairs={{0,1},{1,0},{2,3},{3,2},{4,5},{5,4},{6,7},{7,6},{8,9},{9,8},{10,11... | collective-permute-start | bytes 1544 | tf_op jit(solution)/shard_map/ppermute | solution.py:298
  52.4 15.4 %collective-permute-start.7 = (bf16[2,320,256]{2,1,0:T(8,128)(2,1)S(1)}, bf16[2,320,256]{2,1,0:T(8,128)(2,1)S(1)}, u32[]{:S(2)}, u32[]{:S(2)}) collective-permute-start(bf16[2,320,256]{2,1,0:T(8,128)(2,1)S(1)} %get-tuple-element.39.after), channel_id=1, source_target_pairs={{0,128},{128,0},{1,129},{129,1},{2,130},{130,2},{3,131},{131,3},{4... | collective-permute-start | bytes 983048 | tf_op jit(solution)/shard_map/ppermute | solution.py:352
  55.1 16.7 %collective-permute-start.6 = (bf16[2,320,256]{2,1,0:T(8,128)(2,1)S(1)}, bf16[2,320,256]{2,1,0:T(8,128)(2,1)S(1)}, u32[]{:S(2)}, u32[]{:S(2)}) collective-permute-start(bf16[2,320,256]{2,1,0:T(8,128)(2,1)S(1)} %get-tuple-element.40.after), channel_id=1, source_target_pairs={{0,128},{128,0},{1,129},{129,1},{2,130},{130,2},{3,131},{131,3},{4... | collective-permute-start | bytes 983048 | tf_op jit(solution)/shard_map/ppermute | solution.py:352
  60.0 18.9 %collective-permute-start.5 = (bf16[2,320,256]{2,1,0:T(8,128)(2,1)S(1)}, bf16[2,320,256]{2,1,0:T(8,128)(2,1)S(1)}, u32[]{:S(2)}, u32[]{:S(2)}) collective-permute-start(bf16[2,320,256]{2,1,0:T(8,128)(2,1)S(1)} %get-tuple-element.41.after), channel_id=1, source_target_pairs={{0,128},{128,0},{1,129},{129,1},{2,130},{130,2},{3,131},{131,3},{4... | collective-permute-start | bytes 983048 | tf_op jit(solution)/shard_map/ppermute | solution.py:352
  64.8 19.2 %collective-permute-start.4 = (bf16[2,320,256]{2,1,0:T(8,128)(2,1)S(1)}, bf16[2,320,256]{2,1,0:T(8,128)(2,1)S(1)}, u32[]{:S(2)}, u32[]{:S(2)}) collective-permute-start(bf16[2,320,256]{2,1,0:T(8,128)(2,1)S(1)} %get-tuple-element.43), channel_id=1, source_target_pairs={{0,128},{128,0},{1,129},{129,1},{2,130},{130,2},{3,131},{131,3},{4... | collective-permute-start | bytes 983048 | tf_op jit(solution)/shard_map/ppermute | solution.py:352

commit v9 on v8

--- a/solution.py
+++ b/solution.py
@@ -349,7 +349,8 @@
         )(flags, x, mid, st2, cols, w2t, zt, inner, outer, st1, norm_gains[0], w1t, after)
         after = residual
         listed = [r for begin, end in wanted for r in range(begin, end)]
-        pieces.append((listed, block, lax.ppermute(residual, "branch", [(0, 1), (1, 0)])))
+        route = [(0, 1)] if pieces else [(0, 1), (1, 0)]
+        pieces.append((listed, block, lax.ppermute(residual, "branch", route)))
     whole = shaped((rows, c, width), BF16)
     out = None
     for listed, block, arrived in pieces:

time: 85.3 us -> 85.3 us (level)
  starting transfers between devices: 11.2 us -> 8.34 us
  waiting for transfers between devices: 14 us -> 16.7 us
    ppermute x4, starting transfers between devices: 7.59 us -> 4.77 us  [on_device(): pieces.append((listed, block, lax.ppermute(residual, 'branch', route)))]
    ppermute x4, waiting for transfers between devices: 13.7 us -> 16.5 us  [on_device(): pieces.append((listed, block, lax.ppermute(residual, 'branch', route)))]
where the time goes in v9:
time: 85.3 us; the launch traced here: 85.1 us
  blocking collectives  37.6 us (44%)
  Pallas kernels  20.6 us (24%)
  waiting for transfers between devices  16.7 us (20%)
  starting transfers between devices  8.34 us (10%)
  local copies, waits for them, and re-layouts  1.47 us (2%)
    all_to_all x2, blocking collectives, spread(): rows_of_all = lax.all_to_all(sent, 'strip', 0, 0, axis_index_groups=chips)  37.6 us
    ppermute x4, waiting for transfers between devices, on_device(): pieces.append((listed, block, lax.ppermute(residual, 'branch', route)))  16.5 us
    pallas_call x4, Pallas kernels, on_device(): call(functools.partial(second_kernel, wanted), 'conv_second', 12, (shaped...  9.69 us
    pallas_call x1, Pallas kernels, on_device(): call(first_kernel, 'conv_first', 8, (shaped((rows, c, width), F32), stat,...  5.54 us
    ppermute x4, starting transfers between devices, on_device(): pieces.append((listed, block, lax.ppermute(residual, 'branch', route)))  4.77 us
    pallas_call x4, Pallas kernels, mix(): pl.pallas_call(functools.partial(mix_kernel, wanted), out_shape=whole, in...  3.36 us
    ppermute x1, starting transfers between devices, on_device(): inner = lax.ppermute(inner, 'strip', same_chip)  2.75 us
  transfers between devices with their start and end apart: 8, of which 5 were waited for; matrix products, arithmetic and copies ran while one was open for 0% of the time, Pallas kernels for 14%

profile of v9, /device:TPU:16, one launch (start us, length us, event | category | flops | bytes accessed | tf_op | source)
XLA Modules:
  0.0 85.1 jit_solution(10907519037220800779)
XLA Ops:
  0.1 1.3 %copy-done = bf16[1,8,256,320]{2,3,1,0:T(8,128)(2,1)S(1)} copy-done((bf16[1,8,256,320]{2,3,1,0:T(8,128)(2,1)S(1)}, bf16[1,8,256,320]{2,3,1,0:T(8,128)(2,1)}, u32[]{:S(2)}) %copy-start) | copy-done | bytes 1310744
  1.4 0.8 stats_first.1.after
  2.3 0.2 halo.1
  2.5 0.7 collective-permute-start.2
  3.4 2.7 %collective-permute-start.1 = (bf16[2,320,256]{2,1,0:T(8,128)(2,1)S(1)}, bf16[2,320,256]{2,1,0:T(8,128)(2,1)S(1)}, u32[]{:S(2)}, u32[]{:S(2)}) collective-permute-start(bf16[2,320,256]{2,1,0:T(8,128)(2,1)S(1)} %get-tuple-element.27), channel_id=1, source_target_pairs={{0,1},{1,0},{2,3},{3,2},{4,5},{5,4},{6,7},{7,6},{8,9},{9,8},{10,11... | collective-permute-start | bytes 983048 | tf_op jit(solution)/shard_map/ppermute | solution.py:311
  6.1 22.9 %all_to_all.10 = f32[64,2,128]{2,1,0:T(2,128)S(1)} all-to-all(f32[64,2,128]{2,1,0:T(2,128)S(1)} %broadcast_in_dim.31), channel_id=1, replica_groups={{0,2,4,6,8,10,12,14,16,18,20,22,24,26,28,30,32,34,36,38,40,42,44,46,48,..., dimensions={0} | all-to-all | bytes 131072 | tf_op jit(solution)/shard_map/all_to_all | solution.py:302
  29.1 5.5 %conv_first.1 = (f32[8,320,256]{2,1,0:T(8,128)S(1)}, f32[8,128]{1,0:T(8,128)S(1)}, bf16[960,960]{1,0:T(8,128)(2,1)S(1)}, f32[640,128]{1,0:T(8,128)S(1)}) custom-call(f32[8,128]{1,0:T(8,128)S(1)} %iota.16.flags, bf16[8,320,256]{2,1,0:T(8,128)(2,1)S(1)} %bitcast.13, bf16[2,320,256]{2,1,0:T(8,128)(2,1)S(1)} %collective-permute-done.1.inner, ...), custom_call_target="tpu_custom_call" | custom-call | flops 3774873600 | bytes 4194304 | tf_op jit(solution)/shard_map/conv_first/pallas_call | solution.py:313
  34.8 1.0 %prepare.1 = (bf16[960,960]{1,0:T(8,128)(2,1)S(1)}, bf16[320,320]{1,0:T(8,128)(2,1)S(1)}) custom-call(bf16[3,3,320,320]{3,2,1,0:T(8,128)(2,1)S(1)} %bitcast.33, bf16[320,320]{1,0:T(8,128)(2,1)S(1)} %copy-done.5, f32[8,128]{1,0:T(8,128)S(1)} %get-tuple-element.31.after), custom_call_target="tpu_custom_call" | custom-call | flops 1000000000 | bytes 4194304 | tf_op jit(solution)/shard_map/prepare/pallas_call | solution.py:327
  35.9 14.6 %all_to_all.11 = f32[64,2,128]{2,1,0:T(2,128)S(1)} all-to-all(f32[64,2,128]{2,1,0:T(2,128)S(1)} %broadcast_in_dim.32), channel_id=1, replica_groups={{0,2,4,6,8,10,12,14,16,18,20,22,24,26,28,30,32,34,36,38,40,42,44,46,48,..., dimensions={0} | all-to-all | bytes 131072 | tf_op jit(solution)/shard_map/all_to_all | solution.py:302
  50.5 1.9 %conv_second.4 = (f32[2,320,256]{2,1,0:T(8,128)S(1)}, bf16[2,320,256]{2,1,0:T(8,128)(2,1)S(1)}) custom-call(f32[8,128]{1,0:T(8,128)S(1)} %iota.16.flags, bf16[8,320,256]{2,1,0:T(8,128)(2,1)S(1)} %bitcast.14, f32[8,320,256]{2,1,0:T(8,128)S(1)} %get-tuple-element.30.mid, f32[128,128]{1,0:T(8,128)S(1)} %bitcast.23, f32[640,128]{1,0:T(8,128)S(1)} %get-tuple-element.35.cols, ...), custom_call_target="tpu_custom_call" | custom-call | flops 943718400 | bytes 4194304 | tf_op jit(solution)/shard_map/conv_second/pallas_call | solution.py:336
  52.4 0.9 %collective-permute-start.7 = (bf16[2,320,256]{2,1,0:T(8,128)(2,1)S(1)}, bf16[2,320,256]{2,1,0:T(8,128)(2,1)S(1)}, u32[]{:S(2)}, u32[]{:S(2)}) collective-permute-start(bf16[2,320,256]{2,1,0:T(8,128)(2,1)S(1)} %get-tuple-element.39.after), channel_id=1, source_target_pairs={{0,128},{128,0},{1,129},{129,1},{2,130},{130,2},{3,131},{131,3},{4... | collective-permute-start | bytes 983048 | tf_op jit(solution)/shard_map/ppermute | solution.py:353
  53.3 1.9 %conv_second.5 = (f32[2,320,256]{2,1,0:T(8,128)S(1)}, bf16[2,320,256]{2,1,0:T(8,128)(2,1)S(1)}) custom-call(f32[8,128]{1,0:T(8,128)S(1)} %iota.16.flags, bf16[8,320,256]{2,1,0:T(8,128)(2,1)S(1)} %bitcast.15, f32[8,320,256]{2,1,0:T(8,128)S(1)} %get-tuple-element.30.mid, f32[128,128]{1,0:T(8,128)S(1)} %bitcast.24, f32[640,128]{1,0:T(8,128)S(1)} %get-tuple-element.35.cols, ...), custom_call_target="tpu_custom_call" | custom-call | flops 943718400 | bytes 4194304 | tf_op jit(solution)/shard_map/conv_second/pallas_call | solution.py:336
  55.1 1.3 %collective-permute-start.6 = (bf16[2,320,256]{2,1,0:T(8,128)(2,1)S(1)}, bf16[2,320,256]{2,1,0:T(8,128)(2,1)S(1)}, u32[]{:S(2)}, u32[]{:S(2)}) collective-permute-start(bf16[2,320,256]{2,1,0:T(8,128)(2,1)S(1)} %get-tuple-element.40.after), channel_id=1, source_target_pairs={{0,128},{1,129},{2,130},{3,131},{4,132},{5,133},{6,134},{7,135},{8... | collective-permute-start | bytes 983048 | tf_op jit(solution)/shard_map/ppermute | solution.py:353
  56.4 1.9 %conv_second.6 = (f32[2,320,256]{2,1,0:T(8,128)S(1)}, bf16[2,320,256]{2,1,0:T(8,128)(2,1)S(1)}) custom-call(f32[8,128]{1,0:T(8,128)S(1)} %iota.16.flags, bf16[8,320,256]{2,1,0:T(8,128)(2,1)S(1)} %bitcast.16, f32[8,320,256]{2,1,0:T(8,128)S(1)} %get-tuple-element.30.mid, f32[128,128]{1,0:T(8,128)S(1)} %bitcast.25, f32[640,128]{1,0:T(8,128)S(1)} %get-tuple-element.35.cols, ...), custom_call_target="tpu_custom_call" | custom-call | flops 943718400 | bytes 4194304 | tf_op jit(solution)/shard_map/conv_second/pallas_call | solution.py:336
  58.3 1.3 %collective-permute-start.5 = (bf16[2,320,256]{2,1,0:T(8,128)(2,1)S(1)}, bf16[2,320,256]{2,1,0:T(8,128)(2,1)S(1)}, u32[]{:S(2)}, u32[]{:S(2)}) collective-permute-start(bf16[2,320,256]{2,1,0:T(8,128)(2,1)S(1)} %get-tuple-element.41.after), channel_id=1, source_target_pairs={{0,128},{1,129},{2,130},{3,131},{4,132},{5,133},{6,134},{7,135},{8... | collective-permute-start | bytes 983048 | tf_op jit(solution)/shard_map/ppermute | solution.py:353
  59.6 4.1 %conv_second.7 = (f32[2,320,256]{2,1,0:T(8,128)S(1)}, bf16[2,320,256]{2,1,0:T(8,128)(2,1)S(1)}) custom-call(f32[8,128]{1,0:T(8,128)S(1)} %iota.16.flags, bf16[8,320,256]{2,1,0:T(8,128)(2,1)S(1)} %bitcast.17, f32[8,320,256]{2,1,0:T(8,128)S(1)} %get-tuple-element.30.mid, f32[128,128]{1,0:T(8,128)S(1)} %bitcast.26, f32[640,128]{1,0:T(8,128)S(1)} %get-tuple-element.35.cols, ...), custom_call_target="tpu_custom_call" | custom-call | flops 943718400 | bytes 4194304 | tf_op jit(solution)/shard_map/conv_second/pallas_call | solution.py:336
  63.7 1.3 %collective-permute-start.4 = (bf16[2,320,256]{2,1,0:T(8,128)(2,1)S(1)}, bf16[2,320,256]{2,1,0:T(8,128)(2,1)S(1)}, u32[]{:S(2)}, u32[]{:S(2)}) collective-permute-start(bf16[2,320,256]{2,1,0:T(8,128)(2,1)S(1)} %get-tuple-element.43), channel_id=1, source_target_pairs={{0,128},{1,129},{2,130},{3,131},{4,132},{5,133},{6,134},{7,135},{8... | collective-permute-start | bytes 983048 | tf_op jit(solution)/shard_map/ppermute | solution.py:353
  65.1 0.8 mix.4.rest_0_
  65.9 5.9 %collective-permute-done.6.arrived = bf16[2,320,256]{2,1,0:T(8,128)(2,1)S(1)} collective-permute-done((bf16[2,320,256]{2,1,0:T(8,128)(2,1)S(1)}, bf16[2,320,256]{2,1,0:T(8,128)(2,1)S(1)}, u32[]{:S(2)}, u32[]{:S(2)}) %collective-permute-start.6) | collective-permute-done | bytes 327712 | tf_op jit(solution)/shard_map/ppermute | solution.py:353
  71.8 0.8 mix.5.rest_0_
  72.7 6.2 %collective-permute-done.5.arrived = bf16[2,320,256]{2,1,0:T(8,128)(2,1)S(1)} collective-permute-done((bf16[2,320,256]{2,1,0:T(8,128)(2,1)S(1)}, bf16[2,320,256]{2,1,0:T(8,128)(2,1)S(1)}, u32[]{:S(2)}, u32[]{:S(2)}) %collective-permute-start.5) | collective-permute-done | bytes 327712 | tf_op jit(solution)/shard_map/ppermute | solution.py:353
  78.9 0.8 mix.6.rest_0_
  79.7 4.3 %collective-permute-done.4.arrived = bf16[2,320,256]{2,1,0:T(8,128)(2,1)S(1)} collective-permute-done((bf16[2,320,256]{2,1,0:T(8,128)(2,1)S(1)}, bf16[2,320,256]{2,1,0:T(8,128)(2,1)S(1)}, u32[]{:S(2)}, u32[]{:S(2)}) %collective-permute-start.4) | collective-permute-done | bytes 327712 | tf_op jit(solution)/shard_map/ppermute | solution.py:353
  84.1 0.8 mix.7
  (28 shorter events, 0.6 us)
Async XLA Ops:
  0.1 1.3 %copy-start = (bf16[1,8,256,320]{2,3,1,0:T(8,128)(2,1)S(1)}, bf16[1,8,256,320]{2,3,1,0:T(8,128)(2,1)}, u32[]{:S(2)}) copy-start(bf16[1,8,256,320]{2,3,1,0:T(8,128)(2,1)} %param.6) | copy-start | bytes 3932164
  1.4 27.7 %copy-start.1 = (bf16[1,8,256,320]{2,3,1,0:T(8,128)(2,1)S(1)}, bf16[1,8,256,320]{2,3,1,0:T(8,128)(2,1)}, u32[]{:S(2)}) copy-start(bf16[1,8,256,320]{2,3,1,0:T(8,128)(2,1)} %param.6) | copy-start | bytes 3932164
  1.4 27.7 %copy-start.2 = (f32[1,2,320]{2,1,0:T(2,128)S(1)}, f32[1,2,320]{2,1,0:T(2,128)}, u32[]{:S(2)}) copy-start(f32[1,2,320]{2,1,0:T(2,128)} %param.10) | copy-start | bytes 7684
  1.4 27.7 %copy-start.3 = (bf16[1,3,3,320,320]{4,3,2,1,0:T(8,128)(2,1)S(1)}, bf16[1,3,3,320,320]{4,3,2,1,0:T(8,128)(2,1)}, u32[]{:S(2)}) copy-start(bf16[1,3,3,320,320]{4,3,2,1,0:T(8,128)(2,1)} %param.7) | copy-start | bytes 5529604
  1.4 27.7 %copy-start.6 = (f32[1,320]{1,0:T(1,128)S(1)}, f32[1,320]{1,0:T(1,128)}, u32[]{:S(2)}) copy-start(f32[1,320]{1,0:T(1,128)} %shift.1) | copy-start | bytes 3844
  2.2 1.2 %collective-permute-start = (f32[1,128]{1,0:T(1,128)S(1)}, f32[1,128]{1,0:T(1,128)S(1)}, u32[]{:S(2)}, u32[]{:S(2)}) collective-permute-start(f32[1,128]{1,0:T(1,128)S(1)} %slice.8), channel_id=1, source_target_pairs={{0,1},{1,0},{2,3},{3,2},{4,5},{5,4},{6,7},{7,6},{8,9},{9,8},{10,11... | collective-permute-start | bytes 1544 | tf_op jit(solution)/shard_map/ppermute | solution.py:298
  2.5 26.6 %collective-permute-start.2 = (bf16[2,320,256]{2,1,0:T(8,128)(2,1)S(1)}, bf16[2,320,256]{2,1,0:T(8,128)(2,1)S(1)}, u32[]{:S(2)}, u32[]{:S(2)}) collective-permute-start(bf16[2,320,256]{2,1,0:T(8,128)(2,1)S(1)} %get-tuple-element.28), channel_id=1, source_target_pairs={{1,2},{3,4},{5,6},{7,8},{9,10},{11,12},{13,14},{15,16},{17,18},{19... | collective-permute-start | bytes 983048 | tf_op jit(solution)/shard_map/ppermute | solution.py:310
  3.4 25.7 %collective-permute-start.1 = (bf16[2,320,256]{2,1,0:T(8,128)(2,1)S(1)}, bf16[2,320,256]{2,1,0:T(8,128)(2,1)S(1)}, u32[]{:S(2)}, u32[]{:S(2)}) collective-permute-start(bf16[2,320,256]{2,1,0:T(8,128)(2,1)S(1)} %get-tuple-element.27), channel_id=1, source_target_pairs={{0,1},{1,0},{2,3},{3,2},{4,5},{5,4},{6,7},{7,6},{8,9},{9,8},{10,11... | collective-permute-start | bytes 983048 | tf_op jit(solution)/shard_map/ppermute | solution.py:311
  29.1 5.6 %copy-start.4 = (bf16[1,3,3,320,320]{4,3,2,1,0:T(8,128)(2,1)S(1)}, bf16[1,3,3,320,320]{4,3,2,1,0:T(8,128)(2,1)}, u32[]{:S(2)}) copy-start(bf16[1,3,3,320,320]{4,3,2,1,0:T(8,128)(2,1)} %param.8) | copy-start | bytes 5529604
  29.1 5.6 %copy-start.5 = (bf16[320,320]{1,0:T(8,128)(2,1)S(1)}, bf16[320,320]{1,0:T(8,128)(2,1)}, u32[]{:S(2)}) copy-start(bf16[320,320]{1,0:T(8,128)(2,1)} %z.1) | copy-start | bytes 614404
  34.7 1.2 %collective-permute-start.3 = (f32[1,128]{1,0:T(1,128)S(1)}, f32[1,128]{1,0:T(1,128)S(1)}, u32[]{:S(2)}, u32[]{:S(2)}) collective-permute-start(f32[1,128]{1,0:T(1,128)S(1)} %slice.9), channel_id=1, source_target_pairs={{0,1},{1,0},{2,3},{3,2},{4,5},{5,4},{6,7},{7,6},{8,9},{9,8},{10,11... | collective-permute-start | bytes 1544 | tf_op jit(solution)/shard_map/ppermute | solution.py:298
  52.4 12.6 %collective-permute-start.7 = (bf16[2,320,256]{2,1,0:T(8,128)(2,1)S(1)}, bf16[2,320,256]{2,1,0:T(8,128)(2,1)S(1)}, u32[]{:S(2)}, u32[]{:S(2)}) collective-permute-start(bf16[2,320,256]{2,1,0:T(8,128)(2,1)S(1)} %get-tuple-element.39.after), channel_id=1, source_target_pairs={{0,128},{128,0},{1,129},{129,1},{2,130},{130,2},{3,131},{131,3},{4... | collective-permute-start | bytes 983048 | tf_op jit(solution)/shard_map/ppermute | solution.py:353
  55.1 16.7 %collective-permute-start.6 = (bf16[2,320,256]{2,1,0:T(8,128)(2,1)S(1)}, bf16[2,320,256]{2,1,0:T(8,128)(2,1)S(1)}, u32[]{:S(2)}, u32[]{:S(2)}) collective-permute-start(bf16[2,320,256]{2,1,0:T(8,128)(2,1)S(1)} %get-tuple-element.40.after), channel_id=1, source_target_pairs={{0,128},{1,129},{2,130},{3,131},{4,132},{5,133},{6,134},{7,135},{8... | collective-permute-start | bytes 983048 | tf_op jit(solution)/shard_map/ppermute | solution.py:353
  58.3 20.6 %collective-permute-start.5 = (bf16[2,320,256]{2,1,0:T(8,128)(2,1)S(1)}, bf16[2,320,256]{2,1,0:T(8,128)(2,1)S(1)}, u32[]{:S(2)}, u32[]{:S(2)}) collective-permute-start(bf16[2,320,256]{2,1,0:T(8,128)(2,1)S(1)} %get-tuple-element.41.after), channel_id=1, source_target_pairs={{0,128},{1,129},{2,130},{3,131},{4,132},{5,133},{6,134},{7,135},{8... | collective-permute-start | bytes 983048 | tf_op jit(solution)/shard_map/ppermute | solution.py:353
  63.7 20.3 %collective-permute-start.4 = (bf16[2,320,256]{2,1,0:T(8,128)(2,1)S(1)}, bf16[2,320,256]{2,1,0:T(8,128)(2,1)S(1)}, u32[]{:S(2)}, u32[]{:S(2)}) collective-permute-start(bf16[2,320,256]{2,1,0:T(8,128)(2,1)S(1)} %get-tuple-element.43), channel_id=1, source_target_pairs={{0,128},{1,129},{2,130},{3,131},{4,132},{5,133},{6,134},{7,135},{8... | collective-permute-start | bytes 983048 | tf_op jit(solution)/shard_map/ppermute | solution.py:353
